TPU v7x, 32 devices: a whole 2x2x4 slice. The times are simulated.
32 devices in a mesh: frame: 2 (over x), tile: 16 (over z, y, core).
Axes of the slice: x: 2, y: 2, z: 4, core: 2. Of those that a mesh axis runs over, the one named last changes fastest.
Arguments:
- kspace_samples: bfloat16 [4, 64, 32, 128], P('frame', 'tile'), may hold values from -6 to 6
- density: bfloat16 [4, 64, 128], P('frame', 'tile'), may hold values from 0.796875 to 8
- sample_frac: bfloat16 [4, 64, 3, 128], P('frame', 'tile'), may hold values from 0 to 1
- row_offsets: int32 [4, 64, 128], P('frame', 'tile'), may hold values from 0 to 2
- depth_base: int32 [4, 64, 128], P('frame', 'tile'), may hold values from 0 to 127
- block_base: int32 [4, 64, 2], P('frame', 'tile'), may hold values from 0 to 127, as said below
- coil_maps: bfloat16 [16, 2, 128, 128, 128], P(None, None, 'tile'), may hold values from -1.5 to 1.5
- estimate: float32 [4, 2, 128, 128, 128], P('frame', None, 'tile'), may hold values from -6 to 6
Outputs:
- updated: float32 [4, 2, 128, 128, 128], P('frame', None, 'tile')
Inputs may be any that keep to these rules, and one draw needn't show every extreme that they name: `block_base`: block b of a frame is held by tile index b // 4. Its kx planes are xb .. xb + 5 mod 128, and tile number p holds planes p * 8 .. p * 8 + 7. In every frame, at most 1 block of one tile index touch any one tile, and some tile is touched by exactly 1 block of every tile index.
All inputs are finite; a program needn't handle non-finite values.
Results may differ from a plain program's by a relative error of at most 0.0095.
Values may be sent and summed in bfloat16 or wider, within the bound.
No kernel may reach another device: no remote copies, remote signals or barrier semaphores. Data moves between devices by JAX's collectives and lax.ppermute only.
A program may use at most 128 MiB of HBM per device.

v0:
```python
import math

import jax
import jax.numpy as jnp
from jax import lax
from jax.sharding import PartitionSpec as P

WIN = 8


BETA = 13.9
EPS = 0.05
LAMBDA_TV = 0.3


def extended(block, sides, width):
    for axis, dim in sides:
        count = lax.axis_size(axis)
        forward = [(i, i + 1) for i in range(count - 1)]
        backward = [(target, source) for source, target in forward]
        low = lax.ppermute(
            lax.slice_in_dim(block, block.shape[dim] - width, None, axis=dim), axis, forward
        )
        high = lax.ppermute(lax.slice_in_dim(block, 0, width, axis=dim), axis, backward)
        block = jnp.concatenate([low, block, high], axis=dim)
    return block


def bessel_zero(argument):
    quarter = argument * argument / 4.0
    series_term = jnp.ones_like(argument)
    series_sum = jnp.ones_like(argument)
    for power in range(1, 40):
        series_term = series_term * quarter / float(power * power)
        series_sum = series_sum + series_term
    return series_sum


def kaiser(offset, fraction):
    distance = offset.astype(jnp.float32) - 2.0 - fraction
    inside = jnp.maximum(1.0 - distance / 3.0 * (distance / 3.0), 0.0)
    return bessel_zero(BETA * jnp.sqrt(inside)) / bessel_zero(jnp.full_like(distance, BETA))


def dft_table(grid_size):
    positions = jnp.arange(grid_size)
    angles = (positions[:, None] * positions[None, :] % grid_size).astype(jnp.float32) * (
        2.0 * math.pi / grid_size
    )
    cosine = jnp.cos(angles)
    sine_part = jnp.sin(angles)
    upper_rows = jnp.stack([cosine, sine_part], axis=1)
    bottom = jnp.stack([-sine_part, cosine], axis=1)
    return jnp.stack([upper_rows, bottom], axis=0).astype(jnp.bfloat16)


def place_slots(chosen, values):
    return jnp.einsum(
        "fjtk,fj...->ftk...", chosen, values, preferred_element_type=jnp.float32
    ).astype(jnp.bfloat16)


def merge_slots(values):
    return values.reshape((values.shape[0], values.shape[1] * values.shape[2]) + values.shape[3:])


def grid_frame(
    payload, weights_in, fractions, row_shift, depth_start, block_start, planes, grid_size, window
):
    offsets = jnp.arange(6)
    window_rows = jnp.arange(window)
    depth_cells = jnp.arange(grid_size)
    row_cells = jnp.arange(grid_size)
    amplitude_in = payload.astype(jnp.float32)
    weight_rows = weights_in.astype(jnp.float32)
    frac_rows = fractions.astype(jnp.float32)
    shift_rows = row_shift.astype(jnp.int32)
    depth_rows = depth_start.astype(jnp.int32)
    corner_rows = block_start.astype(jnp.int32)
    along_x = kaiser(offsets[None, :, None], frac_rows[:, 0][:, None, :])
    relative = (planes[None, :] - corner_rows[:, 0:1]) % grid_size
    select = (relative[:, :, None] == offsets).astype(jnp.float32)
    weight_x = jnp.sum(select[:, :, :, None] * along_x[:, None, :, :], axis=2)
    lag_rows = window_rows[None, :, None] - shift_rows[:, None, :]
    weight_y = jnp.where(
        (lag_rows >= 0) & (lag_rows < 6), kaiser(lag_rows, frac_rows[:, 1][:, None, :]), 0.0
    )
    lag_depth = (depth_cells[None, :, None] - depth_rows[:, None, :]) % grid_size
    weight_z = jnp.where(lag_depth < 6, kaiser(lag_depth, frac_rows[:, 2][:, None, :]), 0.0).astype(
        jnp.bfloat16
    )
    scaled = weight_rows[:, None, :] * amplitude_in
    outer = (
        scaled[:, :, None, None, :] * weight_x[:, None, :, None, :] * weight_y[:, None, None, :, :]
    ).astype(jnp.bfloat16)
    contrib = jnp.einsum("bcirs,bqs->bcirq", outer, weight_z, preferred_element_type=jnp.float32)
    row_target = (corner_rows[:, 1][:, None] + window_rows[None, :]) % grid_size
    placement = (row_target[:, :, None] == row_cells[None, None, :]).astype(jnp.float32)
    totals = jnp.einsum(
        "bcirq,bry->ciyq",
        contrib,
        placement,
        precision=lax.Precision.HIGHEST,
        preferred_element_type=jnp.float32,
    )
    return totals.astype(jnp.bfloat16)


def on_device(
    kspace_samples, density, sample_frac, row_offsets, depth_base, block_base, coil_maps, estimate
):
    tile_count = lax.axis_size("tile")
    tile_here = lax.axis_index("tile")
    frame_here = lax.axis_index("frame")
    frames_local = kspace_samples.shape[0]
    channels = kspace_samples.shape[2]
    coil_count = channels // 2
    sample_count = kspace_samples.shape[3]
    grid_size = coil_maps.shape[3]
    slab_size = grid_size // tile_count
    capacity = kspace_samples.shape[1] // 4
    scale = 1.0 / (8.0 * math.sqrt(kspace_samples.shape[1] * tile_count * sample_count))
    offsets = jnp.arange(6)
    planes_hit = (block_base[:, :, 0:1] + offsets) % grid_size
    owners = planes_hit // slab_size
    touched = jnp.any(owners[:, :, :, None] == jnp.arange(tile_count), axis=2)
    counts = touched.astype(jnp.int32)
    before = jnp.cumsum(counts, axis=1) - counts
    picked = touched[..., None] & (before[..., None] == jnp.arange(capacity))
    chosen = picked.astype(jnp.bfloat16)
    send_payload = place_slots(chosen, kspace_samples)
    send_weights = place_slots(chosen, density)
    send_fractions = place_slots(chosen, sample_frac)
    send_shift = place_slots(chosen, row_offsets.astype(jnp.bfloat16))
    send_depth = place_slots(chosen, depth_base.astype(jnp.bfloat16))
    send_corner = place_slots(chosen, block_base.astype(jnp.bfloat16))
    got_payload, got_weights, got_fractions, got_shift, got_depth, got_corner = (
        lax.all_to_all(send_payload, "tile", split_axis=1, concat_axis=1, tiled=True),
        lax.all_to_all(send_weights, "tile", split_axis=1, concat_axis=1, tiled=True),
        lax.all_to_all(send_fractions, "tile", split_axis=1, concat_axis=1, tiled=True),
        lax.all_to_all(send_shift, "tile", split_axis=1, concat_axis=1, tiled=True),
        lax.all_to_all(send_depth, "tile", split_axis=1, concat_axis=1, tiled=True),
        lax.all_to_all(send_corner, "tile", split_axis=1, concat_axis=1, tiled=True),
    )
    planes = tile_here * slab_size + jnp.arange(slab_size)
    gridded = []
    for frame_pos in range(frames_local):
        gridded.append(
            grid_frame(
                merge_slots(got_payload)[frame_pos],
                merge_slots(got_weights)[frame_pos],
                merge_slots(got_fractions)[frame_pos],
                merge_slots(got_shift)[frame_pos],
                merge_slots(got_depth)[frame_pos],
                merge_slots(got_corner)[frame_pos],
                planes,
                grid_size,
                WIN,
            )
        )
    kspace = jnp.stack(gridded, axis=0).reshape(
        frames_local, coil_count, 2, slab_size, grid_size, grid_size
    )
    dft_matrix = dft_table(grid_size)
    first = jnp.einsum(
        "fcsxkz,sktn->fctxnz", kspace, dft_matrix, preferred_element_type=jnp.float32
    ).astype(jnp.bfloat16)
    second = jnp.einsum(
        "fcsxyk,sktn->fctxyn", first, dft_matrix, preferred_element_type=jnp.float32
    ).astype(jnp.bfloat16)
    moved = lax.all_to_all(second, "tile", split_axis=4, concat_axis=3, tiled=True)
    images = jnp.einsum(
        "fcskyz,sktn->fctynz", moved, dft_matrix, preferred_element_type=jnp.float32
    )
    maps_real = coil_maps[:, 0].astype(jnp.float32)[None]
    maps_imag = coil_maps[:, 1].astype(jnp.float32)[None]
    image_real = images[:, :, 0]
    image_imag = images[:, :, 1]
    back_real = scale * jnp.sum(maps_real * image_real + maps_imag * image_imag, axis=1)
    back_imag = scale * jnp.sum(maps_real * image_imag - maps_imag * image_real, axis=1)
    half = estimate + jnp.stack([back_real, back_imag], axis=1)
    padded = extended(half.astype(jnp.bfloat16), (("frame", 0),), 1).astype(half.dtype)
    change = padded[1:] - padded[:-1]
    magnitude = jnp.sqrt(change[:, 0] * change[:, 0] + change[:, 1] * change[:, 1] + EPS * EPS)
    psi = change / magnitude[:, None]
    pair_index = frame_here * frames_local + jnp.arange(frames_local + 1) - 1
    frame_total = lax.axis_size("frame") * frames_local
    valid = (pair_index >= 0) & (pair_index <= frame_total - 2)
    psi = jnp.where(valid[:, None, None, None, None], psi, 0.0)
    return half - LAMBDA_TV * (psi[:-1] - psi[1:])


def solution(mesh):
    in_specs = (
        P("frame", "tile", None, None),
        P("frame", "tile", None),
        P("frame", "tile", None, None),
        P("frame", "tile", None),
        P("frame", "tile", None),
        P("frame", "tile", None),
        P(None, None, "tile", None, None),
        P("frame", None, "tile", None, None),
    )
    out_specs = P("frame", None, "tile", None, None)
    return jax.shard_map(
        on_device, mesh=mesh, in_specs=in_specs, out_specs=out_specs, check_vma=False
    )
```

profile of v0, /device:TPU:12, one launch (start us, length us, event | category | flops | bytes accessed | tf_op | source)
XLA Modules:
  0.0 612.8 jit_solution(14040327068444946041)
XLA Ops:
  2.4 6.2 %all-to-all-start = ((bf16[2,16,1,2]{3,0,2,1:T(2,128)(2,1)}), bf16[2,16,1,2]{3,0,2,1:T(2,128)(2,1)S(1)}, u32[]{:S(2)}, u32[]{:S(2)}) async-start(bf16[2,16,1,2]{3,0,2,1:T(2,128)(2,1)} %copy.111), calls=%async_computation | async-start | bytes 16384 | tf_op jit(solution)/shard_map/all_to_all | solution.py:143
  16.3 6.0 all-to-all-start.1
  26.4 5.7 all-to-all-start.5
  32.0 4.1 all-to-all-done.5
  36.2 5.7 all-to-all-start.4
  41.9 4.1 all-to-all-done.4
  46.0 5.7 all-to-all-start.3
  51.7 4.2 all-to-all-done.3
  55.9 5.9 all-to-all-start.2
  63.5 6.1 %all-to-all-done.2 = bf16[2,16,1,32,128]{4,3,0,2,1:T(8,128)(2,1)S(1)} async-done(((bf16[2,16,1,32,128]{4,3,0,2,1:T(8,128)(2,1)}), bf16[2,16,1,32,128]{4,3,0,2,1:T(8,128)(2,1)S(1)}, u32[]{:S(2)}, u32[]{:S(2)}) %all-to-all-start.2) | async-done | bytes 262176 | tf_op jit(solution)/shard_map/all_to_all | solution.py:138
  70.0 9.5 %fusion.17 = f32[16,32,8,8,128]{4,3,2,1,0:T(8,128)} fusion(f32[16,8,128]{2,1,0:T(8,128)S(1)} %multiply_select_fusion, f32[16,32,8,128]{3,2,1,0:T(8,128)S(1)} %broadcast_multiply_fusion, f32[16,128]{1,0:T(8,128)S(1)} %get-tuple-element.20, s32[16,128]{1,0:T(8,128)S(1)} %bitcast.202), kind=kOutput, calls=%fused_computation.24 | convolution fusion | flops 1119092736 | bytes 18956288 | tf_op jit(solution)/shard_map/bcirs,bqs->bcirq/dot_general | solution.py:96
  79.5 26.1 %bitcast_convert_fusion.2 = bf16[128,32,8,128]{3,0,2,1:T(8,128)(2,1)} fusion(f32[16,32,8,8,128]{4,3,2,1,0:T(8,128)} %fusion.17, s32[16,8]{0,1:T(8,128)S(1)} %add_select_fusion.6), kind=kOutput, calls=%fused_computation.12 | convolution fusion | flops 6446661632 | bytes 25166336 | tf_op jit(solution)/shard_map/bcirq,bry->ciyq/dot_general | solution.py:99
  105.6 9.5 %fusion.16 = f32[16,32,8,8,128]{4,3,2,1,0:T(8,128)} fusion(f32[16,8,128]{2,1,0:T(8,128)S(1)} %multiply_select_fusion.1, f32[16,32,8,128]{3,2,1,0:T(8,128)S(1)} %broadcast_multiply_fusion.1, f32[16,128]{1,0:T(8,128)S(1)} %get-tuple-element.15, s32[16,128]{1,0:T(8,128)S(1)} %bitcast.201), kind=kOutput, calls=%fused_computation.23 | convolution fusion | flops 1119092736 | bytes 18956288 | tf_op jit(solution)/shard_map/bcirs,bqs->bcirq/dot_general | solution.py:96
  115.1 26.2 %bitcast_convert_fusion.3 = bf16[128,32,8,128]{3,0,2,1:T(8,128)(2,1)} fusion(f32[16,32,8,8,128]{4,3,2,1,0:T(8,128)} %fusion.16, s32[16,8]{0,1:T(8,128)S(1)} %get-tuple-element.41), kind=kOutput, calls=%fused_computation.13 | convolution fusion | flops 6446661632 | bytes 25166336 | tf_op jit(solution)/shard_map/bcirq,bry->ciyq/dot_general | solution.py:99
  141.3 16.2 %fusion = bf16[2,16,2,8,128,128]{4,5,3,1,0,2:T(8,128)(2,1)} fusion(bf16[1,128,2,128]{1,3,0,2:T(8,128)(2,1)S(1)} %get-tuple-element.14, bf16[1,128,2,128]{1,3,0,2:T(8,128)(2,1)S(1)} %get-tuple-element.13, bf16[1,16,2,8,128,128]{5,4,3,2,1,0:T(8,128)(2,1)} %bitcast.195, bf16[1,16,2,8,128,128]{5,4,3,2,1,0:T(8,128)(2,1)} %bitcast.196), kind=kOutput, calls=%fused_computation.2 | convolution fusion | flops 8615624704 | bytes 33685504 | tf_op jit(solution)/shard_map/fcsxyk,sktn->fctxyn/dot_general | solution.py:168
  157.5 23.6 %copy.130 = bf16[2,16,2,8,128,128]{5,3,1,0,2,4:T(8,128)(2,1)} copy(bf16[2,16,2,8,128,128]{4,5,3,1,0,2:T(8,128)(2,1)} %fusion) | data formatting | bytes 33554432 | tf_op jit(solution)/shard_map/convert_element_type | solution.py:170
  181.2 7.3 %all-to-all-start.6 = ((bf16[2,16,2,8,128,128]{5,3,1,0,2,4:T(8,128)(2,1)}), bf16[2,16,2,8,128,128]{5,3,1,0,2,4:T(8,128)(2,1)}, u32[]{:S(2)}, u32[]{:S(2)}) async-start(bf16[2,16,2,8,128,128]{5,3,1,0,2,4:T(8,128)(2,1)} %copy.130), calls=%async_computation.6 | async-start | bytes 33554432 | tf_op jit(solution)/shard_map/all_to_all | solution.py:171
  188.5 11.3 %bitcast_convert_fusion.5 = (f32[16,8,128,128]{3,2,1,0:T(8,128)}, f32[16,8,128,128]{3,2,1,0:T(8,128)}) fusion(bf16[16,2,8,128,128]{4,3,2,1,0:T(8,128)(2,1)} %param.14), kind=kLoop, calls=%fused_computation.30 | loop fusion | flops 4194304 | bytes 25165824 | tf_op jit(solution)/shard_map/convert_element_type | solution.py:175
  199.8 350.7 %all-to-all-done.6 = bf16[2,16,2,8,128,128]{5,3,1,0,2,4:T(8,128)(2,1)} async-done(((bf16[2,16,2,8,128,128]{5,3,1,0,2,4:T(8,128)(2,1)}), bf16[2,16,2,8,128,128]{5,3,1,0,2,4:T(8,128)(2,1)}, u32[]{:S(2)}, u32[]{:S(2)}) %all-to-all-start.6) | async-done | bytes 16777248 | tf_op jit(solution)/shard_map/all_to_all | solution.py:171
  550.5 17.1 %fusion.11 = f32[2,16,2,8,128,128]{5,4,3,1,0,2:T(8,128)} fusion(bf16[2,16,2,16,8,8,128]{6,4,1,0,2,5,3:T(8,128)(2,1)} %bitcast.70, bf16[1,128,2,128]{1,3,0,2:T(8,128)(2,1)S(1)} %get-tuple-element.14, bf16[1,128,2,128]{1,3,0,2:T(8,128)(2,1)S(1)} %get-tuple-element.13), kind=kOutput, calls=%fused_computation.22 | convolution fusion | flops 4295229440 | bytes 50462720 | tf_op jit(solution)/shard_map/fcskyz,sktn->fctynz/dot_general | solution.py:172
  567.6 17.5 %add_reduce_fusion = (f32[2,8,128,128]{3,2,1,0:T(8,128)S(1)}, f32[2,8,128,128]{3,2,1,0:T(8,128)S(1)}) fusion(f32[2,16,2,8,128,128]{5,4,3,1,0,2:T(8,128)} %fusion.11, f32[16,8,128,128]{3,2,1,0:T(8,128)} %get-tuple-element.8, f32[16,8,128,128]{3,2,1,0:T(8,128)} %get-tuple-element.7), kind=kLoop, calls=%fused_computation.19 | loop fusion | flops 33030144 | bytes 52428800 | tf_op jit(solution)/shard_map/reduce_sum | solution.py:179
  586.7 4.2 collective-permute-start
  592.5 9.5 %collective-permute-done = bf16[1,2,8,128,128]{4,3,2,1,0:T(8,128)(2,1)} collective-permute-done((bf16[1,2,8,128,128]{4,3,2,1,0:T(8,128)(2,1)}, bf16[1,2,8,128,128]{4,3,2,1,0:T(8,128)(2,1)}, u32[]{:S(2)}, u32[]{:S(2)}) %collective-permute-start) | collective-permute-done | bytes 524320 | tf_op jit(solution)/shard_map/ppermute | solution.py:21
  602.0 4.9 collective-permute-done.1
  (74 shorter events, 24.6 us)
Async XLA Ops:
  0.0 13.3 %copy-start = (bf16[2,4,32,128]{3,2,1,0:T(8,128)(2,1)S(1)}, bf16[2,4,32,128]{3,2,1,0:T(8,128)(2,1)}, u32[]{:S(2)}) copy-start(bf16[2,4,32,128]{3,2,1,0:T(8,128)(2,1)} %param.8) | copy-start | bytes 196612
  2.4 13.9 %all-to-all-start = ((bf16[2,16,1,2]{3,0,2,1:T(2,128)(2,1)}), bf16[2,16,1,2]{3,0,2,1:T(2,128)(2,1)S(1)}, u32[]{:S(2)}, u32[]{:S(2)}) async-start(bf16[2,16,1,2]{3,0,2,1:T(2,128)(2,1)} %copy.111), calls=%async_computation | async-start | bytes 16384 | tf_op jit(solution)/shard_map/all_to_all | solution.py:143
  16.3 10.1 %all-to-all-start.1 = ((bf16[2,16,1,128]{3,0,2,1:T(2,128)(2,1)}), bf16[2,16,1,128]{3,0,2,1:T(2,128)(2,1)S(1)}, u32[]{:S(2)}, u32[]{:S(2)}) async-start(bf16[2,16,1,128]{3,0,2,1:T(2,128)(2,1)} %copy.113), calls=%async_computation.1 | async-start | bytes 16384 | tf_op jit(solution)/shard_map/all_to_all | solution.py:139
  26.4 9.8 %all-to-all-start.5 = ((bf16[2,16,1,128]{3,0,2,1:T(2,128)(2,1)}), bf16[2,16,1,128]{3,0,2,1:T(2,128)(2,1)S(1)}, u32[]{:S(2)}, u32[]{:S(2)}) async-start(bf16[2,16,1,128]{3,0,2,1:T(2,128)(2,1)} %copy.121), calls=%async_computation.5 | async-start | bytes 16384 | tf_op jit(solution)/shard_map/all_to_all | solution.py:142
  36.2 9.8 %all-to-all-start.4 = ((bf16[2,16,1,128]{3,0,2,1:T(2,128)(2,1)}), bf16[2,16,1,128]{3,0,2,1:T(2,128)(2,1)S(1)}, u32[]{:S(2)}, u32[]{:S(2)}) async-start(bf16[2,16,1,128]{3,0,2,1:T(2,128)(2,1)} %copy.120), calls=%async_computation.4 | async-start | bytes 16384 | tf_op jit(solution)/shard_map/all_to_all | solution.py:141
  46.0 9.9 %all-to-all-start.3 = ((bf16[2,16,1,3,128]{4,0,3,2,1:T(2,128)(2,1)}), bf16[2,16,1,3,128]{4,0,3,2,1:T(2,128)(2,1)S(1)}, u32[]{:S(2)}, u32[]{:S(2)}) async-start(bf16[2,16,1,3,128]{4,0,3,2,1:T(2,128)(2,1)} %copy.117), calls=%async_computation.3 | async-start | bytes 49152 | tf_op jit(solution)/shard_map/all_to_all | solution.py:140
  55.9 13.7 %all-to-all-start.2 = ((bf16[2,16,1,32,128]{4,3,0,2,1:T(8,128)(2,1)}), bf16[2,16,1,32,128]{4,3,0,2,1:T(8,128)(2,1)S(1)}, u32[]{:S(2)}, u32[]{:S(2)}) async-start(bf16[2,16,1,32,128]{4,3,0,2,1:T(8,128)(2,1)} %copy.115), calls=%async_computation.2 | async-start | bytes 524288 | tf_op jit(solution)/shard_map/all_to_all | solution.py:138
  181.2 369.3 %all-to-all-start.6 = ((bf16[2,16,2,8,128,128]{5,3,1,0,2,4:T(8,128)(2,1)}), bf16[2,16,2,8,128,128]{5,3,1,0,2,4:T(8,128)(2,1)}, u32[]{:S(2)}, u32[]{:S(2)}) async-start(bf16[2,16,2,8,128,128]{5,3,1,0,2,4:T(8,128)(2,1)} %copy.130), calls=%async_computation.6 | async-start | bytes 33554432 | tf_op jit(solution)/shard_map/all_to_all | solution.py:171
  567.6 17.7 %copy-start.2 = (f32[2,2,8,128,128]{4,3,2,1,0:T(8,128)S(1)}, f32[2,2,8,128,128]{4,3,2,1,0:T(8,128)}, u32[]{:S(2)}) copy-start(f32[2,2,8,128,128]{4,3,2,1,0:T(8,128)} %param.15) | copy-start | bytes 6291460
  586.7 15.3 %collective-permute-start = (bf16[1,2,8,128,128]{4,3,2,1,0:T(8,128)(2,1)}, bf16[1,2,8,128,128]{4,3,2,1,0:T(8,128)(2,1)}, u32[]{:S(2)}, u32[]{:S(2)}) collective-permute-start(bf16[1,2,8,128,128]{4,3,2,1,0:T(8,128)(2,1)} %get-tuple-element.9), channel_id=1, source_target_pairs={{0,16},{1,17},{2,18},{3,19},{4,20},{5,21},{6,22},{7,23},{8,24},{9,... | collective-permute-start | bytes 1572872 | tf_op jit(solution)/shard_map/ppermute | solution.py:21
  590.9 16.0 %collective-permute-start.1 = (bf16[1,2,8,128,128]{4,3,2,1,0:T(8,128)(2,1)}, bf16[1,2,8,128,128]{4,3,2,1,0:T(8,128)(2,1)}, u32[]{:S(2)}, u32[]{:S(2)}) collective-permute-start(bf16[1,2,8,128,128]{4,3,2,1,0:T(8,128)(2,1)} %get-tuple-element.10), channel_id=1, source_target_pairs={{16,0},{17,1},{18,2},{19,3},{20,4},{21,5},{22,6},{23,7},{24,8},{25... | collective-permute-start | bytes 1572872 | tf_op jit(solution)/shard_map/ppermute | solution.py:24
  608.7 1.6 copy-start.3
  608.7 3.6 copy-start.1
where the time goes:
time: 619 us; the launch traced here: 613 us
  waiting for transfers between devices  387 us (63%)
  matrix products  109 us (18%)
  starting transfers between devices  48.3 us (8%)
  other arithmetic  37.4 us (6%)
  local copies, waits for them, and re-layouts  29.9 us (5%)
    all_to_all x1, waiting for transfers between devices, on_device(): lax.all_to_all(second, 'tile', split_axis=4, concat_axis=3, tiled=True)  351 us
    dot_general x2, matrix products, grid_frame(): jnp.einsum('bcirq,bry->ciyq', contrib, placement, precision=lax.Precision...  52.3 us
    convert_element_type x1, local copies, waits for them, and re-layouts, on_device(): second = jnp.einsum('fcsxyk,sktn->fctxyn', first, dft_matrix, preferred_e...  23.6 us
    dot_general x2, matrix products, grid_frame(): jnp.einsum('bcirs,bqs->bcirq', outer, weight_z, preferred_element_type=jn...  19 us
    reduce_sum x1, other arithmetic, on_device(): jnp.sum(maps_real * image_real + maps_imag * image_imag, axis=1)  17.5 us
    dot_general x1, matrix products, on_device(): jnp.einsum('fcskyz,sktn->fctynz', moved, dft_matrix, preferred_element_ty...  17.1 us
    dot_general x1, matrix products, on_device(): jnp.einsum('fcsxyk,sktn->fctxyn', first, dft_matrix, preferred_element_ty...  16.2 us
  transfers between devices with their start and end apart: 9, of which 8 were waited for; matrix products, arithmetic and copies ran while one was open for 3% of the time, Pallas kernels for 0%

commit v1 on v0

v1 whole, which is shorter than its diff:
```python
import functools
import math

import jax
import jax.numpy as jnp
import numpy as np
from jax import lax
from jax.experimental import pallas as pl
from jax.experimental.pallas import tpu as pltpu
from jax.sharding import PartitionSpec as P

TAPS = 6
WIN = 8
YROWS = 8
META = 8
BETA = 13.9
EPS = 0.05
LAMBDA_TV = 0.3
TERMS = 40
VMEM_LIMIT = 56 * 1024 * 1024


def kaiser_coefficients():
    quarter = BETA * BETA / 4.0
    terms = [quarter**power / math.factorial(power) ** 2 for power in range(TERMS)]
    total = math.fsum(terms)
    return [term / total for term in terms]


def kaiser(distance):
    coefficients = kaiser_coefficients()
    inside = jnp.maximum(1.0 - distance / 3.0 * (distance / 3.0), 0.0)
    value = jnp.full_like(inside, coefficients[-1])
    for coefficient in coefficients[-2::-1]:
        value = value * inside + coefficient
    return value


def dft_angles(grid_size):
    positions = np.arange(grid_size)
    return (positions[:, None] * positions[None, :] % grid_size) * (2.0 * math.pi / grid_size)


def depth_table(grid_size):
    angles = dft_angles(grid_size)
    return jnp.asarray(np.concatenate([np.cos(angles), np.sin(angles)], axis=0), jnp.bfloat16)


def plane_table(grid_size):
    angles = dft_angles(grid_size)
    cosine, sine = np.cos(angles), np.sin(angles)
    return jnp.asarray(np.block([[cosine, -sine], [sine, cosine]]), jnp.bfloat16)


def row_tables(grid_size, first_row):
    rows = jnp.arange(grid_size + WIN)[:, None] * (first_row + jnp.arange(YROWS))[None, :]
    angles = (rows % grid_size).astype(jnp.float32) * (2.0 * math.pi / grid_size)
    shape = (grid_size + WIN, YROWS, 128)
    return (
        jnp.broadcast_to(jnp.cos(angles)[:, :, None], shape),
        jnp.broadcast_to(jnp.sin(angles)[:, :, None], shape),
    )


def frame_kernel(
    corner, own, other, cos_rows, sin_rows, depth_dft, plane_dft, maps_hbm, estimate_hbm,
    half, half_small,
    grid_real, grid_imag, weights, weight_x, weight_y, maps, estimate, sems,
    *, scale,
):
    blocks = own.shape[0]
    samples = own.shape[2]
    coils, _, slab, grid_size, _ = maps.shape
    plane_rows = coils * YROWS
    copies = [
        pltpu.make_async_copy(maps_hbm, maps, sems.at[0]),
        pltpu.make_async_copy(estimate_hbm.at[corner[0]], estimate, sems.at[1]),
    ]
    for copy in copies:
        copy.start()

    def clear(step, carry):
        zeros = jnp.zeros((plane_rows, 128), jnp.float32)
        at = pl.ds(pl.multiple_of(step * plane_rows, plane_rows), plane_rows)
        grid_real[at, :] = zeros
        grid_imag[at, :] = zeros
        return carry

    lax.fori_loop(0, grid_size + WIN, clear, 0)

    table = depth_dft[...]
    taps = lax.broadcasted_iota(jnp.int32, (8, samples), 0).astype(jnp.float32)
    cells = lax.broadcasted_iota(jnp.int32, (grid_size, samples), 0)

    def prepare(source, offset):
        def one(block):
            meta = source[block].astype(jnp.float32)[2 * coils :]
            density, frac_x, frac_y, frac_z, shift, depth = (meta[row : row + 1] for row in range(6))
            weight_x[offset + block] = kaiser(taps - 2.0 - frac_x) * density
            lag = taps - shift
            weight_y[offset + block] = jnp.where(
                (lag >= 0.0) & (lag < float(TAPS)), kaiser(lag - 2.0 - frac_y), 0.0
            )
            tap_z = kaiser(taps - 2.0 - frac_z)
            lag_z = (cells - depth.astype(jnp.int32)) & (grid_size - 1)
            spread = jnp.zeros((grid_size, samples), jnp.float32)
            for tap in range(TAPS):
                spread = jnp.where(lag_z == tap, tap_z[tap : tap + 1], spread)
            turned = jnp.dot(
                table, spread.astype(jnp.bfloat16), preferred_element_type=jnp.float32
            ).astype(jnp.bfloat16)
            real, imag = turned[:grid_size], turned[grid_size:]
            weights[offset + block, :, :samples] = turned
            weights[offset + block, :grid_size, samples:] = -imag
            weights[offset + block, grid_size:, samples:] = real

        def step(index, carry):
            for part in range(2):
                one(index * 2 + part)
            return carry

        lax.fori_loop(0, blocks // 2, step, 0)

    prepare(own, 0)
    prepare(other, blocks)

    def spread_planes(source, offset):
        def one(block):
            first_plane = corner[1 + 2 * (offset + block)]
            first_row = corner[2 + 2 * (offset + block)]
            payload = source[block].astype(jnp.float32)
            row_weights = weight_y[offset + block]
            turn_real = jnp.zeros((YROWS, samples), jnp.float32)
            turn_imag = jnp.zeros((YROWS, samples), jnp.float32)
            for row in range(WIN):
                weight = row_weights[row : row + 1]
                turn_real = turn_real + cos_rows[first_row + row] * weight
                turn_imag = turn_imag + sin_rows[first_row + row] * weight
            real, imag = [], []
            for coil in range(coils):
                amp_real = payload[2 * coil : 2 * coil + 1]
                amp_imag = payload[2 * coil + 1 : 2 * coil + 2]
                real.append(amp_real * turn_real - amp_imag * turn_imag)
                imag.append(amp_real * turn_imag + amp_imag * turn_real)
            amplitude = jnp.concatenate(
                [jnp.concatenate(real, axis=0), jnp.concatenate(imag, axis=0)], axis=1
            )
            plane_weights = weight_x[offset + block]
            plane_weights = jnp.concatenate([plane_weights, plane_weights], axis=1)
            depth_weights = weights[offset + block]
            base = first_plane * plane_rows
            for tap in range(TAPS):
                left = (amplitude * plane_weights[tap : tap + 1]).astype(jnp.bfloat16)
                product = lax.dot_general(
                    left, depth_weights, (((1,), (1,)), ((), ())),
                    preferred_element_type=jnp.float32,
                )
                at = pl.ds(pl.multiple_of(base + tap * plane_rows, plane_rows), plane_rows)
                grid_real[at, :] = grid_real[at, :] + product[:, :grid_size]
                grid_imag[at, :] = grid_imag[at, :] + product[:, grid_size:]

        def step(index, carry):
            for part in range(2):
                one(index * 2 + part)
            return carry

        lax.fori_loop(0, blocks // 2, step, 0)

    spread_planes(own, 0)
    spread_planes(other, blocks)

    wrap = (TAPS - 1) * plane_rows
    for ref in (grid_real, grid_imag):
        ref[:wrap, :] = ref[:wrap, :] + ref[grid_size * plane_rows : grid_size * plane_rows + wrap, :]

    for copy in copies:
        copy.wait()
    plane_matrix = plane_dft[...]

    def image_row(row, carry):
        total_real = jnp.zeros((grid_size, grid_size), jnp.float32)
        total_imag = jnp.zeros((grid_size, grid_size), jnp.float32)
        for pair in range(coils // 2):
            columns = []
            for coil in (2 * pair, 2 * pair + 1):
                at = pl.ds(coil * YROWS + row, grid_size, stride=plane_rows)
                columns.append(jnp.concatenate(
                    [grid_real[at, :].astype(jnp.bfloat16), grid_imag[at, :].astype(jnp.bfloat16)],
                    axis=0,
                ))
            images = jnp.dot(
                plane_matrix, jnp.concatenate(columns, axis=1), preferred_element_type=jnp.float32
            )
            for place, coil in enumerate((2 * pair, 2 * pair + 1)):
                image = images[:, place * grid_size : (place + 1) * grid_size]
                image_real, image_imag = image[:grid_size], image[grid_size:]
                map_real = maps[coil, 0, row].astype(jnp.float32)
                map_imag = maps[coil, 1, row].astype(jnp.float32)
                total_real = total_real + (map_real * image_real + map_imag * image_imag)
                total_imag = total_imag + (map_real * image_imag - map_imag * image_real)
        for part, total in enumerate((total_real, total_imag)):
            value = estimate[part, row] + scale * total
            half[part, row] = value
            half_small[part, row] = value.astype(jnp.bfloat16)
        return carry

    lax.fori_loop(0, slab, image_row, 0)


def frame_image(corner, own, other, tables, coil_maps, estimate, scale):
    blocks, _, samples = own.shape
    coils, _, slab, grid_size, _ = coil_maps.shape
    shape = (2, slab, grid_size, grid_size)
    whole = pl.BlockSpec(memory_space=pltpu.VMEM)
    away = pl.BlockSpec(memory_space=pl.ANY)
    grid_shape = ((grid_size + WIN) * coils * YROWS, grid_size)
    return pl.pallas_call(
        functools.partial(frame_kernel, scale=scale),
        out_shape=(
            jax.ShapeDtypeStruct(shape, jnp.float32),
            jax.ShapeDtypeStruct(shape, jnp.bfloat16),
        ),
        in_specs=[pl.BlockSpec(memory_space=pltpu.SMEM)] + [whole] * 6 + [away] * 2,
        out_specs=(whole, whole),
        scratch_shapes=[
            pltpu.VMEM(grid_shape, jnp.float32),
            pltpu.VMEM(grid_shape, jnp.float32),
            pltpu.VMEM((2 * blocks, 2 * grid_size, 2 * samples), jnp.bfloat16),
            pltpu.VMEM((2 * blocks, 8, samples), jnp.float32),
            pltpu.VMEM((2 * blocks, 8, samples), jnp.float32),
            pltpu.VMEM(coil_maps.shape, jnp.bfloat16),
            pltpu.VMEM(shape, jnp.float32),
            pltpu.SemaphoreType.DMA((2,)),
        ],
        compiler_params=pltpu.CompilerParams(vmem_limit_bytes=VMEM_LIMIT),
        cost_estimate=pl.CostEstimate(
            flops=2 * 2 * blocks * TAPS * coils * YROWS * 4 * samples * grid_size,
            bytes_accessed=coil_maps.size * 2,
            transcendentals=0,
        ),
    )(corner, own, other, *tables, coil_maps, estimate)


def swap(values, axis, bit):
    count = lax.axis_size(axis)
    return lax.ppermute(values, axis, [(index, index ^ bit) for index in range(count)])


def gather_blocks(packed):
    count = lax.axis_size("tile")
    held = packed[None]
    bits = [1 << place for place in range(1, count.bit_length() - 1)]
    for bit in reversed(bits):
        held = jnp.concatenate([held, swap(held, "tile", bit)], axis=0)
    held = held.reshape((-1,) + packed.shape[1:])
    return held, swap(held, "tile", 1)


def on_device(
    kspace_samples, density, sample_frac, row_offsets, depth_base, block_base, coil_maps, estimate
):
    tile_count = lax.axis_size("tile")
    tile_here = lax.axis_index("tile")
    frame_count = lax.axis_size("frame")
    frame_here = lax.axis_index("frame")
    frames_local, blocks_local, channels, sample_count = kspace_samples.shape
    grid_size = coil_maps.shape[3]
    slab = coil_maps.shape[2]
    scale = 1.0 / (8.0 * math.sqrt(blocks_local * tile_count * sample_count))
    last = frames_local - 1

    corner_rows = jnp.broadcast_to(
        block_base.astype(jnp.bfloat16)[..., None], block_base.shape + (sample_count,)
    )
    packed = jnp.concatenate(
        [
            kspace_samples,
            density[:, :, None],
            sample_frac,
            row_offsets.astype(jnp.bfloat16)[:, :, None],
            depth_base.astype(jnp.bfloat16)[:, :, None],
            corner_rows,
        ],
        axis=2,
    )
    tables = row_tables(grid_size, tile_here * slab) + (
        depth_table(grid_size), plane_table(grid_size),
    )
    even = frame_here % 2 == 0
    order = [jnp.where(even, last, 0), jnp.where(even, 0, last)]

    halves, received = [], []
    for place, frame in enumerate(order):
        own, other = gather_blocks(lax.dynamic_index_in_dim(packed, frame, 0, keepdims=False))
        corner = jnp.concatenate([own[:, -2:, 0], other[:, -2:, 0]], axis=0)
        corner = jnp.concatenate([frame[None].astype(jnp.int32), corner.reshape(-1).astype(jnp.int32)])
        half, small = frame_image(corner, own, other, tables, coil_maps, estimate, scale)
        halves.append(half)
        if place == 0:
            pairs = [(index, index ^ 1) for index in range(frame_count) if index ^ 1 < frame_count]
        else:
            pairs = [(index, index - 1) for index in range(2, frame_count, 2)]
            pairs += [(target, source) for source, target in pairs]
        received.append(lax.ppermute(small, "frame", pairs) if pairs else jnp.zeros_like(small))

    first = jnp.where(even, halves[1], halves[0])
    second = jnp.where(even, halves[0], halves[1])
    before = jnp.where(even, received[1], received[0]).astype(jnp.float32)
    after = jnp.where(even, received[0], received[1]).astype(jnp.float32)

    def psi(low, high):
        change = high - low
        return change / jnp.sqrt(
            change[0] * change[0] + change[1] * change[1] + EPS * EPS
        )[None]

    middle = psi(first, second)
    low = jnp.where(frame_here > 0, psi(before, first), 0.0)
    high = jnp.where(frame_here < frame_count - 1, psi(second, after), 0.0)
    return jnp.stack(
        [first - LAMBDA_TV * (low - middle), second - LAMBDA_TV * (middle - high)], axis=0
    )


def solution(mesh):
    in_specs = (
        P("frame", "tile", None, None),
        P("frame", "tile", None),
        P("frame", "tile", None, None),
        P("frame", "tile", None),
        P("frame", "tile", None),
        P("frame", "tile", None),
        P(None, None, "tile", None, None),
        P("frame", None, "tile", None, None),
    )
    out_specs = P("frame", None, "tile", None, None)
    return jax.shard_map(
        on_device, mesh=mesh, in_specs=in_specs, out_specs=out_specs, check_vma=False
    )
```

time: 619 us -> 133 us (0.21)
  the two profiles are of different devices: /device:TPU:12 before, /device:TPU:0 now
where the time goes in v1:
time: 133 us
  Pallas kernels  96.4 us (72%)
  starting transfers between devices  13 us (10%)
  waiting for transfers between devices  9.19 us (7%)
  other arithmetic  8.39 us (6%)
  local copies, waits for them, and re-layouts  5.69 us (4%)
    pallas_call x2, Pallas kernels, frame_image(): pl.pallas_call(functools.partial(frame_kernel, scale=scale), out_shape=(j...  96.4 us
    ppermute x8, starting transfers between devices, swap(): lax.ppermute(values, axis, [(index, index ^ bit) for index in range(count)])  11.3 us
    ppermute x8, waiting for transfers between devices, swap(): lax.ppermute(values, axis, [(index, index ^ bit) for index in range(count)])  9.19 us
  transfers between devices with their start and end apart: 9, of which 6 were waited for; matrix products, arithmetic and copies ran while one was open for 1% of the time, Pallas kernels for 36%

profile of v1, /device:TPU:0, one launch (start us, length us, event | category | flops | bytes accessed | tf_op | source)
XLA Modules:
  0.0 133.0 jit_solution(6466631815989090192)
XLA Ops:
  0.0 0.7 convert_element_type.39
  0.8 0.7 convert_bitcast_fusion.1
  1.5 0.7 convert_bitcast_fusion
  2.2 0.7 copy.34
  2.9 0.7 copy.35
  3.7 0.9 concatenate.37
  4.6 4.1 %collective-permute-start.4 = (bf16[1,4,40,128]{3,2,1,0:T(8,128)(2,1)S(1)}, bf16[1,4,40,128]{3,2,1,0:T(8,128)(2,1)S(1)}, u32[]{:S(2)}, u32[]{:S(2)}) collective-permute-start(bf16[1,4,40,128]{3,2,1,0:T(8,128)(2,1)S(1)} %get-tuple-element.18), channel_id=1, source_target_pairs={{0,8},{1,9},{2,10},{3,11},{4,12},{5,13},{6,14},{7,15},{8,0},{9,1},... | collective-permute-start | bytes 122888 | tf_op jit(solution)/shard_map/ppermute | solution.py:246
  8.8 2.3 %collective-permute-done.4 = bf16[1,4,40,128]{3,2,1,0:T(8,128)(2,1)S(1)} collective-permute-done((bf16[1,4,40,128]{3,2,1,0:T(8,128)(2,1)S(1)}, bf16[1,4,40,128]{3,2,1,0:T(8,128)(2,1)S(1)}, u32[]{:S(2)}, u32[]{:S(2)}) %collective-permute-start.4) | collective-permute-done | bytes 40992 | tf_op jit(solution)/shard_map/ppermute | solution.py:246
  11.1 1.9 %collective-permute-start.5 = (bf16[2,4,40,128]{3,2,1,0:T(8,128)(2,1)S(1)}, bf16[2,4,40,128]{3,2,1,0:T(8,128)(2,1)S(1)}, u32[]{:S(2)}, u32[]{:S(2)}) collective-permute-start(bf16[2,4,40,128]{3,2,1,0:T(8,128)(2,1)S(1)} %pad_maximum_fusion.6), channel_id=1, source_target_pairs={{0,4},{1,5},{2,6},{3,7},{4,0},{5,1},{6,2},{7,3},{8,12},{9,13},{10,... | collective-permute-start | bytes 245768 | tf_op jit(solution)/shard_map/ppermute | solution.py:246
  13.1 0.7 collective-permute-done
  13.7 1.5 %collective-permute-start.1 = (bf16[2,4,40,128]{3,2,1,0:T(8,128)(2,1)S(1)}, bf16[2,4,40,128]{3,2,1,0:T(8,128)(2,1)S(1)}, u32[]{:S(2)}, u32[]{:S(2)}) collective-permute-start(bf16[2,4,40,128]{3,2,1,0:T(8,128)(2,1)S(1)} %pad_maximum_fusion.5), channel_id=1, source_target_pairs={{0,4},{1,5},{2,6},{3,7},{4,0},{5,1},{6,2},{7,3},{8,12},{9,13},{10,... | collective-permute-start | bytes 245768 | tf_op jit(solution)/shard_map/ppermute | solution.py:246
  15.2 1.1 collective-permute-done.5
  16.3 2.0 %collective-permute-start.6 = (bf16[4,4,40,128]{3,2,1,0:T(8,128)(2,1)S(1)}, bf16[4,4,40,128]{3,2,1,0:T(8,128)(2,1)S(1)}, u32[]{:S(2)}, u32[]{:S(2)}) collective-permute-start(bf16[4,4,40,128]{3,2,1,0:T(8,128)(2,1)S(1)} %pad_maximum_fusion.4), channel_id=1, source_target_pairs={{0,2},{1,3},{2,0},{3,1},{4,6},{5,7},{6,4},{7,5},{8,10},{9,11},{10,... | collective-permute-start | bytes 491528 | tf_op jit(solution)/shard_map/ppermute | solution.py:246
  18.3 1.5 %collective-permute-start.2 = (bf16[4,4,40,128]{3,2,1,0:T(8,128)(2,1)S(1)}, bf16[4,4,40,128]{3,2,1,0:T(8,128)(2,1)S(1)}, u32[]{:S(2)}, u32[]{:S(2)}) collective-permute-start(bf16[4,4,40,128]{3,2,1,0:T(8,128)(2,1)S(1)} %pad_maximum_fusion.3), channel_id=1, source_target_pairs={{0,2},{1,3},{2,0},{3,1},{4,6},{5,7},{6,4},{7,5},{8,10},{9,11},{10,... | collective-permute-start | bytes 491528 | tf_op jit(solution)/shard_map/ppermute | solution.py:246
  19.9 2.9 %collective-permute-done.6 = bf16[4,4,40,128]{3,2,1,0:T(8,128)(2,1)S(1)} collective-permute-done((bf16[4,4,40,128]{3,2,1,0:T(8,128)(2,1)S(1)}, bf16[4,4,40,128]{3,2,1,0:T(8,128)(2,1)S(1)}, u32[]{:S(2)}, u32[]{:S(2)}) %collective-permute-start.6) | collective-permute-done | bytes 163872 | tf_op jit(solution)/shard_map/ppermute | solution.py:246
  22.9 1.6 %collective-permute-done.2 = bf16[4,4,40,128]{3,2,1,0:T(8,128)(2,1)S(1)} collective-permute-done((bf16[4,4,40,128]{3,2,1,0:T(8,128)(2,1)S(1)}, bf16[4,4,40,128]{3,2,1,0:T(8,128)(2,1)S(1)}, u32[]{:S(2)}, u32[]{:S(2)}) %collective-permute-start.2) | collective-permute-done | bytes 163872 | tf_op jit(solution)/shard_map/ppermute | solution.py:246
  27.4 1.0 broadcast_in_dim.53.cos_rows
  28.4 1.0 broadcast_in_dim.54.sin_rows
  29.4 48.2 %shard_map.101 = (f32[2,8,128,128]{3,2,1,0:T(8,128)}, bf16[2,8,128,128]{3,2,1,0:T(8,128)(2,1)}) custom-call(s32[129]{0:T(256)} %pad_add_fusion.1.corner, bf16[32,40,128]{2,1,0:T(8,128)(2,1)} %bitcast.28, bf16[32,40,128]{2,1,0:T(8,128)(2,1)} %copy-done.5, f32[136,8,128]{2,1,0:T(8,128)} %broadcast_in_dim.53.cos_rows, ...), custom_call_target="tpu_custom_call" | custom-call | flops 6442450944 | bytes 8388608 | tf_op jit(solution)/shard_map/pallas_call | solution.py:217
  77.6 1.8 %collective-permute-start.8 = (bf16[2,8,128,128]{3,2,1,0:T(8,128)(2,1)}, bf16[2,8,128,128]{3,2,1,0:T(8,128)(2,1)S(1)}, u32[]{:S(2)}, u32[]{:S(2)}) collective-permute-start(bf16[2,8,128,128]{3,2,1,0:T(8,128)(2,1)} %get-tuple-element.10), channel_id=1, source_target_pairs={{0,16},{16,0},{1,17},{17,1},{2,18},{18,2},{3,19},{19,3},{4,20},{20... | collective-permute-start | bytes 1572872 | tf_op jit(solution)/shard_map/ppermute | solution.py:304
  80.0 48.3 %shard_map.100 = (f32[2,8,128,128]{3,2,1,0:T(8,128)}, bf16[2,8,128,128]{3,2,1,0:T(8,128)(2,1)}) custom-call(s32[129]{0:T(256)} %pad_add_fusion.corner, bf16[32,40,128]{2,1,0:T(8,128)(2,1)} %bitcast.25, bf16[32,40,128]{2,1,0:T(8,128)(2,1)} %copy-done.4, f32[136,8,128]{2,1,0:T(8,128)} %broadcast_in_dim.53.cos_rows, f32[136,8,128]{2,1,0:T(8,128)} %broadcast_in_dim.54.sin_rows, ...), custom_call_target="tpu_custom_call" | custom-call | flops 6442450944 | bytes 8388608 | tf_op jit(solution)/shard_map/pallas_call | solution.py:217
  128.3 1.5 %convert_subtract_fusion.1 = (f32[2,8,128,128]{3,2,1,0:T(8,128)S(1)}, f32[2,8,128,128]{3,2,1,0:T(8,128)S(1)}) fusion(bf16[2,8,128,128]{3,2,1,0:T(8,128)(2,1)S(1)} %collective-permute-done.8, pred[]{:T(512)S(6)} %eq.7, f32[2,8,128,128]{3,2,1,0:T(8,128)} %get-tuple-element.8, f32[2,8,128,128]{3,2,1,0:T(8,128)S(1)} %copy-done), kind=kLoop, calls=%fused_computation.4 | loop fusion | flops 1048576 | bytes 4718593 | tf_op jit(solution)/shard_map/sub | solution.py:312
  130.8 0.7 subtract_bitcast_fusion.1
  131.5 1.5 %pad_maximum_fusion = f32[2,2,8,128,128]{4,3,2,1,0:T(8,128)} fusion(f32[1,2,8,128,128]{4,3,2,1,0:T(8,128)S(1)} %get-tuple-element.16, f32[1,2,8,128,128]{4,3,2,1,0:T(8,128)S(1)} %get-tuple-element.15), kind=kLoop, calls=%fused_computation | loop fusion | flops 524288 | bytes 4194304 | tf_op jit(solution)/shard_map/stack | solution.py:320
  (54 shorter events, 4.8 us)
Async XLA Ops:
  4.6 6.5 %collective-permute-start.4 = (bf16[1,4,40,128]{3,2,1,0:T(8,128)(2,1)S(1)}, bf16[1,4,40,128]{3,2,1,0:T(8,128)(2,1)S(1)}, u32[]{:S(2)}, u32[]{:S(2)}) collective-permute-start(bf16[1,4,40,128]{3,2,1,0:T(8,128)(2,1)S(1)} %get-tuple-element.18), channel_id=1, source_target_pairs={{0,8},{1,9},{2,10},{3,11},{4,12},{5,13},{6,14},{7,15},{8,0},{9,1},... | collective-permute-start | bytes 122888 | tf_op jit(solution)/shard_map/ppermute | solution.py:246
  8.7 5.0 %collective-permute-start = (bf16[1,4,40,128]{3,2,1,0:T(8,128)(2,1)S(1)}, bf16[1,4,40,128]{3,2,1,0:T(8,128)(2,1)S(1)}, u32[]{:S(2)}, u32[]{:S(2)}) collective-permute-start(bf16[1,4,40,128]{3,2,1,0:T(8,128)(2,1)S(1)} %get-tuple-element.17), channel_id=1, source_target_pairs={{0,8},{1,9},{2,10},{3,11},{4,12},{5,13},{6,14},{7,15},{8,0},{9,1},... | collective-permute-start | bytes 122888 | tf_op jit(solution)/shard_map/ppermute | solution.py:246
  11.1 5.2 %collective-permute-start.5 = (bf16[2,4,40,128]{3,2,1,0:T(8,128)(2,1)S(1)}, bf16[2,4,40,128]{3,2,1,0:T(8,128)(2,1)S(1)}, u32[]{:S(2)}, u32[]{:S(2)}) collective-permute-start(bf16[2,4,40,128]{3,2,1,0:T(8,128)(2,1)S(1)} %pad_maximum_fusion.6), channel_id=1, source_target_pairs={{0,4},{1,5},{2,6},{3,7},{4,0},{5,1},{6,2},{7,3},{8,12},{9,13},{10,... | collective-permute-start | bytes 245768 | tf_op jit(solution)/shard_map/ppermute | solution.py:246
  13.7 4.6 %collective-permute-start.1 = (bf16[2,4,40,128]{3,2,1,0:T(8,128)(2,1)S(1)}, bf16[2,4,40,128]{3,2,1,0:T(8,128)(2,1)S(1)}, u32[]{:S(2)}, u32[]{:S(2)}) collective-permute-start(bf16[2,4,40,128]{3,2,1,0:T(8,128)(2,1)S(1)} %pad_maximum_fusion.5), channel_id=1, source_target_pairs={{0,4},{1,5},{2,6},{3,7},{4,0},{5,1},{6,2},{7,3},{8,12},{9,13},{10,... | collective-permute-start | bytes 245768 | tf_op jit(solution)/shard_map/ppermute | solution.py:246
  16.3 6.4 %collective-permute-start.6 = (bf16[4,4,40,128]{3,2,1,0:T(8,128)(2,1)S(1)}, bf16[4,4,40,128]{3,2,1,0:T(8,128)(2,1)S(1)}, u32[]{:S(2)}, u32[]{:S(2)}) collective-permute-start(bf16[4,4,40,128]{3,2,1,0:T(8,128)(2,1)S(1)} %pad_maximum_fusion.4), channel_id=1, source_target_pairs={{0,2},{1,3},{2,0},{3,1},{4,6},{5,7},{6,4},{7,5},{8,10},{9,11},{10,... | collective-permute-start | bytes 491528 | tf_op jit(solution)/shard_map/ppermute | solution.py:246
  18.3 6.2 %collective-permute-start.2 = (bf16[4,4,40,128]{3,2,1,0:T(8,128)(2,1)S(1)}, bf16[4,4,40,128]{3,2,1,0:T(8,128)(2,1)S(1)}, u32[]{:S(2)}, u32[]{:S(2)}) collective-permute-start(bf16[4,4,40,128]{3,2,1,0:T(8,128)(2,1)S(1)} %pad_maximum_fusion.3), channel_id=1, source_target_pairs={{0,2},{1,3},{2,0},{3,1},{4,6},{5,7},{6,4},{7,5},{8,10},{9,11},{10,... | collective-permute-start | bytes 491528 | tf_op jit(solution)/shard_map/ppermute | solution.py:246
  22.8 6.6 %copy-start.3 = (bf16[8,4,40,128]{3,2,1,0:T(8,128)(2,1)}, bf16[8,4,40,128]{3,2,1,0:T(8,128)(2,1)S(1)}, u32[]{:S(2)}) copy-start(bf16[8,4,40,128]{3,2,1,0:T(8,128)(2,1)S(1)} %pad_maximum_fusion.2) | copy-start | bytes 983044
  22.8 2.4 %collective-permute-start.7 = (bf16[32,40,128]{2,1,0:T(8,128)(2,1)S(1)}, bf16[32,40,128]{2,1,0:T(8,128)(2,1)S(1)}, u32[]{:S(2)}, u32[]{:S(2)}) collective-permute-start(bf16[32,40,128]{2,1,0:T(8,128)(2,1)S(1)} %bitcast.26), channel_id=1, source_target_pairs={{0,1},{1,0},{2,3},{3,2},{4,5},{5,4},{6,7},{7,6},{8,9},{9,8},{10,11... | collective-permute-start | bytes 983048 | tf_op jit(solution)/shard_map/ppermute | solution.py:246
  24.6 53.0 %copy-start.2 = (bf16[8,4,40,128]{3,2,1,0:T(8,128)(2,1)}, bf16[8,4,40,128]{3,2,1,0:T(8,128)(2,1)S(1)}, u32[]{:S(2)}) copy-start(bf16[8,4,40,128]{3,2,1,0:T(8,128)(2,1)S(1)} %pad_maximum_fusion.1) | copy-start | bytes 983044
  24.6 1.7 %collective-permute-start.3 = (bf16[32,40,128]{2,1,0:T(8,128)(2,1)S(1)}, bf16[32,40,128]{2,1,0:T(8,128)(2,1)S(1)}, u32[]{:S(2)}, u32[]{:S(2)}) collective-permute-start(bf16[32,40,128]{2,1,0:T(8,128)(2,1)S(1)} %bitcast.23), channel_id=1, source_target_pairs={{0,1},{1,0},{2,3},{3,2},{4,5},{5,4},{6,7},{7,6},{8,9},{9,8},{10,11... | collective-permute-start | bytes 983048 | tf_op jit(solution)/shard_map/ppermute | solution.py:246
  25.2 4.1 %copy-start.5 = (bf16[32,40,128]{2,1,0:T(8,128)(2,1)}, bf16[32,40,128]{2,1,0:T(8,128)(2,1)S(1)}, u32[]{:S(2)}) copy-start(bf16[32,40,128]{2,1,0:T(8,128)(2,1)S(1)} %collective-permute-done.7.other) | copy-start | bytes 983044
  26.3 51.3 %copy-start.4 = (bf16[32,40,128]{2,1,0:T(8,128)(2,1)}, bf16[32,40,128]{2,1,0:T(8,128)(2,1)S(1)}, u32[]{:S(2)}) copy-start(bf16[32,40,128]{2,1,0:T(8,128)(2,1)S(1)} %collective-permute-done.3.other) | copy-start | bytes 983044
  77.6 50.7 %collective-permute-start.8 = (bf16[2,8,128,128]{3,2,1,0:T(8,128)(2,1)}, bf16[2,8,128,128]{3,2,1,0:T(8,128)(2,1)S(1)}, u32[]{:S(2)}, u32[]{:S(2)}) collective-permute-start(bf16[2,8,128,128]{3,2,1,0:T(8,128)(2,1)} %get-tuple-element.10), channel_id=1, source_target_pairs={{0,16},{16,0},{1,17},{17,1},{2,18},{18,2},{3,19},{19,3},{4,20},{20... | collective-permute-start | bytes 1572872 | tf_op jit(solution)/shard_map/ppermute | solution.py:304
  80.0 48.3 %copy-start = (f32[2,8,128,128]{3,2,1,0:T(8,128)S(1)}, f32[2,8,128,128]{3,2,1,0:T(8,128)}, u32[]{:S(2)}) copy-start(f32[2,8,128,128]{3,2,1,0:T(8,128)} %get-tuple-element.9) | copy-start | bytes 3145732
  128.3 1.7 %copy-start.1 = (f32[2,8,128,128]{3,2,1,0:T(8,128)S(1)}, f32[2,8,128,128]{3,2,1,0:T(8,128)}, u32[]{:S(2)}) copy-start(f32[2,8,128,128]{3,2,1,0:T(8,128)} %get-tuple-element.8) | copy-start | bytes 3145732

commit v2 on v1

v2 whole, which is shorter than its diff:
```python
import functools
import math

import jax
import jax.numpy as jnp
import numpy as np
from jax import lax
from jax.experimental import pallas as pl
from jax.experimental.pallas import tpu as pltpu
from jax.sharding import PartitionSpec as P

TAPS = 6
WIN = 8
YROWS = 8
META = 8
BETA = 13.9
EPS = 0.05
LAMBDA_TV = 0.3
TERMS = 40
UNROLL = 8
VMEM_LIMIT = 56 * 1024 * 1024


def kaiser_coefficients():
    quarter = BETA * BETA / 4.0
    terms = [quarter**power / math.factorial(power) ** 2 for power in range(TERMS)]
    total = math.fsum(terms)
    return [term / total for term in terms]


def kaiser(distance):
    coefficients = kaiser_coefficients()
    inside = jnp.maximum(1.0 - distance / 3.0 * (distance / 3.0), 0.0)
    value = jnp.full_like(inside, coefficients[-1])
    for coefficient in coefficients[-2::-1]:
        value = value * inside + coefficient
    return value


def dft_angles(grid_size):
    positions = np.arange(grid_size)
    return (positions[:, None] * positions[None, :] % grid_size) * (2.0 * math.pi / grid_size)


def depth_table(grid_size):
    angles = dft_angles(grid_size)
    return jnp.asarray(np.concatenate([np.cos(angles), np.sin(angles)], axis=0), jnp.bfloat16)


def plane_table(grid_size):
    angles = dft_angles(grid_size)
    cosine, sine = np.cos(angles), np.sin(angles)
    parts = np.stack([np.concatenate([cosine, -sine], 1), np.concatenate([sine, cosine], 1)])
    tiles = parts.reshape(2, grid_size // 8, 8, 2 * grid_size).swapaxes(0, 1)
    return jnp.asarray(tiles.reshape(2 * grid_size, 2 * grid_size), jnp.bfloat16)


def row_tables(grid_size, first_row):
    rows = jnp.arange(grid_size + WIN)[:, None] * (first_row + jnp.arange(YROWS))[None, :]
    angles = (rows % grid_size).astype(jnp.float32) * (2.0 * math.pi / grid_size)
    shape = (grid_size + WIN, YROWS, 128)
    return (
        jnp.broadcast_to(jnp.cos(angles)[:, :, None], shape),
        jnp.broadcast_to(jnp.sin(angles)[:, :, None], shape),
    )


def frame_kernel(
    corner, own, other, cos_rows, sin_rows, depth_dft, plane_dft, maps_hbm, estimate_hbm,
    half, half_small,
    grid_real, grid_imag, left, weights, weight_x, weight_y, columns, maps, estimate, total, sems,
    *, scale,
):
    blocks = own.shape[0]
    samples = own.shape[2]
    unroll = len(left)
    coils, _, slab, grid_size, _ = maps.shape
    copies = [
        pltpu.make_async_copy(maps_hbm, maps, sems.at[0]),
        pltpu.make_async_copy(estimate_hbm.at[corner[0]], estimate, sems.at[1]),
    ]
    for copy in copies:
        copy.start()

    table = depth_dft[...]
    taps = lax.broadcasted_iota(jnp.int32, (8, 2 * samples), 0).astype(jnp.float32)
    cells = lax.broadcasted_iota(jnp.int32, (grid_size, 2 * samples), 0).astype(jnp.bfloat16)
    clear_rows = grid_real[0].shape[0] // (blocks // unroll)

    def prepare(source, offset, cleared):
        def two(first):
            meta = jnp.concatenate(
                [source[first + part].astype(jnp.float32)[2 * coils :] for part in range(2)], axis=1
            )
            density, frac_x, frac_y, frac_z, shift, depth = (meta[row : row + 1] for row in range(6))
            tap_x = kaiser(taps - 2.0 - frac_x) * density
            lag = taps - shift
            tap_y = jnp.where((lag >= 0.0) & (lag < float(TAPS)), kaiser(lag - 2.0 - frac_y), 0.0)
            tap_z = kaiser(taps - 2.0 - frac_z).astype(jnp.bfloat16)
            cell = depth + taps
            cell = jnp.where(cell >= float(grid_size), cell - float(grid_size), cell)
            cell = cell.astype(jnp.bfloat16)
            spread = jnp.zeros((grid_size, 2 * samples), jnp.bfloat16)
            for tap in range(TAPS):
                spread = jnp.where(cells == cell[tap : tap + 1], tap_z[tap : tap + 1], spread)
            turned = jnp.dot(table, spread, preferred_element_type=jnp.float32).astype(jnp.bfloat16)
            real, imag = turned[:grid_size], turned[grid_size:]
            for part in range(2):
                at, here = offset + first + part, slice(part * samples, (part + 1) * samples)
                weight_x[at] = tap_x[:, here]
                weight_y[at] = tap_y[:, here]
                weights[at, :, :samples] = turned[:, here]
                weights[at, :grid_size, samples:] = -imag[:, here]
                weights[at, grid_size:, samples:] = real[:, here]

        def step(index, carry):
            for ref in cleared:
                at = pl.ds(pl.multiple_of(index * clear_rows, 8), clear_rows)
                ref[at, :] = jnp.zeros((clear_rows, grid_size), jnp.float32)
            for part in range(0, unroll, 2):
                two(index * unroll + part)
            return carry

        lax.fori_loop(0, blocks // unroll, step, 0)

    prepare(own, 0, grid_real)
    prepare(other, blocks, grid_imag)

    def build(source, offset, block, slot):
        first_row = corner[2 + 2 * (offset + block)]
        payload = source[block].astype(jnp.float32)
        row_weights = weight_y[offset + block]
        plane_weights = weight_x[offset + block]
        turn_real = jnp.zeros((YROWS, samples), jnp.float32)
        turn_imag = jnp.zeros((YROWS, samples), jnp.float32)
        for row in range(WIN):
            weight = row_weights[row : row + 1]
            turn_real = turn_real + cos_rows[first_row + row] * weight
            turn_imag = turn_imag + sin_rows[first_row + row] * weight
        by_plane = []
        for tap in range(0, TAPS, 2):
            by_plane.append(jnp.concatenate(
                [jnp.broadcast_to(plane_weights[at : at + 1], (YROWS, samples)) for at in (tap, tap + 1)],
                axis=0,
            ).astype(jnp.bfloat16))
        for coil in range(coils):
            amp_real = payload[2 * coil : 2 * coil + 1]
            amp_imag = payload[2 * coil + 1 : 2 * coil + 2]
            parts = (
                amp_real * turn_real - amp_imag * turn_imag,
                amp_real * turn_imag + amp_imag * turn_real,
            )
            for part, value in enumerate(parts):
                twice = jnp.concatenate([value, value], axis=0).astype(jnp.bfloat16)
                for pair, weight in enumerate(by_plane):
                    left[slot][
                        pl.ds(coil * TAPS * YROWS + pair * 2 * YROWS, 2 * YROWS),
                        pl.ds(part * samples, samples),
                    ] = twice * weight

    def spread(offset, block, slot):
        first_plane = corner[1 + 2 * (offset + block)]
        product = lax.dot_general(
            left[slot][...], weights[offset + block], (((1,), (1,)), ((), ())),
            preferred_element_type=jnp.float32,
        )
        rows = TAPS * YROWS
        for coil in range(coils):
            at = pl.ds(pl.multiple_of(first_plane * YROWS, YROWS), rows)
            part = product[coil * rows : (coil + 1) * rows]
            grid_real[coil][at, :] = grid_real[coil][at, :] + part[:, :grid_size]
            grid_imag[coil][at, :] = grid_imag[coil][at, :] + part[:, grid_size:]

    def spread_planes(source, offset):
        build(source, offset, 0, 0)

        def step(index, carry):
            block = index * unroll
            for part in range(unroll):
                later = jnp.minimum(block + part + 1, blocks - 1)
                build(source, offset, later, (part + 1) % unroll)
                spread(offset, block + part, part)
            return carry

        lax.fori_loop(0, blocks // unroll, step, 0)

    spread_planes(own, 0)
    spread_planes(other, blocks)

    wrap = (TAPS - 1) * YROWS
    top = grid_size * YROWS
    for ref in grid_real + grid_imag:
        ref[:wrap, :] = ref[:wrap, :] + ref[top : top + wrap, :]

    for copy in copies:
        copy.wait()

    def transpose(row, slot):
        at = pl.ds(row, grid_size, stride=YROWS)
        for coil in range(coils):
            lanes = pl.ds((coil % 2) * grid_size, grid_size)
            columns[slot][coil // 2, :grid_size, lanes] = grid_real[coil][at, :].astype(jnp.bfloat16)
            columns[slot][coil // 2, grid_size:, lanes] = grid_imag[coil][at, :].astype(jnp.bfloat16)

    def image_row(row, slot):
        for quad in range(coils // 4):
            images = [
                jnp.dot(plane_dft[...], columns[slot][pair], preferred_element_type=jnp.float32)
                for pair in (2 * quad, 2 * quad + 1)
            ]
            for tile in range(grid_size // 16):
                sums = [[], []]
                for place in range(4):
                    coil = 4 * quad + place
                    column = (place % 2) * grid_size
                    image = images[place // 2][tile * 32 : tile * 32 + 32, column : column + grid_size]
                    image_real = jnp.concatenate([image[:8], image[16:24]], axis=0)
                    image_imag = jnp.concatenate([image[8:16], image[24:]], axis=0)
                    map_real = maps[coil, 0, row, pl.ds(tile * 16, 16)].astype(jnp.float32)
                    map_imag = maps[coil, 1, row, pl.ds(tile * 16, 16)].astype(jnp.float32)
                    sums[0].append(map_real * image_real + map_imag * image_imag)
                    sums[1].append(map_real * image_imag - map_imag * image_real)
                at = pl.ds(tile * 16, 16)
                for part in range(2):
                    value = (sums[part][0] + sums[part][1]) + (sums[part][2] + sums[part][3])
                    if quad > 0:
                        value = value + total[part, at]
                    if quad < coils // 4 - 1:
                        total[part, at] = value
                    else:
                        value = estimate[part, row, at] + scale * value
                        half[part, row, at] = value
                        half_small[part, row, at] = value.astype(jnp.bfloat16)

    transpose(0, 0)

    def two_rows(index, carry):
        row = 2 * index
        transpose(row + 1, 1)
        image_row(row, 0)
        transpose(jnp.minimum(row + 2, slab - 1), 0)
        image_row(row + 1, 1)
        return carry

    lax.fori_loop(0, slab // 2, two_rows, 0)


def frame_image(corner, own, other, tables, coil_maps, estimate, scale):
    blocks, _, samples = own.shape
    coils, _, slab, grid_size, _ = coil_maps.shape
    shape = (2, slab, grid_size, grid_size)
    whole = pl.BlockSpec(memory_space=pltpu.VMEM)
    away = pl.BlockSpec(memory_space=pl.ANY)
    grid_shape = ((grid_size + WIN) * YROWS, grid_size)
    return pl.pallas_call(
        functools.partial(frame_kernel, scale=scale),
        out_shape=(
            jax.ShapeDtypeStruct(shape, jnp.float32),
            jax.ShapeDtypeStruct(shape, jnp.bfloat16),
        ),
        in_specs=[pl.BlockSpec(memory_space=pltpu.SMEM)] + [whole] * 6 + [away] * 2,
        out_specs=(whole, whole),
        scratch_shapes=[
            [pltpu.VMEM(grid_shape, jnp.float32)] * coils,
            [pltpu.VMEM(grid_shape, jnp.float32)] * coils,
            [pltpu.VMEM((coils * TAPS * YROWS, 2 * samples), jnp.bfloat16)] * math.gcd(blocks, UNROLL),
            pltpu.VMEM((2 * blocks, 2 * grid_size, 2 * samples), jnp.bfloat16),
            pltpu.VMEM((2 * blocks, 8, samples), jnp.float32),
            pltpu.VMEM((2 * blocks, 8, samples), jnp.float32),
            [pltpu.VMEM((coils // 2, 2 * grid_size, 2 * grid_size), jnp.bfloat16)] * 2,
            pltpu.VMEM(coil_maps.shape, jnp.bfloat16),
            pltpu.VMEM(shape, jnp.float32),
            pltpu.VMEM((2, grid_size, grid_size), jnp.float32),
            pltpu.SemaphoreType.DMA((2,)),
        ],
        compiler_params=pltpu.CompilerParams(vmem_limit_bytes=VMEM_LIMIT),
        cost_estimate=pl.CostEstimate(
            flops=2 * 2 * blocks * TAPS * coils * YROWS * 4 * samples * grid_size,
            bytes_accessed=coil_maps.size * 2,
            transcendentals=0,
        ),
    )(corner, own, other, *tables, coil_maps, estimate)


def swap(values, axis, bit):
    count = lax.axis_size(axis)
    return lax.ppermute(values, axis, [(index, index ^ bit) for index in range(count)])


def gather_blocks(packed):
    count = lax.axis_size("tile")
    held = packed[None]
    bits = [1 << place for place in range(1, count.bit_length() - 1)]
    for bit in reversed(bits):
        held = jnp.concatenate([held, swap(held, "tile", bit)], axis=0)
    held = held.reshape((-1,) + packed.shape[1:])
    return held, swap(held, "tile", 1)


def on_device(
    kspace_samples, density, sample_frac, row_offsets, depth_base, block_base, coil_maps, estimate
):
    tile_count = lax.axis_size("tile")
    tile_here = lax.axis_index("tile")
    frame_count = lax.axis_size("frame")
    frame_here = lax.axis_index("frame")
    frames_local, blocks_local, channels, sample_count = kspace_samples.shape
    grid_size = coil_maps.shape[3]
    slab = coil_maps.shape[2]
    scale = 1.0 / (8.0 * math.sqrt(blocks_local * tile_count * sample_count))
    last = frames_local - 1

    corner_rows = jnp.broadcast_to(
        block_base.astype(jnp.bfloat16)[..., None], block_base.shape + (sample_count,)
    )
    packed = jnp.concatenate(
        [
            kspace_samples,
            density[:, :, None],
            sample_frac,
            row_offsets.astype(jnp.bfloat16)[:, :, None],
            depth_base.astype(jnp.bfloat16)[:, :, None],
            corner_rows,
        ],
        axis=2,
    )
    tables = row_tables(grid_size, tile_here * slab) + (
        depth_table(grid_size), plane_table(grid_size),
    )
    even = frame_here % 2 == 0
    order = [jnp.where(even, last, 0), jnp.where(even, 0, last)]

    halves, received = [], []
    for place, frame in enumerate(order):
        own, other = gather_blocks(lax.dynamic_index_in_dim(packed, frame, 0, keepdims=False))
        corner = jnp.concatenate([own[:, -2:, 0], other[:, -2:, 0]], axis=0)
        corner = jnp.concatenate([frame[None].astype(jnp.int32), corner.reshape(-1).astype(jnp.int32)])
        half, small = frame_image(corner, own, other, tables, coil_maps, estimate, scale)
        halves.append(half)
        if place == 0:
            pairs = [(index, index ^ 1) for index in range(frame_count) if index ^ 1 < frame_count]
        else:
            pairs = [(index, index - 1) for index in range(2, frame_count, 2)]
            pairs += [(target, source) for source, target in pairs]
        received.append(lax.ppermute(small, "frame", pairs) if pairs else jnp.zeros_like(small))

    first = jnp.where(even, halves[1], halves[0])
    second = jnp.where(even, halves[0], halves[1])
    before = jnp.where(even, received[1], received[0]).astype(jnp.float32)
    after = jnp.where(even, received[0], received[1]).astype(jnp.float32)

    def psi(low, high):
        change = high - low
        return change / jnp.sqrt(
            change[0] * change[0] + change[1] * change[1] + EPS * EPS
        )[None]

    middle = psi(first, second)
    low = jnp.where(frame_here > 0, psi(before, first), 0.0)
    high = jnp.where(frame_here < frame_count - 1, psi(second, after), 0.0)
    return jnp.stack(
        [first - LAMBDA_TV * (low - middle), second - LAMBDA_TV * (middle - high)], axis=0
    )


def solution(mesh):
    in_specs = (
        P("frame", "tile", None, None),
        P("frame", "tile", None),
        P("frame", "tile", None, None),
        P("frame", "tile", None),
        P("frame", "tile", None),
        P("frame", "tile", None),
        P(None, None, "tile", None, None),
        P("frame", None, "tile", None, None),
    )
    out_specs = P("frame", None, "tile", None, None)
    return jax.shard_map(
        on_device, mesh=mesh, in_specs=in_specs, out_specs=out_specs, check_vma=False
    )
```

time: 133 us -> 92.9 us (0.70)
  Pallas kernels: 96.4 us -> 55.9 us
    pallas_call x2, Pallas kernels: 96.4 us -> 55.9 us  [frame_image(): pl.pallas_call(functools.partial(frame_kernel, scale=scale), out_shape=(j...]
  transfers between devices with their start and end apart: 9 -> 9, of which waited for: 6 -> 6; matrix products, arithmetic and copies ran while one was open for 1% -> 2% of each run, Pallas kernels for 36% -> 30%
where the time goes in v2:
time: 92.9 us; the launch traced here: 92.5 us
  Pallas kernels  55.9 us (60%)
  starting transfers between devices  13.1 us (14%)
  waiting for transfers between devices  9.19 us (10%)
  other arithmetic  8.39 us (9%)
  local copies, waits for them, and re-layouts  5.69 us (6%)
    pallas_call x2, Pallas kernels, frame_image(): pl.pallas_call(functools.partial(frame_kernel, scale=scale), out_shape=(j...  55.9 us
    ppermute x8, starting transfers between devices, swap(): lax.ppermute(values, axis, [(index, index ^ bit) for index in range(count)])  11.3 us
    ppermute x8, waiting for transfers between devices, swap(): lax.ppermute(values, axis, [(index, index ^ bit) for index in range(count)])  9.19 us
    another operation x2, other arithmetic, on_device(): jnp.stack([first - LAMBDA_TV * (low - middle), second - LAMBDA_TV * (midd...  2.19 us
  transfers between devices with their start and end apart: 9, of which 6 were waited for; matrix products, arithmetic and copies ran while one was open for 2% of the time, Pallas kernels for 30%

profile of v2, /device:TPU:0, one launch (start us, length us, event | category | flops | bytes accessed | tf_op | source)
XLA Modules:
  0.0 92.5 jit_solution(5960102806849709104)
XLA Ops:
  0.0 0.7 convert_element_type.39
  0.8 0.7 convert_bitcast_fusion.1
  1.5 0.7 convert_bitcast_fusion
  2.2 0.7 copy.34
  2.9 0.7 copy.35
  3.7 0.9 concatenate.37
  4.6 4.1 %collective-permute-start.4 = (bf16[1,4,40,128]{3,2,1,0:T(8,128)(2,1)S(1)}, bf16[1,4,40,128]{3,2,1,0:T(8,128)(2,1)S(1)}, u32[]{:S(2)}, u32[]{:S(2)}) collective-permute-start(bf16[1,4,40,128]{3,2,1,0:T(8,128)(2,1)S(1)} %get-tuple-element.18), channel_id=1, source_target_pairs={{0,8},{1,9},{2,10},{3,11},{4,12},{5,13},{6,14},{7,15},{8,0},{9,1},... | collective-permute-start | bytes 122888 | tf_op jit(solution)/shard_map/ppermute | solution.py:287
  8.8 2.3 %collective-permute-done.4 = bf16[1,4,40,128]{3,2,1,0:T(8,128)(2,1)S(1)} collective-permute-done((bf16[1,4,40,128]{3,2,1,0:T(8,128)(2,1)S(1)}, bf16[1,4,40,128]{3,2,1,0:T(8,128)(2,1)S(1)}, u32[]{:S(2)}, u32[]{:S(2)}) %collective-permute-start.4) | collective-permute-done | bytes 40992 | tf_op jit(solution)/shard_map/ppermute | solution.py:287
  11.1 1.9 %collective-permute-start.5 = (bf16[2,4,40,128]{3,2,1,0:T(8,128)(2,1)S(1)}, bf16[2,4,40,128]{3,2,1,0:T(8,128)(2,1)S(1)}, u32[]{:S(2)}, u32[]{:S(2)}) collective-permute-start(bf16[2,4,40,128]{3,2,1,0:T(8,128)(2,1)S(1)} %pad_maximum_fusion.6), channel_id=1, source_target_pairs={{0,4},{1,5},{2,6},{3,7},{4,0},{5,1},{6,2},{7,3},{8,12},{9,13},{10,... | collective-permute-start | bytes 245768 | tf_op jit(solution)/shard_map/ppermute | solution.py:287
  13.1 0.7 collective-permute-done
  13.7 1.5 %collective-permute-start.1 = (bf16[2,4,40,128]{3,2,1,0:T(8,128)(2,1)S(1)}, bf16[2,4,40,128]{3,2,1,0:T(8,128)(2,1)S(1)}, u32[]{:S(2)}, u32[]{:S(2)}) collective-permute-start(bf16[2,4,40,128]{3,2,1,0:T(8,128)(2,1)S(1)} %pad_maximum_fusion.5), channel_id=1, source_target_pairs={{0,4},{1,5},{2,6},{3,7},{4,0},{5,1},{6,2},{7,3},{8,12},{9,13},{10,... | collective-permute-start | bytes 245768 | tf_op jit(solution)/shard_map/ppermute | solution.py:287
  15.2 1.1 %collective-permute-done.5 = bf16[2,4,40,128]{3,2,1,0:T(8,128)(2,1)S(1)} collective-permute-done((bf16[2,4,40,128]{3,2,1,0:T(8,128)(2,1)S(1)}, bf16[2,4,40,128]{3,2,1,0:T(8,128)(2,1)S(1)}, u32[]{:S(2)}, u32[]{:S(2)}) %collective-permute-start.5) | collective-permute-done | bytes 81952 | tf_op jit(solution)/shard_map/ppermute | solution.py:287
  16.3 2.0 %collective-permute-start.6 = (bf16[4,4,40,128]{3,2,1,0:T(8,128)(2,1)S(1)}, bf16[4,4,40,128]{3,2,1,0:T(8,128)(2,1)S(1)}, u32[]{:S(2)}, u32[]{:S(2)}) collective-permute-start(bf16[4,4,40,128]{3,2,1,0:T(8,128)(2,1)S(1)} %pad_maximum_fusion.4), channel_id=1, source_target_pairs={{0,2},{1,3},{2,0},{3,1},{4,6},{5,7},{6,4},{7,5},{8,10},{9,11},{10,... | collective-permute-start | bytes 491528 | tf_op jit(solution)/shard_map/ppermute | solution.py:287
  18.3 1.5 %collective-permute-start.2 = (bf16[4,4,40,128]{3,2,1,0:T(8,128)(2,1)S(1)}, bf16[4,4,40,128]{3,2,1,0:T(8,128)(2,1)S(1)}, u32[]{:S(2)}, u32[]{:S(2)}) collective-permute-start(bf16[4,4,40,128]{3,2,1,0:T(8,128)(2,1)S(1)} %pad_maximum_fusion.3), channel_id=1, source_target_pairs={{0,2},{1,3},{2,0},{3,1},{4,6},{5,7},{6,4},{7,5},{8,10},{9,11},{10,... | collective-permute-start | bytes 491528 | tf_op jit(solution)/shard_map/ppermute | solution.py:287
  19.9 2.9 %collective-permute-done.6 = bf16[4,4,40,128]{3,2,1,0:T(8,128)(2,1)S(1)} collective-permute-done((bf16[4,4,40,128]{3,2,1,0:T(8,128)(2,1)S(1)}, bf16[4,4,40,128]{3,2,1,0:T(8,128)(2,1)S(1)}, u32[]{:S(2)}, u32[]{:S(2)}) %collective-permute-start.6) | collective-permute-done | bytes 163872 | tf_op jit(solution)/shard_map/ppermute | solution.py:287
  22.9 1.6 %collective-permute-done.2 = bf16[4,4,40,128]{3,2,1,0:T(8,128)(2,1)S(1)} collective-permute-done((bf16[4,4,40,128]{3,2,1,0:T(8,128)(2,1)S(1)}, bf16[4,4,40,128]{3,2,1,0:T(8,128)(2,1)S(1)}, u32[]{:S(2)}, u32[]{:S(2)}) %collective-permute-start.2) | collective-permute-done | bytes 163872 | tf_op jit(solution)/shard_map/ppermute | solution.py:287
  27.4 1.0 %broadcast_in_dim.53.cos_rows = f32[136,8,128]{2,1,0:T(8,128)} broadcast(f32[136,8]{1,0:T(8,128)S(1)} %copy.41), dimensions={0,1} | broadcast | bytes 561408 | tf_op jit(solution)/shard_map/broadcast_in_dim | solution.py:63
  28.4 1.0 %broadcast_in_dim.54.sin_rows = f32[136,8,128]{2,1,0:T(8,128)} broadcast(f32[136,8]{1,0:T(8,128)S(1)} %copy.42), dimensions={0,1} | broadcast | bytes 561408 | tf_op jit(solution)/shard_map/broadcast_in_dim | solution.py:64
  29.4 27.8 %shard_map.101 = (f32[2,8,128,128]{3,2,1,0:T(8,128)}, bf16[2,8,128,128]{3,2,1,0:T(8,128)(2,1)}) custom-call(s32[129]{0:T(256)} %pad_add_fusion.1.corner, bf16[32,40,128]{2,1,0:T(8,128)(2,1)} %bitcast.28, bf16[32,40,128]{2,1,0:T(8,128)(2,1)} %copy-done.5, f32[136,8,128]{2,1,0:T(8,128)} %broadcast_in_dim.53.cos_rows, ...), custom_call_target="tpu_custom_call" | custom-call | flops 6442450944 | bytes 8388608 | tf_op jit(solution)/shard_map/pallas_call | solution.py:255
  57.3 1.8 %collective-permute-start.8 = (bf16[2,8,128,128]{3,2,1,0:T(8,128)(2,1)}, bf16[2,8,128,128]{3,2,1,0:T(8,128)(2,1)S(1)}, u32[]{:S(2)}, u32[]{:S(2)}) collective-permute-start(bf16[2,8,128,128]{3,2,1,0:T(8,128)(2,1)} %get-tuple-element.10), channel_id=1, source_target_pairs={{0,16},{16,0},{1,17},{17,1},{2,18},{18,2},{3,19},{19,3},{4,20},{20... | collective-permute-start | bytes 1572872 | tf_op jit(solution)/shard_map/ppermute | solution.py:345
  59.7 28.0 %shard_map.100 = (f32[2,8,128,128]{3,2,1,0:T(8,128)}, bf16[2,8,128,128]{3,2,1,0:T(8,128)(2,1)}) custom-call(s32[129]{0:T(256)} %pad_add_fusion.corner, bf16[32,40,128]{2,1,0:T(8,128)(2,1)} %bitcast.25, bf16[32,40,128]{2,1,0:T(8,128)(2,1)} %copy-done.4, f32[136,8,128]{2,1,0:T(8,128)} %broadcast_in_dim.53.cos_rows, f32[136,8,128]{2,1,0:T(8,128)} %broadcast_in_dim.54.sin_rows, ...), custom_call_target="tpu_custom_call" | custom-call | flops 6442450944 | bytes 8388608 | tf_op jit(solution)/shard_map/pallas_call | solution.py:255
  87.8 1.5 %convert_subtract_fusion.1 = (f32[2,8,128,128]{3,2,1,0:T(8,128)S(1)}, f32[2,8,128,128]{3,2,1,0:T(8,128)S(1)}) fusion(bf16[2,8,128,128]{3,2,1,0:T(8,128)(2,1)S(1)} %collective-permute-done.8, pred[]{:T(512)S(6)} %eq.7, f32[2,8,128,128]{3,2,1,0:T(8,128)} %get-tuple-element.8, f32[2,8,128,128]{3,2,1,0:T(8,128)S(1)} %copy-done), kind=kLoop, calls=%fused_computation.4 | loop fusion | flops 1048576 | bytes 4718593 | tf_op jit(solution)/shard_map/sub | solution.py:353
  90.3 0.7 subtract_bitcast_fusion.1
  91.0 1.5 %pad_maximum_fusion = f32[2,2,8,128,128]{4,3,2,1,0:T(8,128)} fusion(f32[1,2,8,128,128]{4,3,2,1,0:T(8,128)S(1)} %get-tuple-element.16, f32[1,2,8,128,128]{4,3,2,1,0:T(8,128)S(1)} %get-tuple-element.15), kind=kLoop, calls=%fused_computation | loop fusion | flops 524288 | bytes 4194304 | tf_op jit(solution)/shard_map/stack | solution.py:361
  (54 shorter events, 4.8 us)
Async XLA Ops:
  4.6 6.5 %collective-permute-start.4 = (bf16[1,4,40,128]{3,2,1,0:T(8,128)(2,1)S(1)}, bf16[1,4,40,128]{3,2,1,0:T(8,128)(2,1)S(1)}, u32[]{:S(2)}, u32[]{:S(2)}) collective-permute-start(bf16[1,4,40,128]{3,2,1,0:T(8,128)(2,1)S(1)} %get-tuple-element.18), channel_id=1, source_target_pairs={{0,8},{1,9},{2,10},{3,11},{4,12},{5,13},{6,14},{7,15},{8,0},{9,1},... | collective-permute-start | bytes 122888 | tf_op jit(solution)/shard_map/ppermute | solution.py:287
  8.7 5.0 %collective-permute-start = (bf16[1,4,40,128]{3,2,1,0:T(8,128)(2,1)S(1)}, bf16[1,4,40,128]{3,2,1,0:T(8,128)(2,1)S(1)}, u32[]{:S(2)}, u32[]{:S(2)}) collective-permute-start(bf16[1,4,40,128]{3,2,1,0:T(8,128)(2,1)S(1)} %get-tuple-element.17), channel_id=1, source_target_pairs={{0,8},{1,9},{2,10},{3,11},{4,12},{5,13},{6,14},{7,15},{8,0},{9,1},... | collective-permute-start | bytes 122888 | tf_op jit(solution)/shard_map/ppermute | solution.py:287
  11.1 5.2 %collective-permute-start.5 = (bf16[2,4,40,128]{3,2,1,0:T(8,128)(2,1)S(1)}, bf16[2,4,40,128]{3,2,1,0:T(8,128)(2,1)S(1)}, u32[]{:S(2)}, u32[]{:S(2)}) collective-permute-start(bf16[2,4,40,128]{3,2,1,0:T(8,128)(2,1)S(1)} %pad_maximum_fusion.6), channel_id=1, source_target_pairs={{0,4},{1,5},{2,6},{3,7},{4,0},{5,1},{6,2},{7,3},{8,12},{9,13},{10,... | collective-permute-start | bytes 245768 | tf_op jit(solution)/shard_map/ppermute | solution.py:287
  13.7 4.6 %collective-permute-start.1 = (bf16[2,4,40,128]{3,2,1,0:T(8,128)(2,1)S(1)}, bf16[2,4,40,128]{3,2,1,0:T(8,128)(2,1)S(1)}, u32[]{:S(2)}, u32[]{:S(2)}) collective-permute-start(bf16[2,4,40,128]{3,2,1,0:T(8,128)(2,1)S(1)} %pad_maximum_fusion.5), channel_id=1, source_target_pairs={{0,4},{1,5},{2,6},{3,7},{4,0},{5,1},{6,2},{7,3},{8,12},{9,13},{10,... | collective-permute-start | bytes 245768 | tf_op jit(solution)/shard_map/ppermute | solution.py:287
  16.3 6.4 %collective-permute-start.6 = (bf16[4,4,40,128]{3,2,1,0:T(8,128)(2,1)S(1)}, bf16[4,4,40,128]{3,2,1,0:T(8,128)(2,1)S(1)}, u32[]{:S(2)}, u32[]{:S(2)}) collective-permute-start(bf16[4,4,40,128]{3,2,1,0:T(8,128)(2,1)S(1)} %pad_maximum_fusion.4), channel_id=1, source_target_pairs={{0,2},{1,3},{2,0},{3,1},{4,6},{5,7},{6,4},{7,5},{8,10},{9,11},{10,... | collective-permute-start | bytes 491528 | tf_op jit(solution)/shard_map/ppermute | solution.py:287
  18.3 6.2 %collective-permute-start.2 = (bf16[4,4,40,128]{3,2,1,0:T(8,128)(2,1)S(1)}, bf16[4,4,40,128]{3,2,1,0:T(8,128)(2,1)S(1)}, u32[]{:S(2)}, u32[]{:S(2)}) collective-permute-start(bf16[4,4,40,128]{3,2,1,0:T(8,128)(2,1)S(1)} %pad_maximum_fusion.3), channel_id=1, source_target_pairs={{0,2},{1,3},{2,0},{3,1},{4,6},{5,7},{6,4},{7,5},{8,10},{9,11},{10,... | collective-permute-start | bytes 491528 | tf_op jit(solution)/shard_map/ppermute | solution.py:287
  22.8 6.6 %copy-start.3 = (bf16[8,4,40,128]{3,2,1,0:T(8,128)(2,1)}, bf16[8,4,40,128]{3,2,1,0:T(8,128)(2,1)S(1)}, u32[]{:S(2)}) copy-start(bf16[8,4,40,128]{3,2,1,0:T(8,128)(2,1)S(1)} %pad_maximum_fusion.2) | copy-start | bytes 983044
  22.8 2.4 %collective-permute-start.7 = (bf16[32,40,128]{2,1,0:T(8,128)(2,1)S(1)}, bf16[32,40,128]{2,1,0:T(8,128)(2,1)S(1)}, u32[]{:S(2)}, u32[]{:S(2)}) collective-permute-start(bf16[32,40,128]{2,1,0:T(8,128)(2,1)S(1)} %bitcast.26), channel_id=1, source_target_pairs={{0,1},{1,0},{2,3},{3,2},{4,5},{5,4},{6,7},{7,6},{8,9},{9,8},{10,11... | collective-permute-start | bytes 983048 | tf_op jit(solution)/shard_map/ppermute | solution.py:287
  24.6 32.7 %copy-start.2 = (bf16[8,4,40,128]{3,2,1,0:T(8,128)(2,1)}, bf16[8,4,40,128]{3,2,1,0:T(8,128)(2,1)S(1)}, u32[]{:S(2)}) copy-start(bf16[8,4,40,128]{3,2,1,0:T(8,128)(2,1)S(1)} %pad_maximum_fusion.1) | copy-start | bytes 983044
  24.6 1.7 %collective-permute-start.3 = (bf16[32,40,128]{2,1,0:T(8,128)(2,1)S(1)}, bf16[32,40,128]{2,1,0:T(8,128)(2,1)S(1)}, u32[]{:S(2)}, u32[]{:S(2)}) collective-permute-start(bf16[32,40,128]{2,1,0:T(8,128)(2,1)S(1)} %bitcast.23), channel_id=1, source_target_pairs={{0,1},{1,0},{2,3},{3,2},{4,5},{5,4},{6,7},{7,6},{8,9},{9,8},{10,11... | collective-permute-start | bytes 983048 | tf_op jit(solution)/shard_map/ppermute | solution.py:287
  25.2 4.1 %copy-start.5 = (bf16[32,40,128]{2,1,0:T(8,128)(2,1)}, bf16[32,40,128]{2,1,0:T(8,128)(2,1)S(1)}, u32[]{:S(2)}) copy-start(bf16[32,40,128]{2,1,0:T(8,128)(2,1)S(1)} %collective-permute-done.7.other) | copy-start | bytes 983044
  26.3 31.0 %copy-start.4 = (bf16[32,40,128]{2,1,0:T(8,128)(2,1)}, bf16[32,40,128]{2,1,0:T(8,128)(2,1)S(1)}, u32[]{:S(2)}) copy-start(bf16[32,40,128]{2,1,0:T(8,128)(2,1)S(1)} %collective-permute-done.3.other) | copy-start | bytes 983044
  57.3 30.5 %collective-permute-start.8 = (bf16[2,8,128,128]{3,2,1,0:T(8,128)(2,1)}, bf16[2,8,128,128]{3,2,1,0:T(8,128)(2,1)S(1)}, u32[]{:S(2)}, u32[]{:S(2)}) collective-permute-start(bf16[2,8,128,128]{3,2,1,0:T(8,128)(2,1)} %get-tuple-element.10), channel_id=1, source_target_pairs={{0,16},{16,0},{1,17},{17,1},{2,18},{18,2},{3,19},{19,3},{4,20},{20... | collective-permute-start | bytes 1572872 | tf_op jit(solution)/shard_map/ppermute | solution.py:345
  59.7 28.1 %copy-start = (f32[2,8,128,128]{3,2,1,0:T(8,128)S(1)}, f32[2,8,128,128]{3,2,1,0:T(8,128)}, u32[]{:S(2)}) copy-start(f32[2,8,128,128]{3,2,1,0:T(8,128)} %get-tuple-element.9) | copy-start | bytes 3145732
  87.8 1.7 %copy-start.1 = (f32[2,8,128,128]{3,2,1,0:T(8,128)S(1)}, f32[2,8,128,128]{3,2,1,0:T(8,128)}, u32[]{:S(2)}) copy-start(f32[2,8,128,128]{3,2,1,0:T(8,128)} %get-tuple-element.8) | copy-start | bytes 3145732

commit v3 on v2

v3 whole, which is shorter than its diff:
```python
import functools
import math

import jax
import jax.numpy as jnp
import numpy as np
from jax import lax
from jax.experimental import pallas as pl
from jax.experimental.pallas import tpu as pltpu
from jax.sharding import PartitionSpec as P

TAPS = 6
WIN = 8
YROWS = 8
META = 8
BETA = 13.9
EPS = 0.05
LAMBDA_TV = 0.3
TERMS = 40
UNROLL = 8
GROUPS = 8
LAST_REFS = 15
VMEM_LIMIT = 56 * 1024 * 1024


def kaiser_coefficients():
    quarter = BETA * BETA / 4.0
    terms = [quarter**power / math.factorial(power) ** 2 for power in range(TERMS)]
    total = math.fsum(terms)
    return [term / total for term in terms]


def kaiser(distance):
    coefficients = kaiser_coefficients()
    inside = jnp.maximum(1.0 - distance / 3.0 * (distance / 3.0), 0.0)
    value = jnp.full_like(inside, coefficients[-1])
    for coefficient in coefficients[-2::-1]:
        value = value * inside + coefficient
    return value


def dft_angles(grid_size):
    positions = np.arange(grid_size)
    return (positions[:, None] * positions[None, :] % grid_size) * (2.0 * math.pi / grid_size)


def depth_table(grid_size):
    angles = dft_angles(grid_size)
    return jnp.asarray(np.concatenate([np.cos(angles), np.sin(angles)], axis=0), jnp.bfloat16)


def plane_table(grid_size):
    angles = dft_angles(grid_size)
    cosine, sine = np.cos(angles), np.sin(angles)
    parts = np.stack([np.concatenate([cosine, -sine], 1), np.concatenate([sine, cosine], 1)])
    tiles = parts.reshape(2, grid_size // 8, 8, 2 * grid_size).swapaxes(0, 1)
    return jnp.asarray(tiles.reshape(2 * grid_size, 2 * grid_size), jnp.bfloat16)


def row_table(grid_size, tile_count):
    slab = grid_size // tile_count
    lanes = -(-(grid_size + WIN) // 128) * 128
    rows = np.arange(tile_count)[:, None, None] * slab + np.arange(YROWS)[:, None]
    angles = (rows * np.arange(lanes) % grid_size) * (2.0 * math.pi / grid_size)
    return jnp.asarray(np.stack([np.cos(angles), np.sin(angles)], axis=1), jnp.float32)


def shared_first():
    return lax.rem(lax.axis_index("frame"), 2) == 0


def pack_kernel(samples, density, fractions, shift, depth, corner, *packed):
    frames, blocks, _, count = samples.shape
    last = frames - 1
    for place, out in enumerate(packed):
        frame = jnp.where(shared_first(), last - place, place)
        rows = [
            density[frame].astype(jnp.float32)[:, None],
            fractions[frame].astype(jnp.float32),
            shift[frame].astype(jnp.float32)[:, None],
            depth[frame].astype(jnp.float32)[:, None],
        ]
        for block in range(blocks):
            ends = [
                jnp.full((1, count), corner[frame, block, axis], jnp.int32).astype(jnp.float32)
                for axis in range(2)
            ]
            parts = [samples[frame, block].astype(jnp.float32)] + [row[block] for row in rows] + ends
            out[block] = jnp.concatenate(parts, axis=0).astype(jnp.bfloat16)


def pack_blocks(samples, density, fractions, shift, depth, corner):
    frames, blocks, channels, count = samples.shape
    whole = pl.BlockSpec(memory_space=pltpu.VMEM)
    shape = jax.ShapeDtypeStruct((blocks, channels + META, count), jnp.bfloat16)
    return pl.pallas_call(
        pack_kernel,
        out_shape=(shape,) * frames,
        in_specs=[whole] * 5 + [pl.BlockSpec(memory_space=pltpu.SMEM)],
        out_specs=(whole,) * frames,
    )(samples, density, fractions, shift, depth, corner)


def frame_kernel(
    own, other, depth_dft, plane_dft, rows_hbm, maps_hbm, estimate_hbm, half, *rest, place, scale,
):
    half_small = rest[0] if len(rest) == LAST_REFS + 1 else None
    frame_body(
        own, other, depth_dft, plane_dft, rows_hbm, maps_hbm, estimate_hbm, half, half_small,
        *rest[-LAST_REFS:], place=place, scale=scale,
    )


def frame_body(
    own, other, depth_dft, plane_dft, rows_hbm, maps_hbm, estimate_hbm, half, half_small,
    cos_rows, sin_rows, corner_rows, corner, row_phases,
    grid_real, grid_imag, left, weights, weight_x, weight_y, maps, estimate, total, sems,
    *, place, scale,
):
    blocks = own.shape[0]
    samples = own.shape[2]
    unroll = len(left)
    coils, _, slab, grid_size, _ = maps.shape
    frame = jnp.where(shared_first(), estimate_hbm.shape[0] - 1 - place, place)
    copies = [
        pltpu.make_async_copy(maps_hbm, maps, sems.at[0]),
        pltpu.make_async_copy(estimate_hbm.at[frame], estimate, sems.at[1]),
    ]
    phases = pltpu.make_async_copy(rows_hbm.at[lax.axis_index("tile")], row_phases, sems.at[2])
    phases.start()
    for copy in copies:
        copy.start()
    for source, offset in ((own, 0), (other, blocks)):
        for block in range(blocks):
            ends = source[block].astype(jnp.float32)[2 * coils + META - 2 :]
            corner_rows[pl.ds(offset + block, 1), :] = (ends[:1] + grid_size * ends[1:]).astype(jnp.int32)
    corners = pltpu.make_async_copy(corner_rows, corner, sems.at[3])
    corners.start()
    phases.wait()
    for position in range(grid_size + WIN):
        at = slice(position, position + 1)
        cos_rows[position] = jnp.broadcast_to(row_phases[0, :, at], (YROWS, samples))
        sin_rows[position] = jnp.broadcast_to(row_phases[1, :, at], (YROWS, samples))

    table = depth_dft[...]
    taps = lax.broadcasted_iota(jnp.int32, (8, 2 * samples), 0).astype(jnp.float32)
    cells = lax.broadcasted_iota(jnp.int32, (grid_size, 2 * samples), 0).astype(jnp.bfloat16)
    clear_rows = grid_real[0].shape[1] // (blocks // unroll)

    def prepare(source, offset, cleared):
        def two(first):
            meta = jnp.concatenate(
                [source[first + part].astype(jnp.float32)[2 * coils :] for part in range(2)], axis=1
            )
            density, frac_x, frac_y, frac_z, shift, depth = (meta[row : row + 1] for row in range(6))
            tap_x = kaiser(taps - 2.0 - frac_x) * density
            lag = taps - shift
            tap_y = jnp.where((lag >= 0.0) & (lag < float(TAPS)), kaiser(lag - 2.0 - frac_y), 0.0)
            tap_z = kaiser(taps - 2.0 - frac_z).astype(jnp.bfloat16)
            cell = depth + taps
            cell = jnp.where(cell >= float(grid_size), cell - float(grid_size), cell)
            cell = cell.astype(jnp.bfloat16)
            spread = jnp.zeros((grid_size, 2 * samples), jnp.bfloat16)
            for tap in range(TAPS):
                spread = jnp.where(cells == cell[tap : tap + 1], tap_z[tap : tap + 1], spread)
            turned = jnp.dot(table, spread, preferred_element_type=jnp.float32).astype(jnp.bfloat16)
            real, imag = turned[:grid_size], turned[grid_size:]
            for part in range(2):
                at, here = offset + first + part, slice(part * samples, (part + 1) * samples)
                weight_x[at] = tap_x[:, here]
                weight_y[at] = tap_y[:, here]
                weights[at, :, :samples] = turned[:, here]
                weights[at, :grid_size, samples:] = -imag[:, here]
                weights[at, grid_size:, samples:] = real[:, here]

        def step(index, carry):
            for ref in cleared:
                at = pl.ds(pl.multiple_of(index * clear_rows, 8), clear_rows)
                ref[:, at, :] = jnp.zeros((ref.shape[0], clear_rows, grid_size), jnp.float32)
            for part in range(0, unroll, 2):
                two(index * unroll + part)
            return carry

        lax.fori_loop(0, blocks // unroll, step, 0)

    prepare(own, 0, grid_real)
    prepare(other, blocks, grid_imag)

    def build(source, offset, block, slot):
        first_row = corner[offset + block, 0] // grid_size
        payload = source[block].astype(jnp.float32)
        row_weights = weight_y[offset + block]
        plane_weights = weight_x[offset + block]
        turn_real = jnp.zeros((YROWS, samples), jnp.float32)
        turn_imag = jnp.zeros((YROWS, samples), jnp.float32)
        for row in range(WIN):
            weight = row_weights[row : row + 1]
            turn_real = turn_real + cos_rows[first_row + row] * weight
            turn_imag = turn_imag + sin_rows[first_row + row] * weight
        by_plane = []
        for tap in range(0, TAPS, 2):
            by_plane.append(jnp.concatenate(
                [jnp.broadcast_to(plane_weights[at : at + 1], (YROWS, samples)) for at in (tap, tap + 1)],
                axis=0,
            ).astype(jnp.bfloat16))
        for coil in range(coils):
            amp_real = payload[2 * coil : 2 * coil + 1]
            amp_imag = payload[2 * coil + 1 : 2 * coil + 2]
            parts = (
                amp_real * turn_real - amp_imag * turn_imag,
                amp_real * turn_imag + amp_imag * turn_real,
            )
            for part, value in enumerate(parts):
                twice = jnp.concatenate([value, value], axis=0).astype(jnp.bfloat16)
                for pair, weight in enumerate(by_plane):
                    left[slot][
                        pl.ds(coil * TAPS * YROWS + pair * 2 * YROWS, 2 * YROWS),
                        pl.ds(part * samples, samples),
                    ] = twice * weight

    def spread(offset, block, slot):
        first_plane = lax.rem(corner[offset + block, 0], grid_size)
        product = lax.dot_general(
            left[slot][...], weights[offset + block], (((1,), (1,)), ((), ())),
            preferred_element_type=jnp.float32,
        )
        rows = TAPS * YROWS
        per = grid_real[0].shape[0]
        for coil in range(coils):
            at = pl.ds(pl.multiple_of(first_plane * YROWS, YROWS), rows)
            part = product[coil * rows : (coil + 1) * rows]
            real, imag = grid_real[coil // per], grid_imag[coil // per]
            real[coil % per, at, :] = real[coil % per, at, :] + part[:, :grid_size]
            imag[coil % per, at, :] = imag[coil % per, at, :] + part[:, grid_size:]

    def spread_planes(source, offset):
        build(source, offset, 0, 0)

        def step(index, carry):
            block = index * unroll
            for part in range(unroll):
                later = jnp.minimum(block + part + 1, blocks - 1)
                build(source, offset, later, (part + 1) % unroll)
                spread(offset, block + part, part)
            return carry

        lax.fori_loop(0, blocks // unroll, step, 0)

    corners.wait()
    spread_planes(own, 0)
    spread_planes(other, blocks)

    wrap = (TAPS - 1) * YROWS
    top = grid_size * YROWS
    for ref in grid_real + grid_imag:
        ref[:, :wrap, :] = ref[:, :wrap, :] + ref[:, top : top + wrap, :]

    for copy in copies:
        copy.wait()

    columns = weights
    groups = len(grid_real)

    def coil_sums(index, carry):
        for place in range(groups):
            lanes = slice((place % 2) * grid_size, (place % 2 + 1) * grid_size)
            first = (place // 2) * YROWS
            for part, refs in enumerate((grid_real, grid_imag)):
                for start in range(0, grid_size, 16):
                    planes = refs[place][index, start * YROWS : (start + 16) * YROWS, :]
                    rows = jnp.swapaxes(planes.reshape(16, YROWS, grid_size), 0, 1)
                    at = slice(part * grid_size + start, part * grid_size + start + 16)
                    columns[first : first + YROWS, at, lanes] = rows.astype(jnp.bfloat16)
        for row in range(slab):
            images = [
                jnp.dot(
                    plane_dft[...], columns[pair * YROWS + row], preferred_element_type=jnp.float32
                )
                for pair in range(groups // 2)
            ]
            for tile in range(grid_size // 16):
                at = pl.ds(tile * 16, 16)
                sum_real, sum_imag = total[0, row, at], total[1, row, at]
                for place in range(groups):
                    coil = place * (coils // groups) + index
                    column = (place % 2) * grid_size
                    image = images[place // 2][tile * 32 : tile * 32 + 32, column : column + grid_size]
                    image_real = jnp.concatenate([image[:8], image[16:24]], axis=0)
                    image_imag = jnp.concatenate([image[8:16], image[24:]], axis=0)
                    map_real = maps[coil, 0, row, at].astype(jnp.float32)
                    map_imag = maps[coil, 1, row, at].astype(jnp.float32)
                    sum_real = sum_real + (map_real * image_real + map_imag * image_imag)
                    sum_imag = sum_imag + (map_real * image_imag - map_imag * image_real)
                total[0, row, at] = sum_real
                total[1, row, at] = sum_imag
        return carry

    total[...] = jnp.zeros_like(total)
    lax.fori_loop(0, coils // groups, coil_sums, 0)
    for part in range(2):
        for row in range(slab):
            value = estimate[part, row] + scale * total[part, row]
            half[part, row] = value
            if half_small is not None:
                half_small[part, row] = value.astype(jnp.bfloat16)


def frame_image(own, other, tables, coil_maps, estimate, scale, place, shared):
    blocks, _, samples = own.shape
    coils, _, slab, grid_size, _ = coil_maps.shape
    shape = (2, slab, grid_size, grid_size)
    whole = pl.BlockSpec(memory_space=pltpu.VMEM)
    away = pl.BlockSpec(memory_space=pl.ANY)
    unroll = math.gcd(blocks, UNROLL)
    grid_shape = (coils // GROUPS, (grid_size + WIN) * YROWS, grid_size)
    outs = (jnp.float32, jnp.bfloat16)[: 2 if shared else 1]
    return pl.pallas_call(
        functools.partial(frame_kernel, place=place, scale=scale),
        out_shape=tuple(jax.ShapeDtypeStruct(shape, kind) for kind in outs),
        in_specs=[whole] * 4 + [away] * 3,
        out_specs=(whole,) * len(outs),
        scratch_shapes=[
            pltpu.VMEM((grid_size + WIN, YROWS, samples), jnp.float32),
            pltpu.VMEM((grid_size + WIN, YROWS, samples), jnp.float32),
            pltpu.VMEM((2 * blocks, samples), jnp.int32),
            pltpu.SMEM((2 * blocks, samples), jnp.int32),
            pltpu.VMEM(tables[2].shape[1:], jnp.float32),
            [pltpu.VMEM(grid_shape, jnp.float32)] * GROUPS,
            [pltpu.VMEM(grid_shape, jnp.float32)] * GROUPS,
            [pltpu.VMEM((coils * TAPS * YROWS, 2 * samples), jnp.bfloat16)] * unroll,
            pltpu.VMEM((2 * blocks, 2 * grid_size, 2 * samples), jnp.bfloat16),
            pltpu.VMEM((2 * blocks, 8, samples), jnp.float32),
            pltpu.VMEM((2 * blocks, 8, samples), jnp.float32),
            pltpu.VMEM(coil_maps.shape, jnp.bfloat16),
            pltpu.VMEM(shape, jnp.float32),
            pltpu.VMEM(shape, jnp.float32),
            pltpu.SemaphoreType.DMA((4,)),
        ],
        compiler_params=pltpu.CompilerParams(vmem_limit_bytes=VMEM_LIMIT),
        cost_estimate=pl.CostEstimate(
            flops=2 * 2 * blocks * TAPS * coils * YROWS * 4 * samples * grid_size,
            bytes_accessed=coil_maps.size * 2,
            transcendentals=0,
        ),
    )(own, other, *tables, coil_maps, estimate)


def step_kernel(first, second, beside_first, beside_second, out):
    index, count = lax.axis_index("frame"), lax.axis_size("frame")
    even = shared_first()

    def slope(low, high):
        change = high - low
        return change * lax.rsqrt(change[0] * change[0] + change[1] * change[1] + EPS * EPS)[None]

    values = first[...], second[...]
    pull = slope(values[0], values[1])
    has = (
        jnp.where(even, index + 1 < count, True),
        jnp.where(even, index > 0, index + 1 < count),
    )
    place = jnp.where(even, 1, 0)
    for value, inner, beside, there, at in (
        (values[0], pull, beside_first, has[0], place),
        (values[1], -pull, beside_second, has[1], 1 - place),
    ):
        if beside is not None:
            outer = slope(value, beside[...].astype(jnp.float32))
            inner = inner + jnp.where(there, outer, 0.0)
        out[at] = value + LAMBDA_TV * inner


def tv_step(halves, received):
    parts, slab, grid_size, _ = halves[0].shape
    block = pl.BlockSpec((parts, 1, grid_size, grid_size), lambda row: (0, row, 0, 0))
    given = [value for value in received if value is not None]

    def kernel(first, second, *rest):
        step_kernel(first, second, rest[0], rest[1] if len(given) > 1 else None, rest[-1])

    return pl.pallas_call(
        kernel,
        grid=(slab,),
        out_shape=jax.ShapeDtypeStruct((2,) + halves[0].shape, jnp.float32),
        in_specs=[block] * (2 + len(given)),
        out_specs=pl.BlockSpec((2, parts, 1, grid_size, grid_size), lambda row: (0, 0, row, 0, 0)),
    )(*halves, *given)


def swap(values, axis, bit):
    count = lax.axis_size(axis)
    return lax.ppermute(values, axis, [(index, index ^ bit) for index in range(count)])


def gather_blocks(packed):
    count = lax.axis_size("tile")
    held = packed[None]
    bits = [1 << place for place in range(1, count.bit_length() - 1)]
    for bit in reversed(bits):
        held = jnp.concatenate([held, swap(held, "tile", bit)], axis=0)
    held = held.reshape((-1,) + packed.shape[1:])
    return held, swap(held, "tile", 1)


def on_device(
    kspace_samples, density, sample_frac, row_offsets, depth_base, block_base, coil_maps, estimate
):
    tile_count = lax.axis_size("tile")
    frame_count = lax.axis_size("frame")
    frames_local, blocks_local, channels, sample_count = kspace_samples.shape
    grid_size = coil_maps.shape[3]
    scale = 1.0 / (8.0 * math.sqrt(blocks_local * tile_count * sample_count))

    packed = pack_blocks(
        kspace_samples, density, sample_frac, row_offsets, depth_base, block_base
    )
    tables = depth_table(grid_size), plane_table(grid_size), row_table(grid_size, tile_count)
    pairs = [
        [(index, index ^ 1) for index in range(frame_count) if index ^ 1 < frame_count],
        [(index, index - 1) for index in range(2, frame_count, 2)],
    ]
    pairs[1] += [(target, source) for source, target in pairs[1]]
    halves, received = [], []
    for place in range(2):
        own, other = gather_blocks(packed[place])
        half, *small = frame_image(
            own, other, tables, coil_maps, estimate, scale, place, bool(pairs[place])
        )
        halves.append(half)
        received.append(lax.ppermute(small[0], "frame", pairs[place]) if small else None)
    return tv_step(halves, received)


def solution(mesh):
    in_specs = (
        P("frame", "tile", None, None),
        P("frame", "tile", None),
        P("frame", "tile", None, None),
        P("frame", "tile", None),
        P("frame", "tile", None),
        P("frame", "tile", None),
        P(None, None, "tile", None, None),
        P("frame", None, "tile", None, None),
    )
    out_specs = P("frame", None, "tile", None, None)
    return jax.shard_map(
        on_device, mesh=mesh, in_specs=in_specs, out_specs=out_specs, check_vma=False
    )
```

time: 92.9 us -> 104 us (1.12)
  Pallas kernels: 55.9 us -> 64.5 us
  waiting for transfers between devices: 9.19 us -> 15.9 us
  other arithmetic: 8.39 us -> 4.79 us
    pallas_call x2 -> x4, Pallas kernels: 55.9 us -> 64.5 us  [the longest x2 57 us: frame_image(): pl.pallas_call(functools.partial(frame_kernel, place=place, scale=scale),...]
    ppermute x8, waiting for transfers between devices: 9.19 us -> 15.9 us  [swap(): lax.ppermute(values, axis, [(index, index ^ bit) for index in range(count)])]
    concatenate x6, other arithmetic: 0.12 us -> 4.79 us  [gather_blocks(): held = jnp.concatenate([held, swap(held, 'tile', bit)], axis=0)]
    unnamed x13 -> x12, local copies, waits for them, and re-layouts: 0.72 us -> 4.9 us
    broadcast_in_dim x6 -> x0, local copies, waits for them, and re-layouts: 2.8 us -> none  [the longest x1 1.01 us: row_tables(): jnp.broadcast_to(jnp.sin(angles)[:, :, None], shape)]
    another operation x2 -> x0, other arithmetic: 2.19 us -> none  [on_device(): jnp.stack([first - LAMBDA_TV * (low - middle), second - LAMBDA_TV * (midd...]
    sub x3 -> x0, other arithmetic: 1.85 us -> none  [psi(): change = high - low]
    broadcast_in_dim x2 -> x0, other arithmetic: 1.38 us -> none  [the longest x1 0.69 us: on_device(): row_offsets.astype(jnp.bfloat16)[:, :, None]]
  transfers between devices with their start and end apart: 9 -> 9, of which waited for: 6 -> 5; matrix products, arithmetic and copies ran while one was open for 2% -> 3% of each run, Pallas kernels for 30% -> 55%
where the time goes in v3:
time: 104 us; the launch traced here: 103 us
  Pallas kernels  64.5 us (62%)
  waiting for transfers between devices  15.9 us (15%)
  starting transfers between devices  12.9 us (12%)
  local copies, waits for them, and re-layouts  4.9 us (5%)
  other arithmetic  4.79 us (5%)
    pallas_call x2, Pallas kernels, frame_image(): pl.pallas_call(functools.partial(frame_kernel, place=place, scale=scale),...  57 us
    ppermute x8, waiting for transfers between devices, swap(): lax.ppermute(values, axis, [(index, index ^ bit) for index in range(count)])  15.9 us
    ppermute x8, starting transfers between devices, swap(): lax.ppermute(values, axis, [(index, index ^ bit) for index in range(count)])  11.4 us
    pallas_call x1, Pallas kernels, tv_step(): pl.pallas_call(kernel, grid=(slab,), out_shape=jax.ShapeDtypeStruct((2,)...  6 us
    unnamed x12, local copies, waits for them, and re-layouts  4.9 us
    concatenate x6, other arithmetic, gather_blocks(): held = jnp.concatenate([held, swap(held, 'tile', bit)], axis=0)  4.79 us
  transfers between devices with their start and end apart: 9, of which 5 were waited for; matrix products, arithmetic and copies ran while one was open for 3% of the time, Pallas kernels for 55%

profile of v3, /device:TPU:0, one launch (start us, length us, event | category | flops | bytes accessed | tf_op | source)
XLA Modules:
  0.0 103.2 jit_solution(3936136796599563060)
XLA Ops:
  0.0 1.4 %copy.13.corner = s32[2,4,2]{2,1,0:T(4,128)} copy(s32[2,4,2]{1,2,0:T(2,128)} %param.16) | data formatting | bytes 128 | tf_op args[5]
  1.4 1.3 %copy.12.fractions = bf16[2,4,3,128]{3,2,1,0:T(4,128)(2,1)} copy(bf16[2,4,3,128]{3,1,2,0:T(4,128)(2,1)} %param.13) | data formatting | bytes 12288 | tf_op args[2]
  2.6 1.6 %shard_map.109 = (bf16[4,40,128]{2,1,0:T(8,128)(2,1)}, bf16[4,40,128]{2,1,0:T(8,128)(2,1)}) custom-call(bf16[2,4,32,128]{3,2,1,0:T(8,128)(2,1)} %samples.1, bf16[2,4,128]{2,1,0:T(4,128)(2,1)} %density.1, bf16[2,4,3,128]{3,2,1,0:T(4,128)(2,1)} %copy.12.fractions, s32[2,4,128]{2,1,0:T(4,128)} %shift.1, s32[2,4,128]{2,1,0:T(4,128)} %depth.1, ...), custom_call_target="tpu_custom_call" | custom-call | tf_op jit(solution)/shard_map/pallas_call | solution.py:96
  4.2 4.0 %collective-permute-start = (bf16[1,4,40,128]{3,2,1,0:T(8,128)(2,1)}, bf16[1,4,40,128]{3,2,1,0:T(8,128)(2,1)S(1)}, u32[]{:S(2)}, u32[]{:S(2)}) collective-permute-start(bf16[1,4,40,128]{3,2,1,0:T(8,128)(2,1)} %bitcast.8), channel_id=1, source_target_pairs={{0,8},{1,9},{2,10},{3,11},{4,12},{5,13},{6,14},{7,15},{8,0},{9,1},... | collective-permute-start | bytes 122888 | tf_op jit(solution)/shard_map/ppermute | solution.py:392
  8.2 2.6 %collective-permute-done = bf16[1,4,40,128]{3,2,1,0:T(8,128)(2,1)S(1)} collective-permute-done((bf16[1,4,40,128]{3,2,1,0:T(8,128)(2,1)}, bf16[1,4,40,128]{3,2,1,0:T(8,128)(2,1)S(1)}, u32[]{:S(2)}, u32[]{:S(2)}) %collective-permute-start) | collective-permute-done | bytes 40992 | tf_op jit(solution)/shard_map/ppermute | solution.py:392
  10.9 0.8 pad_maximum_fusion.4
  11.7 1.5 %collective-permute-start.1 = (bf16[2,4,40,128]{3,2,1,0:T(8,128)(2,1)S(1)}, bf16[2,4,40,128]{3,2,1,0:T(8,128)(2,1)S(1)}, u32[]{:S(2)}, u32[]{:S(2)}) collective-permute-start(bf16[2,4,40,128]{3,2,1,0:T(8,128)(2,1)S(1)} %pad_maximum_fusion.4), channel_id=1, source_target_pairs={{0,4},{1,5},{2,6},{3,7},{4,0},{5,1},{6,2},{7,3},{8,12},{9,13},{10,... | collective-permute-start | bytes 245768 | tf_op jit(solution)/shard_map/ppermute | solution.py:392
  13.2 3.0 %collective-permute-done.1 = bf16[2,4,40,128]{3,2,1,0:T(8,128)(2,1)S(1)} collective-permute-done((bf16[2,4,40,128]{3,2,1,0:T(8,128)(2,1)S(1)}, bf16[2,4,40,128]{3,2,1,0:T(8,128)(2,1)S(1)}, u32[]{:S(2)}, u32[]{:S(2)}) %collective-permute-start.1) | collective-permute-done | bytes 81952 | tf_op jit(solution)/shard_map/ppermute | solution.py:392
  16.2 0.8 pad_maximum_fusion.2
  17.0 1.8 %collective-permute-start.2 = (bf16[4,4,40,128]{3,2,1,0:T(8,128)(2,1)S(1)}, bf16[4,4,40,128]{3,2,1,0:T(8,128)(2,1)S(1)}, u32[]{:S(2)}, u32[]{:S(2)}) collective-permute-start(bf16[4,4,40,128]{3,2,1,0:T(8,128)(2,1)S(1)} %pad_maximum_fusion.2), channel_id=1, source_target_pairs={{0,2},{1,3},{2,0},{3,1},{4,6},{5,7},{6,4},{7,5},{8,10},{9,11},{10,... | collective-permute-start | bytes 491528 | tf_op jit(solution)/shard_map/ppermute | solution.py:392
  18.7 2.3 %collective-permute-start.4 = (bf16[1,4,40,128]{3,2,1,0:T(8,128)(2,1)}, bf16[1,4,40,128]{3,2,1,0:T(8,128)(2,1)S(1)}, u32[]{:S(2)}, u32[]{:S(2)}) collective-permute-start(bf16[1,4,40,128]{3,2,1,0:T(8,128)(2,1)} %bitcast.4), channel_id=1, source_target_pairs={{0,8},{1,9},{2,10},{3,11},{4,12},{5,13},{6,14},{7,15},{8,0},{9,1},... | collective-permute-start | bytes 122888 | tf_op jit(solution)/shard_map/ppermute | solution.py:392
  21.1 2.9 %collective-permute-done.4 = bf16[1,4,40,128]{3,2,1,0:T(8,128)(2,1)S(1)} collective-permute-done((bf16[1,4,40,128]{3,2,1,0:T(8,128)(2,1)}, bf16[1,4,40,128]{3,2,1,0:T(8,128)(2,1)S(1)}, u32[]{:S(2)}, u32[]{:S(2)}) %collective-permute-start.4) | collective-permute-done | bytes 40992 | tf_op jit(solution)/shard_map/ppermute | solution.py:392
  24.0 0.8 pad_maximum_fusion.5
  24.8 1.2 %collective-permute-start.5 = (bf16[2,4,40,128]{3,2,1,0:T(8,128)(2,1)S(1)}, bf16[2,4,40,128]{3,2,1,0:T(8,128)(2,1)S(1)}, u32[]{:S(2)}, u32[]{:S(2)}) collective-permute-start(bf16[2,4,40,128]{3,2,1,0:T(8,128)(2,1)S(1)} %pad_maximum_fusion.5), channel_id=1, source_target_pairs={{0,4},{1,5},{2,6},{3,7},{4,0},{5,1},{6,2},{7,3},{8,12},{9,13},{10,... | collective-permute-start | bytes 245768 | tf_op jit(solution)/shard_map/ppermute | solution.py:392
  26.0 0.8 pad_maximum_fusion
  26.9 2.4 %collective-permute-done.5 = bf16[2,4,40,128]{3,2,1,0:T(8,128)(2,1)S(1)} collective-permute-done((bf16[2,4,40,128]{3,2,1,0:T(8,128)(2,1)S(1)}, bf16[2,4,40,128]{3,2,1,0:T(8,128)(2,1)S(1)}, u32[]{:S(2)}, u32[]{:S(2)}) %collective-permute-start.5) | collective-permute-done | bytes 81952 | tf_op jit(solution)/shard_map/ppermute | solution.py:392
  29.3 0.8 pad_maximum_fusion.3
  30.4 5.0 %collective-permute-done.6 = bf16[4,4,40,128]{3,2,1,0:T(8,128)(2,1)S(1)} collective-permute-done((bf16[4,4,40,128]{3,2,1,0:T(8,128)(2,1)S(1)}, bf16[4,4,40,128]{3,2,1,0:T(8,128)(2,1)S(1)}, u32[]{:S(2)}, u32[]{:S(2)}) %collective-permute-start.6) | collective-permute-done | bytes 163872 | tf_op jit(solution)/shard_map/ppermute | solution.py:392
  35.4 0.8 pad_maximum_fusion.1
  37.1 28.6 %shard_map.110 = (f32[2,8,128,128]{3,2,1,0:T(8,128)}, bf16[2,8,128,128]{3,2,1,0:T(8,128)(2,1)}) custom-call(bf16[32,40,128]{2,1,0:T(8,128)(2,1)} %bitcast.13, bf16[32,40,128]{2,1,0:T(8,128)(2,1)} %copy-done.3, bf16[256,128]{1,0:T(8,128)(2,1)} %constant.6.clone.depth_dft, bf16[256,256]{1,0:T(8,128)(2,1)} %constant.7.clone.plane_dft, ...), custom_call_target="tpu_custom_call" | custom-call | flops 6442450944 | bytes 8388608 | tf_op jit(solution)/shard_map/pallas_call | solution.py:317
  65.7 1.5 %collective-permute-start.8 = (bf16[2,8,128,128]{3,2,1,0:T(8,128)(2,1)}, bf16[2,8,128,128]{3,2,1,0:T(8,128)(2,1)S(1)}, u32[]{:S(2)}, u32[]{:S(2)}) collective-permute-start(bf16[2,8,128,128]{3,2,1,0:T(8,128)(2,1)} %get-tuple-element.12), channel_id=1, source_target_pairs={{0,16},{16,0},{1,17},{17,1},{2,18},{18,2},{3,19},{19,3},{4,20},{20... | collective-permute-start | bytes 1572872 | tf_op jit(solution)/shard_map/ppermute | solution.py:430
  67.9 28.4 %shard_map.111.second = f32[2,8,128,128]{3,2,1,0:T(8,128)} custom-call(bf16[32,40,128]{2,1,0:T(8,128)(2,1)} %bitcast.15, bf16[32,40,128]{2,1,0:T(8,128)(2,1)} %copy-done.4, bf16[256,128]{1,0:T(8,128)(2,1)} %constant.6.clone.depth_dft, bf16[256,256]{1,0:T(8,128)(2,1)} %constant.7.clone.plane_dft, f32[16,2,8,256]{3,2,1,0:T(8,128)} %constant.8.clone.rows_hbm, ...), custom_call_target="tpu_custom_call" | custom-call | flops 6442450944 | bytes 8388608 | tf_op jit(solution)/shard_map/pallas_call | solution.py:317
  96.4 0.8 copy-done
  97.2 6.0 %shard_map.112 = f32[2,2,8,128,128]{4,3,2,1,0:T(8,128)} custom-call(f32[2,8,128,128]{3,2,1,0:T(8,128)} %get-tuple-element.10.first, f32[2,8,128,128]{3,2,1,0:T(8,128)} %shard_map.111.second, bf16[2,8,128,128]{3,2,1,0:T(8,128)(2,1)} %copy-done), custom_call_target="tpu_custom_call" | custom-call | tf_op jit(solution)/shard_map/pallas_call | solution.py:381
  (16 shorter events, 2.0 us)
Async XLA Ops:
  4.2 6.7 %collective-permute-start = (bf16[1,4,40,128]{3,2,1,0:T(8,128)(2,1)}, bf16[1,4,40,128]{3,2,1,0:T(8,128)(2,1)S(1)}, u32[]{:S(2)}, u32[]{:S(2)}) collective-permute-start(bf16[1,4,40,128]{3,2,1,0:T(8,128)(2,1)} %bitcast.8), channel_id=1, source_target_pairs={{0,8},{1,9},{2,10},{3,11},{4,12},{5,13},{6,14},{7,15},{8,0},{9,1},... | collective-permute-start | bytes 122888 | tf_op jit(solution)/shard_map/ppermute | solution.py:392
  11.7 4.5 %collective-permute-start.1 = (bf16[2,4,40,128]{3,2,1,0:T(8,128)(2,1)S(1)}, bf16[2,4,40,128]{3,2,1,0:T(8,128)(2,1)S(1)}, u32[]{:S(2)}, u32[]{:S(2)}) collective-permute-start(bf16[2,4,40,128]{3,2,1,0:T(8,128)(2,1)S(1)} %pad_maximum_fusion.4), channel_id=1, source_target_pairs={{0,4},{1,5},{2,6},{3,7},{4,0},{5,1},{6,2},{7,3},{8,12},{9,13},{10,... | collective-permute-start | bytes 245768 | tf_op jit(solution)/shard_map/ppermute | solution.py:392
  17.0 9.0 %collective-permute-start.2 = (bf16[4,4,40,128]{3,2,1,0:T(8,128)(2,1)S(1)}, bf16[4,4,40,128]{3,2,1,0:T(8,128)(2,1)S(1)}, u32[]{:S(2)}, u32[]{:S(2)}) collective-permute-start(bf16[4,4,40,128]{3,2,1,0:T(8,128)(2,1)S(1)} %pad_maximum_fusion.2), channel_id=1, source_target_pairs={{0,2},{1,3},{2,0},{3,1},{4,6},{5,7},{6,4},{7,5},{8,10},{9,11},{10,... | collective-permute-start | bytes 491528 | tf_op jit(solution)/shard_map/ppermute | solution.py:392
  18.7 5.2 %collective-permute-start.4 = (bf16[1,4,40,128]{3,2,1,0:T(8,128)(2,1)}, bf16[1,4,40,128]{3,2,1,0:T(8,128)(2,1)S(1)}, u32[]{:S(2)}, u32[]{:S(2)}) collective-permute-start(bf16[1,4,40,128]{3,2,1,0:T(8,128)(2,1)} %bitcast.4), channel_id=1, source_target_pairs={{0,8},{1,9},{2,10},{3,11},{4,12},{5,13},{6,14},{7,15},{8,0},{9,1},... | collective-permute-start | bytes 122888 | tf_op jit(solution)/shard_map/ppermute | solution.py:392
  24.8 4.5 %collective-permute-start.5 = (bf16[2,4,40,128]{3,2,1,0:T(8,128)(2,1)S(1)}, bf16[2,4,40,128]{3,2,1,0:T(8,128)(2,1)S(1)}, u32[]{:S(2)}, u32[]{:S(2)}) collective-permute-start(bf16[2,4,40,128]{3,2,1,0:T(8,128)(2,1)S(1)} %pad_maximum_fusion.5), channel_id=1, source_target_pairs={{0,4},{1,5},{2,6},{3,7},{4,0},{5,1},{6,2},{7,3},{8,12},{9,13},{10,... | collective-permute-start | bytes 245768 | tf_op jit(solution)/shard_map/ppermute | solution.py:392
  26.8 9.6 %copy-start.1 = (bf16[8,4,40,128]{3,2,1,0:T(8,128)(2,1)}, bf16[8,4,40,128]{3,2,1,0:T(8,128)(2,1)S(1)}, u32[]{:S(2)}) copy-start(bf16[8,4,40,128]{3,2,1,0:T(8,128)(2,1)S(1)} %pad_maximum_fusion) | copy-start | bytes 983044
  26.8 9.6 %collective-permute-start.3 = (bf16[32,40,128]{2,1,0:T(8,128)(2,1)S(1)}, bf16[32,40,128]{2,1,0:T(8,128)(2,1)S(1)}, u32[]{:S(2)}, u32[]{:S(2)}) collective-permute-start(bf16[32,40,128]{2,1,0:T(8,128)(2,1)S(1)} %bitcast.12), channel_id=1, source_target_pairs={{0,1},{1,0},{2,3},{3,2},{4,5},{5,4},{6,7},{7,6},{8,9},{9,8},{10,11... | collective-permute-start | bytes 983048 | tf_op jit(solution)/shard_map/ppermute | solution.py:392
  30.1 5.4 %collective-permute-start.6 = (bf16[4,4,40,128]{3,2,1,0:T(8,128)(2,1)S(1)}, bf16[4,4,40,128]{3,2,1,0:T(8,128)(2,1)S(1)}, u32[]{:S(2)}, u32[]{:S(2)}) collective-permute-start(bf16[4,4,40,128]{3,2,1,0:T(8,128)(2,1)S(1)} %pad_maximum_fusion.3), channel_id=1, source_target_pairs={{0,2},{1,3},{2,0},{3,1},{4,6},{5,7},{6,4},{7,5},{8,10},{9,11},{10,... | collective-permute-start | bytes 491528 | tf_op jit(solution)/shard_map/ppermute | solution.py:392
  36.3 29.4 %copy-start.2 = (bf16[8,4,40,128]{3,2,1,0:T(8,128)(2,1)}, bf16[8,4,40,128]{3,2,1,0:T(8,128)(2,1)S(1)}, u32[]{:S(2)}) copy-start(bf16[8,4,40,128]{3,2,1,0:T(8,128)(2,1)S(1)} %pad_maximum_fusion.1) | copy-start | bytes 983044
  36.3 30.9 %collective-permute-start.7 = (bf16[32,40,128]{2,1,0:T(8,128)(2,1)S(1)}, bf16[32,40,128]{2,1,0:T(8,128)(2,1)S(1)}, u32[]{:S(2)}, u32[]{:S(2)}) collective-permute-start(bf16[32,40,128]{2,1,0:T(8,128)(2,1)S(1)} %bitcast.14), channel_id=1, source_target_pairs={{0,1},{1,0},{2,3},{3,2},{4,5},{5,4},{6,7},{7,6},{8,9},{9,8},{10,11... | collective-permute-start | bytes 983048 | tf_op jit(solution)/shard_map/ppermute | solution.py:392
  36.4 0.7 copy-start.3
  65.7 30.7 %collective-permute-start.8 = (bf16[2,8,128,128]{3,2,1,0:T(8,128)(2,1)}, bf16[2,8,128,128]{3,2,1,0:T(8,128)(2,1)S(1)}, u32[]{:S(2)}, u32[]{:S(2)}) collective-permute-start(bf16[2,8,128,128]{3,2,1,0:T(8,128)(2,1)} %get-tuple-element.12), channel_id=1, source_target_pairs={{0,16},{16,0},{1,17},{17,1},{2,18},{18,2},{3,19},{19,3},{4,20},{20... | collective-permute-start | bytes 1572872 | tf_op jit(solution)/shard_map/ppermute | solution.py:430
  67.2 0.7 copy-start.4
  96.4 0.8 copy-start

commit v4 on v3

--- a/solution.py
+++ b/solution.py
@@ -18,9 +18,9 @@
 LAMBDA_TV = 0.3
 TERMS = 40
 UNROLL = 8
-GROUPS = 8
-LAST_REFS = 15
-VMEM_LIMIT = 56 * 1024 * 1024
+GROUPS = 16
+LAST_REFS = 16
+VMEM_LIMIT = 52 * 1024 * 1024
 
 
 def kaiser_coefficients():
@@ -44,25 +44,12 @@
     return (positions[:, None] * positions[None, :] % grid_size) * (2.0 * math.pi / grid_size)
 
 
-def depth_table(grid_size):
-    angles = dft_angles(grid_size)
-    return jnp.asarray(np.concatenate([np.cos(angles), np.sin(angles)], axis=0), jnp.bfloat16)
-
-
 def plane_table(grid_size):
     angles = dft_angles(grid_size)
     cosine, sine = np.cos(angles), np.sin(angles)
     parts = np.stack([np.concatenate([cosine, -sine], 1), np.concatenate([sine, cosine], 1)])
     tiles = parts.reshape(2, grid_size // 8, 8, 2 * grid_size).swapaxes(0, 1)
     return jnp.asarray(tiles.reshape(2 * grid_size, 2 * grid_size), jnp.bfloat16)
-
-
-def row_table(grid_size, tile_count):
-    slab = grid_size // tile_count
-    lanes = -(-(grid_size + WIN) // 128) * 128
-    rows = np.arange(tile_count)[:, None, None] * slab + np.arange(YROWS)[:, None]
-    angles = (rows * np.arange(lanes) % grid_size) * (2.0 * math.pi / grid_size)
-    return jnp.asarray(np.stack([np.cos(angles), np.sin(angles)], axis=1), jnp.float32)
 
 
 def shared_first():
@@ -76,13 +63,13 @@
         frame = jnp.where(shared_first(), last - place, place)
         rows = [
             density[frame].astype(jnp.float32)[:, None],
-            fractions[frame].astype(jnp.float32),
+            jnp.swapaxes(fractions[frame].astype(jnp.float32), 0, 1),
             shift[frame].astype(jnp.float32)[:, None],
             depth[frame].astype(jnp.float32)[:, None],
         ]
         for block in range(blocks):
             ends = [
-                jnp.full((1, count), corner[frame, block, axis], jnp.int32).astype(jnp.float32)
+                jnp.full((1, count), corner[frame, axis, block], jnp.int32).astype(jnp.float32)
                 for axis in range(2)
             ]
             parts = [samples[frame, block].astype(jnp.float32)] + [row[block] for row in rows] + ends
@@ -98,22 +85,22 @@
         out_shape=(shape,) * frames,
         in_specs=[whole] * 5 + [pl.BlockSpec(memory_space=pltpu.SMEM)],
         out_specs=(whole,) * frames,
-    )(samples, density, fractions, shift, depth, corner)
+    )(samples, density, jnp.swapaxes(fractions, 1, 2), shift, depth, jnp.swapaxes(corner, 1, 2))
 
 
 def frame_kernel(
-    own, other, depth_dft, plane_dft, rows_hbm, maps_hbm, estimate_hbm, half, *rest, place, scale,
+    own, other, plane_hbm, maps_hbm, estimate_hbm, half, *rest, place, scale,
 ):
     half_small = rest[0] if len(rest) == LAST_REFS + 1 else None
     frame_body(
-        own, other, depth_dft, plane_dft, rows_hbm, maps_hbm, estimate_hbm, half, half_small,
+        own, other, plane_hbm, maps_hbm, estimate_hbm, half, half_small,
         *rest[-LAST_REFS:], place=place, scale=scale,
     )
 
 
 def frame_body(
-    own, other, depth_dft, plane_dft, rows_hbm, maps_hbm, estimate_hbm, half, half_small,
-    cos_rows, sin_rows, corner_rows, corner, row_phases,
+    own, other, plane_hbm, maps_hbm, estimate_hbm, half, half_small,
+    depth_dft, plane_dft, cos_rows, sin_rows, corner_rows, corner,
     grid_real, grid_imag, left, weights, weight_x, weight_y, maps, estimate, total, sems,
     *, place, scale,
 ):
@@ -126,8 +113,8 @@
         pltpu.make_async_copy(maps_hbm, maps, sems.at[0]),
         pltpu.make_async_copy(estimate_hbm.at[frame], estimate, sems.at[1]),
     ]
-    phases = pltpu.make_async_copy(rows_hbm.at[lax.axis_index("tile")], row_phases, sems.at[2])
-    phases.start()
+    planes = pltpu.make_async_copy(plane_hbm, plane_dft, sems.at[2])
+    planes.start()
     for copy in copies:
         copy.start()
     for source, offset in ((own, 0), (other, blocks)):
@@ -136,11 +123,18 @@
             corner_rows[pl.ds(offset + block, 1), :] = (ends[:1] + grid_size * ends[1:]).astype(jnp.int32)
     corners = pltpu.make_async_copy(corner_rows, corner, sems.at[3])
     corners.start()
-    phases.wait()
-    for position in range(grid_size + WIN):
-        at = slice(position, position + 1)
-        cos_rows[position] = jnp.broadcast_to(row_phases[0, :, at], (YROWS, samples))
-        sin_rows[position] = jnp.broadcast_to(row_phases[1, :, at], (YROWS, samples))
+    lanes = -(-(grid_size + WIN) // 128) * 128
+    position = lax.broadcasted_iota(jnp.int32, (YROWS, lanes), 1)
+    image_y = lax.axis_index("tile") * slab + lax.broadcasted_iota(jnp.int32, (YROWS, lanes), 0)
+    angles = lax.rem(position * image_y, grid_size).astype(jnp.float32) * (2.0 * math.pi / grid_size)
+    for table, phases in ((cos_rows, jnp.cos(angles)), (sin_rows, jnp.sin(angles))):
+        for k in range(grid_size + WIN):
+            table[k] = jnp.broadcast_to(phases[:, k : k + 1], (YROWS, samples))
+    planes.wait()
+    tiles = plane_dft[:, :grid_size].astype(jnp.float32).reshape(grid_size // 8, 2, 8, grid_size)
+    for part in range(2):
+        at = slice(part * grid_size, (part + 1) * grid_size)
+        depth_dft[at, :] = tiles[:, part].reshape(grid_size, grid_size).astype(jnp.bfloat16)
 
     table = depth_dft[...]
     taps = lax.broadcasted_iota(jnp.int32, (8, 2 * samples), 0).astype(jnp.float32)
@@ -259,81 +253,91 @@
         copy.wait()
 
     columns = weights
-    groups = len(grid_real)
-
-    def coil_sums(index, carry):
-        for place in range(groups):
-            lanes = slice((place % 2) * grid_size, (place % 2 + 1) * grid_size)
-            first = (place // 2) * YROWS
+    pairs = coils // 2
+    per = grid_real[0].shape[0]
+
+    def transpose(step, carry):
+        start = step * 16
+        for coil in range(coils):
+            lanes = slice((coil % 2) * grid_size, (coil % 2 + 1) * grid_size)
             for part, refs in enumerate((grid_real, grid_imag)):
-                for start in range(0, grid_size, 16):
-                    planes = refs[place][index, start * YROWS : (start + 16) * YROWS, :]
-                    rows = jnp.swapaxes(planes.reshape(16, YROWS, grid_size), 0, 1)
-                    at = slice(part * grid_size + start, part * grid_size + start + 16)
-                    columns[first : first + YROWS, at, lanes] = rows.astype(jnp.bfloat16)
-        for row in range(slab):
+                at = pl.ds(pl.multiple_of(start * YROWS, 16 * YROWS), 16 * YROWS)
+                planes = refs[coil // per][coil % per, at, :].reshape(16, YROWS, grid_size)
+                rows = jnp.swapaxes(planes, 0, 1).astype(jnp.bfloat16)
+                at = pl.ds(pl.multiple_of(part * grid_size + start, 16), 16)
+                for row in range(slab):
+                    columns[row * pairs + coil // 2, at, lanes] = rows[row]
+        return carry
+
+    lax.fori_loop(0, grid_size // 16, transpose, 0)
+
+    def image_row(row, carry):
+        for quad in range(coils // 4):
             images = [
                 jnp.dot(
-                    plane_dft[...], columns[pair * YROWS + row], preferred_element_type=jnp.float32
+                    plane_dft[...], columns[row * pairs + pair], preferred_element_type=jnp.float32
                 )
-                for pair in range(groups // 2)
+                for pair in (2 * quad, 2 * quad + 1)
             ]
             for tile in range(grid_size // 16):
                 at = pl.ds(tile * 16, 16)
-                sum_real, sum_imag = total[0, row, at], total[1, row, at]
-                for place in range(groups):
-                    coil = place * (coils // groups) + index
+                sums = [[], []]
+                for place in range(4):
+                    coil = 4 * quad + place
                     column = (place % 2) * grid_size
                     image = images[place // 2][tile * 32 : tile * 32 + 32, column : column + grid_size]
                     image_real = jnp.concatenate([image[:8], image[16:24]], axis=0)
                     image_imag = jnp.concatenate([image[8:16], image[24:]], axis=0)
                     map_real = maps[coil, 0, row, at].astype(jnp.float32)
                     map_imag = maps[coil, 1, row, at].astype(jnp.float32)
-                    sum_real = sum_real + (map_real * image_real + map_imag * image_imag)
-                    sum_imag = sum_imag + (map_real * image_imag - map_imag * image_real)
-                total[0, row, at] = sum_real
-                total[1, row, at] = sum_imag
+                    sums[0].append(map_real * image_real + map_imag * image_imag)
+                    sums[1].append(map_real * image_imag - map_imag * image_real)
+                for part in range(2):
+                    value = (sums[part][0] + sums[part][1]) + (sums[part][2] + sums[part][3])
+                    if quad > 0:
+                        value = value + total[part, at]
+                    if quad < coils // 4 - 1:
+                        total[part, at] = value
+                    else:
+                        value = estimate[part, row, at] + scale * value
+                        half[part, row, at] = value
+                        if half_small is not None:
+                            half_small[part, row, at] = value.astype(jnp.bfloat16)
         return carry
 
-    total[...] = jnp.zeros_like(total)
-    lax.fori_loop(0, coils // groups, coil_sums, 0)
-    for part in range(2):
-        for row in range(slab):
-            value = estimate[part, row] + scale * total[part, row]
-            half[part, row] = value
-            if half_small is not None:
-                half_small[part, row] = value.astype(jnp.bfloat16)
-
-
-def frame_image(own, other, tables, coil_maps, estimate, scale, place, shared):
+    lax.fori_loop(0, slab, image_row, 0)
+
+
+def frame_image(own, other, plane_dft, coil_maps, estimate, scale, place, shared):
     blocks, _, samples = own.shape
     coils, _, slab, grid_size, _ = coil_maps.shape
     shape = (2, slab, grid_size, grid_size)
     whole = pl.BlockSpec(memory_space=pltpu.VMEM)
-    away = pl.BlockSpec(memory_space=pl.ANY)
+    away = pl.BlockSpec(memory_space=pltpu.HBM)
     unroll = math.gcd(blocks, UNROLL)
-    grid_shape = (coils // GROUPS, (grid_size + WIN) * YROWS, grid_size)
+    grid_shape = (coils // math.gcd(coils, GROUPS), (grid_size + WIN) * YROWS, grid_size)
     outs = (jnp.float32, jnp.bfloat16)[: 2 if shared else 1]
     return pl.pallas_call(
         functools.partial(frame_kernel, place=place, scale=scale),
         out_shape=tuple(jax.ShapeDtypeStruct(shape, kind) for kind in outs),
-        in_specs=[whole] * 4 + [away] * 3,
+        in_specs=[whole] * 2 + [away] * 3,
         out_specs=(whole,) * len(outs),
         scratch_shapes=[
+            pltpu.VMEM((2 * grid_size, grid_size), jnp.bfloat16),
+            pltpu.VMEM(plane_dft.shape, jnp.bfloat16),
             pltpu.VMEM((grid_size + WIN, YROWS, samples), jnp.float32),
             pltpu.VMEM((grid_size + WIN, YROWS, samples), jnp.float32),
             pltpu.VMEM((2 * blocks, samples), jnp.int32),
             pltpu.SMEM((2 * blocks, samples), jnp.int32),
-            pltpu.VMEM(tables[2].shape[1:], jnp.float32),
-            [pltpu.VMEM(grid_shape, jnp.float32)] * GROUPS,
-            [pltpu.VMEM(grid_shape, jnp.float32)] * GROUPS,
+            [pltpu.VMEM(grid_shape, jnp.float32)] * math.gcd(coils, GROUPS),
+            [pltpu.VMEM(grid_shape, jnp.float32)] * math.gcd(coils, GROUPS),
             [pltpu.VMEM((coils * TAPS * YROWS, 2 * samples), jnp.bfloat16)] * unroll,
             pltpu.VMEM((2 * blocks, 2 * grid_size, 2 * samples), jnp.bfloat16),
             pltpu.VMEM((2 * blocks, 8, samples), jnp.float32),
             pltpu.VMEM((2 * blocks, 8, samples), jnp.float32),
             pltpu.VMEM(coil_maps.shape, jnp.bfloat16),
             pltpu.VMEM(shape, jnp.float32),
-            pltpu.VMEM(shape, jnp.float32),
+            pltpu.VMEM((2, grid_size, grid_size), jnp.float32),
             pltpu.SemaphoreType.DMA((4,)),
         ],
         compiler_params=pltpu.CompilerParams(vmem_limit_bytes=VMEM_LIMIT),
@@ -342,48 +346,55 @@
             bytes_accessed=coil_maps.size * 2,
             transcendentals=0,
         ),
-    )(own, other, *tables, coil_maps, estimate)
-
-
-def step_kernel(first, second, beside_first, beside_second, out):
+    )(own, other, plane_dft, coil_maps, estimate)
+
+
+def step_kernel(first, second, *rest):
+    *besides, out_hbm, out, sems = rest
     index, count = lax.axis_index("frame"), lax.axis_size("frame")
     even = shared_first()
+    place = jnp.where(even, 1, 0)
+    there = (
+        jnp.where(even, index + 1 < count, True),
+        jnp.where(even, index > 0, index + 1 < count),
+    )
 
     def slope(low, high):
         change = high - low
         return change * lax.rsqrt(change[0] * change[0] + change[1] * change[1] + EPS * EPS)[None]
 
-    values = first[...], second[...]
-    pull = slope(values[0], values[1])
-    has = (
-        jnp.where(even, index + 1 < count, True),
-        jnp.where(even, index > 0, index + 1 < count),
-    )
-    place = jnp.where(even, 1, 0)
-    for value, inner, beside, there, at in (
-        (values[0], pull, beside_first, has[0], place),
-        (values[1], -pull, beside_second, has[1], 1 - place),
-    ):
-        if beside is not None:
-            outer = slope(value, beside[...].astype(jnp.float32))
-            inner = inner + jnp.where(there, outer, 0.0)
-        out[at] = value + LAMBDA_TV * inner
+    copies = []
+    for row in range(out.shape[2]):
+        values = first[:, row], second[:, row]
+        pull = slope(values[0], values[1])
+        pulls = [pull, -pull]
+        for side, beside in enumerate(besides):
+            outer = slope(values[side], beside[:, row].astype(jnp.float32))
+            pulls[side] = pulls[side] + jnp.where(there[side], outer, 0.0)
+        for side, at in enumerate((place, 1 - place)):
+            out[side, :, row] = values[side] + LAMBDA_TV * pulls[side]
+            copies.append(pltpu.make_async_copy(
+                out.at[side, :, row], out_hbm.at[at, :, row], sems.at[side, row]
+            ))
+            copies[-1].start()
+    for copy in copies:
+        copy.wait()
 
 
 def tv_step(halves, received):
-    parts, slab, grid_size, _ = halves[0].shape
-    block = pl.BlockSpec((parts, 1, grid_size, grid_size), lambda row: (0, row, 0, 0))
     given = [value for value in received if value is not None]
-
-    def kernel(first, second, *rest):
-        step_kernel(first, second, rest[0], rest[1] if len(given) > 1 else None, rest[-1])
-
+    whole = pl.BlockSpec(memory_space=pltpu.VMEM)
+    shape = (2,) + halves[0].shape
     return pl.pallas_call(
-        kernel,
-        grid=(slab,),
-        out_shape=jax.ShapeDtypeStruct((2,) + halves[0].shape, jnp.float32),
-        in_specs=[block] * (2 + len(given)),
-        out_specs=pl.BlockSpec((2, parts, 1, grid_size, grid_size), lambda row: (0, 0, row, 0, 0)),
+        step_kernel,
+        out_shape=jax.ShapeDtypeStruct(shape, jnp.float32),
+        in_specs=[whole] * (2 + len(given)),
+        out_specs=pl.BlockSpec(memory_space=pltpu.HBM),
+        scratch_shapes=[
+            pltpu.VMEM(shape, jnp.float32),
+            pltpu.SemaphoreType.DMA((2, shape[2])),
+        ],
+        compiler_params=pltpu.CompilerParams(vmem_limit_bytes=VMEM_LIMIT // 4),
     )(*halves, *given)
 
 
@@ -392,14 +403,13 @@
     return lax.ppermute(values, axis, [(index, index ^ bit) for index in range(count)])
 
 
-def gather_blocks(packed):
-    count = lax.axis_size("tile")
-    held = packed[None]
-    bits = [1 << place for place in range(1, count.bit_length() - 1)]
-    for bit in reversed(bits):
-        held = jnp.concatenate([held, swap(held, "tile", bit)], axis=0)
-    held = held.reshape((-1,) + packed.shape[1:])
-    return held, swap(held, "tile", 1)
+def join_halves(held):
+    return jnp.concatenate([held, swap(held, "tile", lax.axis_size("tile") // 2)], axis=0)
+
+
+def chips(held):
+    shifts = range(2, lax.axis_size("tile") // 2, 2)
+    return [held] + [swap(held, "tile", shift) for shift in shifts]
 
 
 def on_device(
@@ -414,17 +424,27 @@
     packed = pack_blocks(
         kspace_samples, density, sample_frac, row_offsets, depth_base, block_base
     )
-    tables = depth_table(grid_size), plane_table(grid_size), row_table(grid_size, tile_count)
+    plane_dft = plane_table(grid_size)
     pairs = [
         [(index, index ^ 1) for index in range(frame_count) if index ^ 1 < frame_count],
         [(index, index - 1) for index in range(2, frame_count, 2)],
     ]
     pairs[1] += [(target, source) for source, target in pairs[1]]
+    shared, rest = packed
+    shared = join_halves(shared)
+    rest, shared = lax.optimization_barrier((rest, shared))
+    rest = join_halves(rest)
+    shared = chips(shared)
+    rest, *shared = lax.optimization_barrier((rest, *shared))
+    held = [jnp.concatenate(shared, axis=0), chips(rest)]
     halves, received = [], []
     for place in range(2):
-        own, other = gather_blocks(packed[place])
+        if place == 1:
+            (*pieces, halves[0]) = lax.optimization_barrier((*held[1], halves[0]))
+            held[1] = jnp.concatenate(pieces, axis=0)
         half, *small = frame_image(
-            own, other, tables, coil_maps, estimate, scale, place, bool(pairs[place])
+            held[place], swap(held[place], "tile", 1), plane_dft, coil_maps, estimate, scale, place,
+            bool(pairs[place]),
         )
         halves.append(half)
         received.append(lax.ppermute(small[0], "frame", pairs[place]) if small else None)

time: 104 us -> 76.7 us (0.74)
  Pallas kernels: 64.5 us -> 52.5 us
  waiting for transfers between devices: 15.9 us -> 5.86 us
  local copies, waits for them, and re-layouts: 4.9 us -> 1.03 us
  other arithmetic: 4.79 us -> 1.58 us
  starting transfers between devices: 12.9 us -> 15.3 us
    ppermute x8 -> x10, waiting for transfers between devices: 15.9 us -> 5.85 us  [swap(): lax.ppermute(values, axis, [(index, index ^ bit) for index in range(count)])]
    pallas_call x2, Pallas kernels: 57 us -> 49.4 us  [frame_image(): pl.pallas_call(functools.partial(frame_kernel, place=place, scale=scale),...]
    pallas_call x1, Pallas kernels: 6 us -> 1.5 us  [tv_step(): pl.pallas_call(step_kernel, out_shape=jax.ShapeDtypeStruct(shape, jnp.flo...]
    unnamed x12, local copies, waits for them, and re-layouts: 4.9 us -> 1 us
    concatenate x6 -> x2, other arithmetic: 4.79 us -> 1.58 us  [join_halves(): jnp.concatenate([held, swap(held, 'tile', lax.axis_size('tile') // 2)], a...]
    ppermute x8 -> x10, starting transfers between devices: 11.4 us -> 13.8 us  [swap(): lax.ppermute(values, axis, [(index, index ^ bit) for index in range(count)])]
  transfers between devices with their start and end apart: 9 -> 11, of which waited for: 5 -> 5; matrix products, arithmetic and copies ran while one was open for 3% -> 1% of each run, Pallas kernels for 55% -> 65%
where the time goes in v4:
time: 76.7 us; the launch traced here: 76.4 us
  Pallas kernels  52.5 us (68%)
  starting transfers between devices  15.3 us (20%)
  waiting for transfers between devices  5.86 us (8%)
  other arithmetic  1.58 us (2%)
  local copies, waits for them, and re-layouts  1.03 us (1%)
    pallas_call x2, Pallas kernels, frame_image(): pl.pallas_call(functools.partial(frame_kernel, place=place, scale=scale),...  49.4 us
    ppermute x10, starting transfers between devices, swap(): lax.ppermute(values, axis, [(index, index ^ bit) for index in range(count)])  13.8 us
    ppermute x10, waiting for transfers between devices, swap(): lax.ppermute(values, axis, [(index, index ^ bit) for index in range(count)])  5.85 us
    concatenate x2, other arithmetic, join_halves(): jnp.concatenate([held, swap(held, 'tile', lax.axis_size('tile') // 2)], a...  1.58 us
    pallas_call x1, Pallas kernels, pack_blocks(): pl.pallas_call(pack_kernel, out_shape=(shape,) * frames, in_specs=[whole]...  1.55 us
  transfers between devices with their start and end apart: 11, of which 5 were waited for; matrix products, arithmetic and copies ran while one was open for 1% of the time, Pallas kernels for 65%

profile of v4, /device:TPU:0, one launch (start us, length us, event | category | flops | bytes accessed | tf_op | source)
XLA Modules:
  0.0 76.4 jit_solution(7229403325661182306)
XLA Ops:
  0.0 1.6 %shard_map.91 = (bf16[4,40,128]{2,1,0:T(8,128)(2,1)}, bf16[4,40,128]{2,1,0:T(8,128)(2,1)}) custom-call(bf16[2,4,32,128]{3,2,1,0:T(8,128)(2,1)} %samples.1, bf16[2,4,128]{2,1,0:T(4,128)(2,1)} %density.1, bf16[2,3,4,128]{3,2,1,0:T(4,128)(2,1)} %bitcast.2, s32[2,4,128]{2,1,0:T(4,128)} %shift.1, s32[2,4,128]{2,1,0:T(4,128)} %depth.1, s32[2,2,4]{2,1,0:T(2,128)} %bitcast.3), custom_call_target="tpu_custom_call" | custom-call | tf_op jit(solution)/shard_map/pallas_call | solution.py:83
  1.6 4.0 %collective-permute-start = (bf16[4,40,128]{2,1,0:T(8,128)(2,1)}, bf16[4,40,128]{2,1,0:T(8,128)(2,1)S(1)}, u32[]{:S(2)}, u32[]{:S(2)}) collective-permute-start(bf16[4,40,128]{2,1,0:T(8,128)(2,1)} %get-tuple-element.22), channel_id=1, source_target_pairs={{0,8},{1,9},{2,10},{3,11},{4,12},{5,13},{6,14},{7,15},{8,0},{9,1},... | collective-permute-start | bytes 122888 | tf_op jit(solution)/shard_map/ppermute | solution.py:403
  5.6 2.6 %collective-permute-done = bf16[4,40,128]{2,1,0:T(8,128)(2,1)S(1)} collective-permute-done((bf16[4,40,128]{2,1,0:T(8,128)(2,1)}, bf16[4,40,128]{2,1,0:T(8,128)(2,1)S(1)}, u32[]{:S(2)}, u32[]{:S(2)}) %collective-permute-start) | collective-permute-done | bytes 40992 | tf_op jit(solution)/shard_map/ppermute | solution.py:403
  8.2 0.8 %pad_maximum_fusion = bf16[8,40,128]{2,1,0:T(8,128)(2,1)S(1)} fusion(bf16[4,40,128]{2,1,0:T(8,128)(2,1)S(1)} %collective-permute-done, bf16[4,40,128]{2,1,0:T(8,128)(2,1)} %get-tuple-element.22), kind=kLoop, calls=%fused_computation | loop fusion | flops 40960 | bytes 163840 | tf_op jit(solution)/shard_map/concatenate | solution.py:407
  9.0 2.6 %collective-permute-start.1 = (bf16[4,40,128]{2,1,0:T(8,128)(2,1)}, bf16[4,40,128]{2,1,0:T(8,128)(2,1)S(1)}, u32[]{:S(2)}, u32[]{:S(2)}) collective-permute-start(bf16[4,40,128]{2,1,0:T(8,128)(2,1)} %get-tuple-element.23), channel_id=1, source_target_pairs={{0,8},{1,9},{2,10},{3,11},{4,12},{5,13},{6,14},{7,15},{8,0},{9,1},... | collective-permute-start | bytes 122888 | tf_op jit(solution)/shard_map/ppermute | solution.py:403
  11.6 2.8 %collective-permute-start.4 = (bf16[8,40,128]{2,1,0:T(8,128)(2,1)S(1)}, bf16[8,40,128]{2,1,0:T(8,128)(2,1)S(1)}, u32[]{:S(2)}, u32[]{:S(2)}) collective-permute-start(bf16[8,40,128]{2,1,0:T(8,128)(2,1)S(1)} %pad_maximum_fusion), channel_id=1, source_target_pairs={{0,6},{1,7},{2,4},{3,5},{4,2},{5,3},{6,0},{7,1},{8,14},{9,15},{10,... | collective-permute-start | bytes 245768 | tf_op jit(solution)/shard_map/ppermute | solution.py:403
  14.4 0.2 collective-permute-start.3
  14.6 0.5 collective-permute-start.2
  15.1 0.8 %pad_maximum_fusion.1 = bf16[8,40,128]{2,1,0:T(8,128)(2,1)S(1)} fusion(bf16[4,40,128]{2,1,0:T(8,128)(2,1)S(1)} %collective-permute-done.1, bf16[4,40,128]{2,1,0:T(8,128)(2,1)} %get-tuple-element.23), kind=kLoop, calls=%fused_computation.1 | loop fusion | flops 40960 | bytes 163840 | tf_op jit(solution)/shard_map/concatenate | solution.py:407
  15.9 1.2 %collective-permute-done.4 = bf16[8,40,128]{2,1,0:T(8,128)(2,1)S(1)} collective-permute-done((bf16[8,40,128]{2,1,0:T(8,128)(2,1)S(1)}, bf16[8,40,128]{2,1,0:T(8,128)(2,1)S(1)}, u32[]{:S(2)}, u32[]{:S(2)}) %collective-permute-start.4) | collective-permute-done | bytes 81952 | tf_op jit(solution)/shard_map/ppermute | solution.py:403
  17.1 1.7 %collective-permute-done.3 = bf16[8,40,128]{2,1,0:T(8,128)(2,1)S(1)} collective-permute-done((bf16[8,40,128]{2,1,0:T(8,128)(2,1)S(1)}, bf16[8,40,128]{2,1,0:T(8,128)(2,1)S(1)}, u32[]{:S(2)}, u32[]{:S(2)}) %collective-permute-start.3) | collective-permute-done | bytes 81952 | tf_op jit(solution)/shard_map/ppermute | solution.py:403
  18.8 0.2 collective-permute-done.2
  19.1 0.0 copy-start.2
  19.1 0.1 collective-permute-start.8
  19.2 1.9 %collective-permute-start.7 = (bf16[8,40,128]{2,1,0:T(8,128)(2,1)S(1)}, bf16[8,40,128]{2,1,0:T(8,128)(2,1)S(1)}, u32[]{:S(2)}, u32[]{:S(2)}) collective-permute-start(bf16[8,40,128]{2,1,0:T(8,128)(2,1)S(1)} %pad_maximum_fusion.1), channel_id=1, source_target_pairs={{0,6},{1,7},{2,4},{3,5},{4,2},{5,3},{6,0},{7,1},{8,14},{9,15},{10,... | collective-permute-start | bytes 245768 | tf_op jit(solution)/shard_map/ppermute | solution.py:403
  21.1 0.2 collective-permute-start.6
  21.2 1.5 %collective-permute-start.5 = (bf16[8,40,128]{2,1,0:T(8,128)(2,1)S(1)}, bf16[8,40,128]{2,1,0:T(8,128)(2,1)S(1)}, u32[]{:S(2)}, u32[]{:S(2)}) collective-permute-start(bf16[8,40,128]{2,1,0:T(8,128)(2,1)S(1)} %pad_maximum_fusion.1), channel_id=1, source_target_pairs={{0,2},{1,3},{2,0},{3,1},{4,6},{5,7},{6,4},{7,5},{8,10},{9,11},{10,... | collective-permute-start | bytes 245768 | tf_op jit(solution)/shard_map/ppermute | solution.py:403
  22.7 0.9 %copy-done.1 = bf16[256,256]{1,0:T(8,128)(2,1)S(1)} copy-done((bf16[256,256]{1,0:T(8,128)(2,1)S(1)}, bf16[256,256]{1,0:T(8,128)(2,1)}, u32[]{:S(2)}) %copy-start.1) | copy-done | bytes 131096
  23.6 25.2 %shard_map.92 = (f32[2,8,128,128]{3,2,1,0:T(8,128)}, bf16[2,8,128,128]{3,2,1,0:T(8,128)(2,1)S(1)}) custom-call(bf16[32,40,128]{2,1,0:T(8,128)(2,1)S(1)} %constant_dynamic-update-slice_fusion.own, bf16[32,40,128]{2,1,0:T(8,128)(2,1)S(1)} %collective-permute-done.8.other, bf16[256,256]{1,0:T(8,128)(2,1)S(1)} %copy-done.1, ...), custom_call_target="tpu_custom_call" | custom-call | flops 6442450944 | bytes 8388608 | tf_op jit(solution)/shard_map/pallas_call | solution.py:320
  49.0 0.1 collective-permute-start.9
  49.0 1.5 %collective-permute-start.10 = (bf16[2,8,128,128]{3,2,1,0:T(8,128)(2,1)S(1)}, bf16[2,8,128,128]{3,2,1,0:T(8,128)(2,1)S(1)}, u32[]{:S(2)}, u32[]{:S(2)}) collective-permute-start(bf16[2,8,128,128]{3,2,1,0:T(8,128)(2,1)S(1)} %get-tuple-element.36), channel_id=1, source_target_pairs={{0,16},{16,0},{1,17},{17,1},{2,18},{18,2},{3,19},{19,3},{4,20},{20... | collective-permute-start | bytes 1572872 | tf_op jit(solution)/shard_map/ppermute | solution.py:450
  50.6 0.1 collective-permute-done.9.other
  50.7 24.2 %shard_map.93.second = f32[2,8,128,128]{3,2,1,0:T(8,128)S(1)} custom-call(bf16[32,40,128]{2,1,0:T(8,128)(2,1)S(1)} %constant_dynamic-update-slice_fusion.4.own, bf16[32,40,128]{2,1,0:T(8,128)(2,1)S(1)} %collective-permute-done.9.other, bf16[256,256]{1,0:T(8,128)(2,1)S(1)} %copy-done.2, bf16[16,2,8,128,128]{4,3,2,1,0:T(8,128)(2,1)} %maps_hbm.3, ...), custom_call_target="tpu_custom_call" | custom-call | flops 6442450944 | bytes 8388608 | tf_op jit(solution)/shard_map/pallas_call | solution.py:320
  74.9 1.5 %shard_map.94 = f32[2,2,8,128,128]{4,3,2,1,0:T(8,128)} custom-call(f32[2,8,128,128]{3,2,1,0:T(8,128)S(1)} %copy-done, f32[2,8,128,128]{3,2,1,0:T(8,128)S(1)} %shard_map.93.second, bf16[2,8,128,128]{3,2,1,0:T(8,128)(2,1)S(1)} %collective-permute-done.10.rest_0_), custom_call_target="tpu_custom_call" | custom-call | tf_op jit(solution)/shard_map/pallas_call | solution.py:388
  (18 shorter events, 0.1 us)
Async XLA Ops:
  1.6 6.7 %collective-permute-start = (bf16[4,40,128]{2,1,0:T(8,128)(2,1)}, bf16[4,40,128]{2,1,0:T(8,128)(2,1)S(1)}, u32[]{:S(2)}, u32[]{:S(2)}) collective-permute-start(bf16[4,40,128]{2,1,0:T(8,128)(2,1)} %get-tuple-element.22), channel_id=1, source_target_pairs={{0,8},{1,9},{2,10},{3,11},{4,12},{5,13},{6,14},{7,15},{8,0},{9,1},... | collective-permute-start | bytes 122888 | tf_op jit(solution)/shard_map/ppermute | solution.py:403
  9.0 6.1 %collective-permute-start.1 = (bf16[4,40,128]{2,1,0:T(8,128)(2,1)}, bf16[4,40,128]{2,1,0:T(8,128)(2,1)S(1)}, u32[]{:S(2)}, u32[]{:S(2)}) collective-permute-start(bf16[4,40,128]{2,1,0:T(8,128)(2,1)} %get-tuple-element.23), channel_id=1, source_target_pairs={{0,8},{1,9},{2,10},{3,11},{4,12},{5,13},{6,14},{7,15},{8,0},{9,1},... | collective-permute-start | bytes 122888 | tf_op jit(solution)/shard_map/ppermute | solution.py:403
  11.6 5.5 %collective-permute-start.4 = (bf16[8,40,128]{2,1,0:T(8,128)(2,1)S(1)}, bf16[8,40,128]{2,1,0:T(8,128)(2,1)S(1)}, u32[]{:S(2)}, u32[]{:S(2)}) collective-permute-start(bf16[8,40,128]{2,1,0:T(8,128)(2,1)S(1)} %pad_maximum_fusion), channel_id=1, source_target_pairs={{0,6},{1,7},{2,4},{3,5},{4,2},{5,3},{6,0},{7,1},{8,14},{9,15},{10,... | collective-permute-start | bytes 245768 | tf_op jit(solution)/shard_map/ppermute | solution.py:403
  14.4 4.4 %collective-permute-start.3 = (bf16[8,40,128]{2,1,0:T(8,128)(2,1)S(1)}, bf16[8,40,128]{2,1,0:T(8,128)(2,1)S(1)}, u32[]{:S(2)}, u32[]{:S(2)}) collective-permute-start(bf16[8,40,128]{2,1,0:T(8,128)(2,1)S(1)} %pad_maximum_fusion), channel_id=1, source_target_pairs={{0,4},{1,5},{2,6},{3,7},{4,0},{5,1},{6,2},{7,3},{8,12},{9,13},{10,... | collective-permute-start | bytes 245768 | tf_op jit(solution)/shard_map/ppermute | solution.py:403
  14.6 4.4 %collective-permute-start.2 = (bf16[8,40,128]{2,1,0:T(8,128)(2,1)S(1)}, bf16[8,40,128]{2,1,0:T(8,128)(2,1)S(1)}, u32[]{:S(2)}, u32[]{:S(2)}) collective-permute-start(bf16[8,40,128]{2,1,0:T(8,128)(2,1)S(1)} %pad_maximum_fusion), channel_id=1, source_target_pairs={{0,2},{1,3},{2,0},{3,1},{4,6},{5,7},{6,4},{7,5},{8,10},{9,11},{10,... | collective-permute-start | bytes 245768 | tf_op jit(solution)/shard_map/ppermute | solution.py:403
  19.1 31.6 %copy-start.2 = (bf16[256,256]{1,0:T(8,128)(2,1)S(1)}, bf16[256,256]{1,0:T(8,128)(2,1)}, u32[]{:S(2)}) copy-start(bf16[256,256]{1,0:T(8,128)(2,1)} %constant.2.clone.plane_hbm) | copy-start | bytes 393220
  19.1 3.6 %collective-permute-start.8 = (bf16[32,40,128]{2,1,0:T(8,128)(2,1)S(1)}, bf16[32,40,128]{2,1,0:T(8,128)(2,1)S(1)}, u32[]{:S(2)}, u32[]{:S(2)}) collective-permute-start(bf16[32,40,128]{2,1,0:T(8,128)(2,1)S(1)} %constant_dynamic-update-slice_fusion.own), channel_id=1, source_target_pairs={{0,1},{1,0},{2,3},{3,2},{4,5},{5,4},{6,7},{7,6},{8,9},{9,8},{10,11... | collective-permute-start | bytes 983048 | tf_op jit(solution)/shard_map/ppermute | solution.py:403
  19.2 29.7 %collective-permute-start.7 = (bf16[8,40,128]{2,1,0:T(8,128)(2,1)S(1)}, bf16[8,40,128]{2,1,0:T(8,128)(2,1)S(1)}, u32[]{:S(2)}, u32[]{:S(2)}) collective-permute-start(bf16[8,40,128]{2,1,0:T(8,128)(2,1)S(1)} %pad_maximum_fusion.1), channel_id=1, source_target_pairs={{0,6},{1,7},{2,4},{3,5},{4,2},{5,3},{6,0},{7,1},{8,14},{9,15},{10,... | collective-permute-start | bytes 245768 | tf_op jit(solution)/shard_map/ppermute | solution.py:403
  21.1 27.8 %collective-permute-start.6 = (bf16[8,40,128]{2,1,0:T(8,128)(2,1)S(1)}, bf16[8,40,128]{2,1,0:T(8,128)(2,1)S(1)}, u32[]{:S(2)}, u32[]{:S(2)}) collective-permute-start(bf16[8,40,128]{2,1,0:T(8,128)(2,1)S(1)} %pad_maximum_fusion.1), channel_id=1, source_target_pairs={{0,4},{1,5},{2,6},{3,7},{4,0},{5,1},{6,2},{7,3},{8,12},{9,13},{10,... | collective-permute-start | bytes 245768 | tf_op jit(solution)/shard_map/ppermute | solution.py:403
  21.2 27.6 %collective-permute-start.5 = (bf16[8,40,128]{2,1,0:T(8,128)(2,1)S(1)}, bf16[8,40,128]{2,1,0:T(8,128)(2,1)S(1)}, u32[]{:S(2)}, u32[]{:S(2)}) collective-permute-start(bf16[8,40,128]{2,1,0:T(8,128)(2,1)S(1)} %pad_maximum_fusion.1), channel_id=1, source_target_pairs={{0,2},{1,3},{2,0},{3,1},{4,6},{5,7},{6,4},{7,5},{8,10},{9,11},{10,... | collective-permute-start | bytes 245768 | tf_op jit(solution)/shard_map/ppermute | solution.py:403
  22.7 0.9 %copy-start.1 = (bf16[256,256]{1,0:T(8,128)(2,1)S(1)}, bf16[256,256]{1,0:T(8,128)(2,1)}, u32[]{:S(2)}) copy-start(bf16[256,256]{1,0:T(8,128)(2,1)} %constant.2.clone.plane_hbm) | copy-start | bytes 393220
  49.0 1.7 %collective-permute-start.9 = (bf16[32,40,128]{2,1,0:T(8,128)(2,1)S(1)}, bf16[32,40,128]{2,1,0:T(8,128)(2,1)S(1)}, u32[]{:S(2)}, u32[]{:S(2)}) collective-permute-start(bf16[32,40,128]{2,1,0:T(8,128)(2,1)S(1)} %constant_dynamic-update-slice_fusion.4.own), channel_id=1, source_target_pairs={{0,1},{1,0},{2,3},{3,2},{4,5},{5,4},{6,7},{7,6},{8,9},{9,8},{10,11... | collective-permute-start | bytes 983048 | tf_op jit(solution)/shard_map/ppermute | solution.py:403
  49.0 25.8 %copy-start = (f32[2,8,128,128]{3,2,1,0:T(8,128)S(1)}, f32[2,8,128,128]{3,2,1,0:T(8,128)}, u32[]{:S(2)}) copy-start(f32[2,8,128,128]{3,2,1,0:T(8,128)} %get-tuple-element.31.first) | copy-start | bytes 3145732
  49.0 25.8 %collective-permute-start.10 = (bf16[2,8,128,128]{3,2,1,0:T(8,128)(2,1)S(1)}, bf16[2,8,128,128]{3,2,1,0:T(8,128)(2,1)S(1)}, u32[]{:S(2)}, u32[]{:S(2)}) collective-permute-start(bf16[2,8,128,128]{3,2,1,0:T(8,128)(2,1)S(1)} %get-tuple-element.36), channel_id=1, source_target_pairs={{0,16},{16,0},{1,17},{17,1},{2,18},{18,2},{3,19},{19,3},{4,20},{20... | collective-permute-start | bytes 1572872 | tf_op jit(solution)/shard_map/ppermute | solution.py:450

commit v5 on v4

--- a/solution.py
+++ b/solution.py
@@ -17,7 +17,8 @@
 EPS = 0.05
 LAMBDA_TV = 0.3
 TERMS = 40
-UNROLL = 8
+UNROLL = 16
+AHEAD = 16
 GROUPS = 16
 LAST_REFS = 16
 VMEM_LIMIT = 52 * 1024 * 1024
@@ -56,10 +57,10 @@
     return lax.rem(lax.axis_index("frame"), 2) == 0
 
 
-def pack_kernel(samples, density, fractions, shift, depth, corner, *packed):
+def pack_kernel(samples, density, fractions, shift, depth, corner, packed):
     frames, blocks, _, count = samples.shape
     last = frames - 1
-    for place, out in enumerate(packed):
+    for place in range(frames):
         frame = jnp.where(shared_first(), last - place, place)
         rows = [
             density[frame].astype(jnp.float32)[:, None],
@@ -73,18 +74,17 @@
                 for axis in range(2)
             ]
             parts = [samples[frame, block].astype(jnp.float32)] + [row[block] for row in rows] + ends
-            out[block] = jnp.concatenate(parts, axis=0).astype(jnp.bfloat16)
+            packed[place, block] = jnp.concatenate(parts, axis=0).astype(jnp.bfloat16)
 
 
 def pack_blocks(samples, density, fractions, shift, depth, corner):
     frames, blocks, channels, count = samples.shape
     whole = pl.BlockSpec(memory_space=pltpu.VMEM)
-    shape = jax.ShapeDtypeStruct((blocks, channels + META, count), jnp.bfloat16)
     return pl.pallas_call(
         pack_kernel,
-        out_shape=(shape,) * frames,
+        out_shape=jax.ShapeDtypeStruct((frames, blocks, channels + META, count), jnp.bfloat16),
         in_specs=[whole] * 5 + [pl.BlockSpec(memory_space=pltpu.SMEM)],
-        out_specs=(whole,) * frames,
+        out_specs=whole,
     )(samples, density, jnp.swapaxes(fractions, 1, 2), shift, depth, jnp.swapaxes(corner, 1, 2))
 
 
@@ -127,9 +127,16 @@
     position = lax.broadcasted_iota(jnp.int32, (YROWS, lanes), 1)
     image_y = lax.axis_index("tile") * slab + lax.broadcasted_iota(jnp.int32, (YROWS, lanes), 0)
     angles = lax.rem(position * image_y, grid_size).astype(jnp.float32) * (2.0 * math.pi / grid_size)
-    for table, phases in ((cos_rows, jnp.cos(angles)), (sin_rows, jnp.sin(angles))):
-        for k in range(grid_size + WIN):
-            table[k] = jnp.broadcast_to(phases[:, k : k + 1], (YROWS, samples))
+    phases = jnp.cos(angles), jnp.sin(angles)
+    stride = 16
+    turn, *chain = (
+        tuple(jnp.broadcast_to(phase[:, k : k + 1], (YROWS, samples)) for phase in phases)
+        for k in (stride, *range(stride))
+    )
+    for k in range(grid_size + WIN):
+        real, imag = chain[k % stride]
+        cos_rows[k], sin_rows[k] = real, imag
+        chain[k % stride] = real * turn[0] - imag * turn[1], real * turn[1] + imag * turn[0]
     planes.wait()
     tiles = plane_dft[:, :grid_size].astype(jnp.float32).reshape(grid_size // 8, 2, 8, grid_size)
     for part in range(2):
@@ -139,7 +146,8 @@
     table = depth_dft[...]
     taps = lax.broadcasted_iota(jnp.int32, (8, 2 * samples), 0).astype(jnp.float32)
     cells = lax.broadcasted_iota(jnp.int32, (grid_size, 2 * samples), 0).astype(jnp.bfloat16)
-    clear_rows = grid_real[0].shape[1] // (blocks // unroll)
+    ahead = math.gcd(blocks, AHEAD)
+    clear_rows = grid_real[0].shape[1] // (blocks // ahead)
 
     def prepare(source, offset, cleared):
         def two(first):
@@ -171,11 +179,11 @@
             for ref in cleared:
                 at = pl.ds(pl.multiple_of(index * clear_rows, 8), clear_rows)
                 ref[:, at, :] = jnp.zeros((ref.shape[0], clear_rows, grid_size), jnp.float32)
-            for part in range(0, unroll, 2):
-                two(index * unroll + part)
+            for part in range(0, ahead, 2):
+                two(index * ahead + part)
             return carry
 
-        lax.fori_loop(0, blocks // unroll, step, 0)
+        lax.fori_loop(0, blocks // ahead, step, 0)
 
     prepare(own, 0, grid_real)
     prepare(other, blocks, grid_imag)
@@ -403,10 +411,6 @@
     return lax.ppermute(values, axis, [(index, index ^ bit) for index in range(count)])
 
 
-def join_halves(held):
-    return jnp.concatenate([held, swap(held, "tile", lax.axis_size("tile") // 2)], axis=0)
-
-
 def chips(held):
     shifts = range(2, lax.axis_size("tile") // 2, 2)
     return [held] + [swap(held, "tile", shift) for shift in shifts]
@@ -430,10 +434,10 @@
         [(index, index - 1) for index in range(2, frame_count, 2)],
     ]
     pairs[1] += [(target, source) for source, target in pairs[1]]
-    shared, rest = packed
-    shared = join_halves(shared)
-    rest, shared = lax.optimization_barrier((rest, shared))
-    rest = join_halves(rest)
+    across = swap(packed, "tile", tile_count // 2)
+    shared, rest = (
+        jnp.concatenate([packed[place], across[place]], axis=0) for place in range(2)
+    )
     shared = chips(shared)
     rest, *shared = lax.optimization_barrier((rest, *shared))
     held = [jnp.concatenate(shared, axis=0), chips(rest)]

time: 76.7 us -> 73.2 us (0.954)
  starting transfers between devices: 15.3 us -> 12.9 us
  Pallas kernels: 52.5 us -> 50.1 us
  waiting for transfers between devices: 5.86 us -> 7.71 us
  other arithmetic: 1.58 us -> 0.02 us
  local copies, waits for them, and re-layouts: 1.03 us -> 1.85 us
    ppermute x10 -> x9, starting transfers between devices: 13.8 us -> 11.3 us  [swap(): lax.ppermute(values, axis, [(index, index ^ bit) for index in range(count)])]
    pallas_call x2, Pallas kernels: 49.4 us -> 47 us  [frame_image(): pl.pallas_call(functools.partial(frame_kernel, place=place, scale=scale),...]
    ppermute x10 -> x9, waiting for transfers between devices: 5.85 us -> 7.7 us  [swap(): lax.ppermute(values, axis, [(index, index ^ bit) for index in range(count)])]
    concatenate x2, other arithmetic: 1.58 us -> 0.02 us  [on_device(): jnp.concatenate([packed[place], across[place]], axis=0)]
    squeeze x0 -> x2, local copies, waits for them, and re-layouts: none -> 0.83 us  [the longest x1 0.82 us: on_device(): packed[place]]
  transfers between devices with their start and end apart: 11 -> 10, of which waited for: 5 -> 4; matrix products, arithmetic and copies ran while one was open for 1% -> 1% of each run, Pallas kernels for 65% -> 65%
where the time goes in v5:
time: 73.2 us; the launch traced here: 72.9 us
  Pallas kernels  50.1 us (68%)
  starting transfers between devices  12.9 us (18%)
  waiting for transfers between devices  7.71 us (11%)
  local copies, waits for them, and re-layouts  1.85 us (3%)
    pallas_call x2, Pallas kernels, frame_image(): pl.pallas_call(functools.partial(frame_kernel, place=place, scale=scale),...  47 us
    ppermute x9, starting transfers between devices, swap(): lax.ppermute(values, axis, [(index, index ^ bit) for index in range(count)])  11.3 us
    ppermute x9, waiting for transfers between devices, swap(): lax.ppermute(values, axis, [(index, index ^ bit) for index in range(count)])  7.7 us
    ppermute x1, starting transfers between devices, on_device(): lax.ppermute(small[0], 'frame', pairs[place])  1.63 us
    pallas_call x1, Pallas kernels, pack_blocks(): pl.pallas_call(pack_kernel, out_shape=jax.ShapeDtypeStruct((frames, block...  1.56 us
    pallas_call x1, Pallas kernels, tv_step(): pl.pallas_call(step_kernel, out_shape=jax.ShapeDtypeStruct(shape, jnp.flo...  1.5 us
  transfers between devices with their start and end apart: 10, of which 4 were waited for; matrix products, arithmetic and copies ran while one was open for 1% of the time, Pallas kernels for 65%

profile of v5, /device:TPU:0, one launch (start us, length us, event | category | flops | bytes accessed | tf_op | source)
XLA Modules:
  0.0 72.9 jit_solution(7476293516546635010)
XLA Ops:
  0.0 1.6 %shard_map.91 = bf16[2,4,40,128]{3,2,1,0:T(8,128)(2,1)} custom-call(bf16[2,4,32,128]{3,2,1,0:T(8,128)(2,1)} %samples.1, bf16[2,4,128]{2,1,0:T(4,128)(2,1)} %density.1, bf16[2,3,4,128]{3,2,1,0:T(4,128)(2,1)} %bitcast.10, s32[2,4,128]{2,1,0:T(4,128)} %shift.1, s32[2,4,128]{2,1,0:T(4,128)} %depth.1, s32[2,2,4]{2,1,0:T(2,128)} %bitcast.11), custom_call_target="tpu_custom_call" | custom-call | tf_op jit(solution)/shard_map/pallas_call | solution.py:83
  1.6 4.0 %collective-permute-start = (bf16[2,4,40,128]{3,2,1,0:T(8,128)(2,1)}, bf16[2,4,40,128]{3,2,1,0:T(8,128)(2,1)S(1)}, u32[]{:S(2)}, u32[]{:S(2)}) collective-permute-start(bf16[2,4,40,128]{3,2,1,0:T(8,128)(2,1)} %shard_map.91), channel_id=1, source_target_pairs={{0,8},{1,9},{2,10},{3,11},{4,12},{5,13},{6,14},{7,15},{8,0},{9,1},... | collective-permute-start | bytes 245768 | tf_op jit(solution)/shard_map/ppermute | solution.py:411
  5.6 0.8 %slice_bitcast_fusion.1 = (bf16[4,40,128]{2,1,0:T(8,128)(2,1)S(1)}, bf16[4,40,128]{2,1,0:T(8,128)(2,1)S(1)}) fusion(bf16[2,4,40,128]{3,2,1,0:T(8,128)(2,1)} %shard_map.91), kind=kLoop, calls=%fused_computation.3 | loop fusion | bytes 163840 | tf_op jit(solution)/shard_map/squeeze | solution.py:439
  6.4 3.6 %collective-permute-done = bf16[2,4,40,128]{3,2,1,0:T(8,128)(2,1)S(1)} collective-permute-done((bf16[2,4,40,128]{3,2,1,0:T(8,128)(2,1)}, bf16[2,4,40,128]{3,2,1,0:T(8,128)(2,1)S(1)}, u32[]{:S(2)}, u32[]{:S(2)}) %collective-permute-start) | collective-permute-done | bytes 81952 | tf_op jit(solution)/shard_map/ppermute | solution.py:411
  10.0 1.8 %collective-permute-start.3 = (bf16[8,40,128]{2,1,0:T(8,128)(2,1)S(1)}, bf16[8,40,128]{2,1,0:T(8,128)(2,1)S(1)}, u32[]{:S(2)}, u32[]{:S(2)}) collective-permute-start(bf16[8,40,128]{2,1,0:T(8,128)(2,1)S(1)} %pad_maximum_fusion.1), channel_id=1, source_target_pairs={{0,6},{1,7},{2,4},{3,5},{4,2},{5,3},{6,0},{7,1},{8,14},{9,15},{10,... | collective-permute-start | bytes 245768 | tf_op jit(solution)/shard_map/ppermute | solution.py:411
  11.9 1.4 %collective-permute-start.2 = (bf16[8,40,128]{2,1,0:T(8,128)(2,1)S(1)}, bf16[8,40,128]{2,1,0:T(8,128)(2,1)S(1)}, u32[]{:S(2)}, u32[]{:S(2)}) collective-permute-start(bf16[8,40,128]{2,1,0:T(8,128)(2,1)S(1)} %pad_maximum_fusion.1), channel_id=1, source_target_pairs={{0,4},{1,5},{2,6},{3,7},{4,0},{5,1},{6,2},{7,3},{8,12},{9,13},{10,... | collective-permute-start | bytes 245768 | tf_op jit(solution)/shard_map/ppermute | solution.py:411
  13.3 0.3 collective-permute-start.1
  13.6 2.2 %collective-permute-done.3 = bf16[8,40,128]{2,1,0:T(8,128)(2,1)S(1)} collective-permute-done((bf16[8,40,128]{2,1,0:T(8,128)(2,1)S(1)}, bf16[8,40,128]{2,1,0:T(8,128)(2,1)S(1)}, u32[]{:S(2)}, u32[]{:S(2)}) %collective-permute-start.3) | collective-permute-done | bytes 81952 | tf_op jit(solution)/shard_map/ppermute | solution.py:411
  15.8 0.9 %collective-permute-done.2 = bf16[8,40,128]{2,1,0:T(8,128)(2,1)S(1)} collective-permute-done((bf16[8,40,128]{2,1,0:T(8,128)(2,1)S(1)}, bf16[8,40,128]{2,1,0:T(8,128)(2,1)S(1)}, u32[]{:S(2)}, u32[]{:S(2)}) %collective-permute-start.2) | collective-permute-done | bytes 81952 | tf_op jit(solution)/shard_map/ppermute | solution.py:411
  16.7 1.0 %collective-permute-done.1 = bf16[8,40,128]{2,1,0:T(8,128)(2,1)S(1)} collective-permute-done((bf16[8,40,128]{2,1,0:T(8,128)(2,1)S(1)}, bf16[8,40,128]{2,1,0:T(8,128)(2,1)S(1)}, u32[]{:S(2)}, u32[]{:S(2)}) %collective-permute-start.1) | collective-permute-done | bytes 81952 | tf_op jit(solution)/shard_map/ppermute | solution.py:411
  17.8 0.0 copy-start.2
  17.8 0.1 collective-permute-start.7
  17.9 1.1 %collective-permute-start.6 = (bf16[8,40,128]{2,1,0:T(8,128)(2,1)S(1)}, bf16[8,40,128]{2,1,0:T(8,128)(2,1)S(1)}, u32[]{:S(2)}, u32[]{:S(2)}) collective-permute-start(bf16[8,40,128]{2,1,0:T(8,128)(2,1)S(1)} %pad_maximum_fusion), channel_id=1, source_target_pairs={{0,6},{1,7},{2,4},{3,5},{4,2},{5,3},{6,0},{7,1},{8,14},{9,15},{10,... | collective-permute-start | bytes 245768 | tf_op jit(solution)/shard_map/ppermute | solution.py:411
  19.0 0.9 %collective-permute-start.5 = (bf16[8,40,128]{2,1,0:T(8,128)(2,1)S(1)}, bf16[8,40,128]{2,1,0:T(8,128)(2,1)S(1)}, u32[]{:S(2)}, u32[]{:S(2)}) collective-permute-start(bf16[8,40,128]{2,1,0:T(8,128)(2,1)S(1)} %pad_maximum_fusion), channel_id=1, source_target_pairs={{0,4},{1,5},{2,6},{3,7},{4,0},{5,1},{6,2},{7,3},{8,12},{9,13},{10,... | collective-permute-start | bytes 245768 | tf_op jit(solution)/shard_map/ppermute | solution.py:411
  19.9 1.6 %collective-permute-start.4 = (bf16[8,40,128]{2,1,0:T(8,128)(2,1)S(1)}, bf16[8,40,128]{2,1,0:T(8,128)(2,1)S(1)}, u32[]{:S(2)}, u32[]{:S(2)}) collective-permute-start(bf16[8,40,128]{2,1,0:T(8,128)(2,1)S(1)} %pad_maximum_fusion), channel_id=1, source_target_pairs={{0,2},{1,3},{2,0},{3,1},{4,6},{5,7},{6,4},{7,5},{8,10},{9,11},{10,... | collective-permute-start | bytes 245768 | tf_op jit(solution)/shard_map/ppermute | solution.py:411
  21.4 0.9 %copy-done.1 = bf16[256,256]{1,0:T(8,128)(2,1)S(1)} copy-done((bf16[256,256]{1,0:T(8,128)(2,1)S(1)}, bf16[256,256]{1,0:T(8,128)(2,1)}, u32[]{:S(2)}) %copy-start.1) | copy-done | bytes 131096
  22.4 23.9 %shard_map.92 = (f32[2,8,128,128]{3,2,1,0:T(8,128)}, bf16[2,8,128,128]{3,2,1,0:T(8,128)(2,1)S(1)}) custom-call(bf16[32,40,128]{2,1,0:T(8,128)(2,1)S(1)} %constant_dynamic-update-slice_fusion.own, bf16[32,40,128]{2,1,0:T(8,128)(2,1)S(1)} %collective-permute-done.7.other, bf16[256,256]{1,0:T(8,128)(2,1)S(1)} %copy-done.1, ...), custom_call_target="tpu_custom_call" | custom-call | flops 6442450944 | bytes 8388608 | tf_op jit(solution)/shard_map/pallas_call | solution.py:328
  46.3 0.0 collective-permute-done.6
  46.3 0.0 collective-permute-done.4
  46.4 0.1 collective-permute-start.8
  46.5 0.0 copy-start
  46.5 1.6 %collective-permute-start.9 = (bf16[2,8,128,128]{3,2,1,0:T(8,128)(2,1)S(1)}, bf16[2,8,128,128]{3,2,1,0:T(8,128)(2,1)S(1)}, u32[]{:S(2)}, u32[]{:S(2)}) collective-permute-start(bf16[2,8,128,128]{3,2,1,0:T(8,128)(2,1)S(1)} %get-tuple-element.28), channel_id=1, source_target_pairs={{0,16},{16,0},{1,17},{17,1},{2,18},{18,2},{3,19},{19,3},{4,20},{20... | collective-permute-start | bytes 1572872 | tf_op jit(solution)/shard_map/ppermute | solution.py:454
  48.1 23.1 %shard_map.93.second = f32[2,8,128,128]{3,2,1,0:T(8,128)S(1)} custom-call(bf16[32,40,128]{2,1,0:T(8,128)(2,1)S(1)} %constant_dynamic-update-slice_fusion.4.own, bf16[32,40,128]{2,1,0:T(8,128)(2,1)S(1)} %collective-permute-done.8.other, bf16[256,256]{1,0:T(8,128)(2,1)S(1)} %copy-done.2, bf16[16,2,8,128,128]{4,3,2,1,0:T(8,128)(2,1)} %maps_hbm.3, ...), custom_call_target="tpu_custom_call" | custom-call | flops 6442450944 | bytes 8388608 | tf_op jit(solution)/shard_map/pallas_call | solution.py:328
  71.3 1.5 %shard_map.94 = f32[2,2,8,128,128]{4,3,2,1,0:T(8,128)} custom-call(f32[2,8,128,128]{3,2,1,0:T(8,128)S(1)} %copy-done, f32[2,8,128,128]{3,2,1,0:T(8,128)S(1)} %shard_map.93.second, bf16[2,8,128,128]{3,2,1,0:T(8,128)(2,1)S(1)} %collective-permute-done.9.rest_0_), custom_call_target="tpu_custom_call" | custom-call | tf_op jit(solution)/shard_map/pallas_call | solution.py:396
  (18 shorter events, 0.2 us)
Async XLA Ops:
  1.6 8.4 %collective-permute-start = (bf16[2,4,40,128]{3,2,1,0:T(8,128)(2,1)}, bf16[2,4,40,128]{3,2,1,0:T(8,128)(2,1)S(1)}, u32[]{:S(2)}, u32[]{:S(2)}) collective-permute-start(bf16[2,4,40,128]{3,2,1,0:T(8,128)(2,1)} %shard_map.91), channel_id=1, source_target_pairs={{0,8},{1,9},{2,10},{3,11},{4,12},{5,13},{6,14},{7,15},{8,0},{9,1},... | collective-permute-start | bytes 245768 | tf_op jit(solution)/shard_map/ppermute | solution.py:411
  10.0 5.8 %collective-permute-start.3 = (bf16[8,40,128]{2,1,0:T(8,128)(2,1)S(1)}, bf16[8,40,128]{2,1,0:T(8,128)(2,1)S(1)}, u32[]{:S(2)}, u32[]{:S(2)}) collective-permute-start(bf16[8,40,128]{2,1,0:T(8,128)(2,1)S(1)} %pad_maximum_fusion.1), channel_id=1, source_target_pairs={{0,6},{1,7},{2,4},{3,5},{4,2},{5,3},{6,0},{7,1},{8,14},{9,15},{10,... | collective-permute-start | bytes 245768 | tf_op jit(solution)/shard_map/ppermute | solution.py:411
  11.9 4.8 %collective-permute-start.2 = (bf16[8,40,128]{2,1,0:T(8,128)(2,1)S(1)}, bf16[8,40,128]{2,1,0:T(8,128)(2,1)S(1)}, u32[]{:S(2)}, u32[]{:S(2)}) collective-permute-start(bf16[8,40,128]{2,1,0:T(8,128)(2,1)S(1)} %pad_maximum_fusion.1), channel_id=1, source_target_pairs={{0,4},{1,5},{2,6},{3,7},{4,0},{5,1},{6,2},{7,3},{8,12},{9,13},{10,... | collective-permute-start | bytes 245768 | tf_op jit(solution)/shard_map/ppermute | solution.py:411
  13.3 4.4 %collective-permute-start.1 = (bf16[8,40,128]{2,1,0:T(8,128)(2,1)S(1)}, bf16[8,40,128]{2,1,0:T(8,128)(2,1)S(1)}, u32[]{:S(2)}, u32[]{:S(2)}) collective-permute-start(bf16[8,40,128]{2,1,0:T(8,128)(2,1)S(1)} %pad_maximum_fusion.1), channel_id=1, source_target_pairs={{0,2},{1,3},{2,0},{3,1},{4,6},{5,7},{6,4},{7,5},{8,10},{9,11},{10,... | collective-permute-start | bytes 245768 | tf_op jit(solution)/shard_map/ppermute | solution.py:411
  17.8 30.4 %copy-start.2 = (bf16[256,256]{1,0:T(8,128)(2,1)S(1)}, bf16[256,256]{1,0:T(8,128)(2,1)}, u32[]{:S(2)}) copy-start(bf16[256,256]{1,0:T(8,128)(2,1)} %constant.2.clone.plane_hbm) | copy-start | bytes 393220
  17.8 3.6 %collective-permute-start.7 = (bf16[32,40,128]{2,1,0:T(8,128)(2,1)S(1)}, bf16[32,40,128]{2,1,0:T(8,128)(2,1)S(1)}, u32[]{:S(2)}, u32[]{:S(2)}) collective-permute-start(bf16[32,40,128]{2,1,0:T(8,128)(2,1)S(1)} %constant_dynamic-update-slice_fusion.own), channel_id=1, source_target_pairs={{0,1},{1,0},{2,3},{3,2},{4,5},{5,4},{6,7},{7,6},{8,9},{9,8},{10,11... | collective-permute-start | bytes 983048 | tf_op jit(solution)/shard_map/ppermute | solution.py:411
  17.9 28.4 %collective-permute-start.6 = (bf16[8,40,128]{2,1,0:T(8,128)(2,1)S(1)}, bf16[8,40,128]{2,1,0:T(8,128)(2,1)S(1)}, u32[]{:S(2)}, u32[]{:S(2)}) collective-permute-start(bf16[8,40,128]{2,1,0:T(8,128)(2,1)S(1)} %pad_maximum_fusion), channel_id=1, source_target_pairs={{0,6},{1,7},{2,4},{3,5},{4,2},{5,3},{6,0},{7,1},{8,14},{9,15},{10,... | collective-permute-start | bytes 245768 | tf_op jit(solution)/shard_map/ppermute | solution.py:411
  19.0 27.3 %collective-permute-start.5 = (bf16[8,40,128]{2,1,0:T(8,128)(2,1)S(1)}, bf16[8,40,128]{2,1,0:T(8,128)(2,1)S(1)}, u32[]{:S(2)}, u32[]{:S(2)}) collective-permute-start(bf16[8,40,128]{2,1,0:T(8,128)(2,1)S(1)} %pad_maximum_fusion), channel_id=1, source_target_pairs={{0,4},{1,5},{2,6},{3,7},{4,0},{5,1},{6,2},{7,3},{8,12},{9,13},{10,... | collective-permute-start | bytes 245768 | tf_op jit(solution)/shard_map/ppermute | solution.py:411
  19.9 26.5 %collective-permute-start.4 = (bf16[8,40,128]{2,1,0:T(8,128)(2,1)S(1)}, bf16[8,40,128]{2,1,0:T(8,128)(2,1)S(1)}, u32[]{:S(2)}, u32[]{:S(2)}) collective-permute-start(bf16[8,40,128]{2,1,0:T(8,128)(2,1)S(1)} %pad_maximum_fusion), channel_id=1, source_target_pairs={{0,2},{1,3},{2,0},{3,1},{4,6},{5,7},{6,4},{7,5},{8,10},{9,11},{10,... | collective-permute-start | bytes 245768 | tf_op jit(solution)/shard_map/ppermute | solution.py:411
  21.4 0.9 %copy-start.1 = (bf16[256,256]{1,0:T(8,128)(2,1)S(1)}, bf16[256,256]{1,0:T(8,128)(2,1)}, u32[]{:S(2)}) copy-start(bf16[256,256]{1,0:T(8,128)(2,1)} %constant.2.clone.plane_hbm) | copy-start | bytes 393220
  46.4 1.7 %collective-permute-start.8 = (bf16[32,40,128]{2,1,0:T(8,128)(2,1)S(1)}, bf16[32,40,128]{2,1,0:T(8,128)(2,1)S(1)}, u32[]{:S(2)}, u32[]{:S(2)}) collective-permute-start(bf16[32,40,128]{2,1,0:T(8,128)(2,1)S(1)} %constant_dynamic-update-slice_fusion.4.own), channel_id=1, source_target_pairs={{0,1},{1,0},{2,3},{3,2},{4,5},{5,4},{6,7},{7,6},{8,9},{9,8},{10,11... | collective-permute-start | bytes 983048 | tf_op jit(solution)/shard_map/ppermute | solution.py:411
  46.5 24.8 %copy-start = (f32[2,8,128,128]{3,2,1,0:T(8,128)S(1)}, f32[2,8,128,128]{3,2,1,0:T(8,128)}, u32[]{:S(2)}) copy-start(f32[2,8,128,128]{3,2,1,0:T(8,128)} %get-tuple-element.23.first) | copy-start | bytes 3145732
  46.5 24.8 %collective-permute-start.9 = (bf16[2,8,128,128]{3,2,1,0:T(8,128)(2,1)S(1)}, bf16[2,8,128,128]{3,2,1,0:T(8,128)(2,1)S(1)}, u32[]{:S(2)}, u32[]{:S(2)}) collective-permute-start(bf16[2,8,128,128]{3,2,1,0:T(8,128)(2,1)S(1)} %get-tuple-element.28), channel_id=1, source_target_pairs={{0,16},{16,0},{1,17},{17,1},{2,18},{18,2},{3,19},{19,3},{4,20},{20... | collective-permute-start | bytes 1572872 | tf_op jit(solution)/shard_map/ppermute | solution.py:454

commit v6 on v5

--- a/solution.py
+++ b/solution.py
@@ -313,7 +313,7 @@
                             half_small[part, row, at] = value.astype(jnp.bfloat16)
         return carry
 
-    lax.fori_loop(0, slab, image_row, 0)
+    lax.fori_loop(0, slab, image_row, 0, unroll=2)
 
 
 def frame_image(own, other, plane_dft, coil_maps, estimate, scale, place, shared):

time: 73.2 us -> 72 us (0.984)
  Pallas kernels: 50.1 us -> 48.9 us
    pallas_call x2, Pallas kernels: 47 us -> 45.8 us  [frame_image(): pl.pallas_call(functools.partial(frame_kernel, place=place, scale=scale),...]
  transfers between devices with their start and end apart: 10 -> 10, of which waited for: 4 -> 4; matrix products, arithmetic and copies ran while one was open for 1% -> 1% of each run, Pallas kernels for 65% -> 64%
where the time goes in v6:
time: 72 us; the launch traced here: 71.8 us
  Pallas kernels  48.9 us (68%)
  starting transfers between devices  13 us (18%)
  waiting for transfers between devices  7.71 us (11%)
  local copies, waits for them, and re-layouts  1.85 us (3%)
    pallas_call x2, Pallas kernels, frame_image(): pl.pallas_call(functools.partial(frame_kernel, place=place, scale=scale),...  45.8 us
    ppermute x9, starting transfers between devices, swap(): lax.ppermute(values, axis, [(index, index ^ bit) for index in range(count)])  11.3 us
    ppermute x9, waiting for transfers between devices, swap(): lax.ppermute(values, axis, [(index, index ^ bit) for index in range(count)])  7.7 us
    ppermute x1, starting transfers between devices, on_device(): lax.ppermute(small[0], 'frame', pairs[place])  1.68 us
    pallas_call x1, Pallas kernels, pack_blocks(): pl.pallas_call(pack_kernel, out_shape=jax.ShapeDtypeStruct((frames, block...  1.56 us
    pallas_call x1, Pallas kernels, tv_step(): pl.pallas_call(step_kernel, out_shape=jax.ShapeDtypeStruct(shape, jnp.flo...  1.5 us
  transfers between devices with their start and end apart: 10, of which 4 were waited for; matrix products, arithmetic and copies ran while one was open for 1% of the time, Pallas kernels for 64%

profile of v6, /device:TPU:0, one launch (start us, length us, event | category | flops | bytes accessed | tf_op | source)
XLA Modules:
  0.0 71.8 jit_solution(15274548830880791044)
XLA Ops:
  0.0 1.6 %shard_map.91 = bf16[2,4,40,128]{3,2,1,0:T(8,128)(2,1)} custom-call(bf16[2,4,32,128]{3,2,1,0:T(8,128)(2,1)} %samples.1, bf16[2,4,128]{2,1,0:T(4,128)(2,1)} %density.1, bf16[2,3,4,128]{3,2,1,0:T(4,128)(2,1)} %bitcast.10, s32[2,4,128]{2,1,0:T(4,128)} %shift.1, s32[2,4,128]{2,1,0:T(4,128)} %depth.1, s32[2,2,4]{2,1,0:T(2,128)} %bitcast.11), custom_call_target="tpu_custom_call" | custom-call | tf_op jit(solution)/shard_map/pallas_call | solution.py:83
  1.6 4.0 %collective-permute-start = (bf16[2,4,40,128]{3,2,1,0:T(8,128)(2,1)}, bf16[2,4,40,128]{3,2,1,0:T(8,128)(2,1)S(1)}, u32[]{:S(2)}, u32[]{:S(2)}) collective-permute-start(bf16[2,4,40,128]{3,2,1,0:T(8,128)(2,1)} %shard_map.91), channel_id=1, source_target_pairs={{0,8},{1,9},{2,10},{3,11},{4,12},{5,13},{6,14},{7,15},{8,0},{9,1},... | collective-permute-start | bytes 245768 | tf_op jit(solution)/shard_map/ppermute | solution.py:411
  5.6 0.8 %slice_bitcast_fusion.1 = (bf16[4,40,128]{2,1,0:T(8,128)(2,1)S(1)}, bf16[4,40,128]{2,1,0:T(8,128)(2,1)S(1)}) fusion(bf16[2,4,40,128]{3,2,1,0:T(8,128)(2,1)} %shard_map.91), kind=kLoop, calls=%fused_computation.3 | loop fusion | bytes 163840 | tf_op jit(solution)/shard_map/squeeze | solution.py:439
  6.4 3.6 %collective-permute-done = bf16[2,4,40,128]{3,2,1,0:T(8,128)(2,1)S(1)} collective-permute-done((bf16[2,4,40,128]{3,2,1,0:T(8,128)(2,1)}, bf16[2,4,40,128]{3,2,1,0:T(8,128)(2,1)S(1)}, u32[]{:S(2)}, u32[]{:S(2)}) %collective-permute-start) | collective-permute-done | bytes 81952 | tf_op jit(solution)/shard_map/ppermute | solution.py:411
  10.0 1.8 %collective-permute-start.3 = (bf16[8,40,128]{2,1,0:T(8,128)(2,1)S(1)}, bf16[8,40,128]{2,1,0:T(8,128)(2,1)S(1)}, u32[]{:S(2)}, u32[]{:S(2)}) collective-permute-start(bf16[8,40,128]{2,1,0:T(8,128)(2,1)S(1)} %pad_maximum_fusion.1), channel_id=1, source_target_pairs={{0,6},{1,7},{2,4},{3,5},{4,2},{5,3},{6,0},{7,1},{8,14},{9,15},{10,... | collective-permute-start | bytes 245768 | tf_op jit(solution)/shard_map/ppermute | solution.py:411
  11.9 1.4 %collective-permute-start.2 = (bf16[8,40,128]{2,1,0:T(8,128)(2,1)S(1)}, bf16[8,40,128]{2,1,0:T(8,128)(2,1)S(1)}, u32[]{:S(2)}, u32[]{:S(2)}) collective-permute-start(bf16[8,40,128]{2,1,0:T(8,128)(2,1)S(1)} %pad_maximum_fusion.1), channel_id=1, source_target_pairs={{0,4},{1,5},{2,6},{3,7},{4,0},{5,1},{6,2},{7,3},{8,12},{9,13},{10,... | collective-permute-start | bytes 245768 | tf_op jit(solution)/shard_map/ppermute | solution.py:411
  13.3 0.3 collective-permute-start.1
  13.6 2.2 %collective-permute-done.3 = bf16[8,40,128]{2,1,0:T(8,128)(2,1)S(1)} collective-permute-done((bf16[8,40,128]{2,1,0:T(8,128)(2,1)S(1)}, bf16[8,40,128]{2,1,0:T(8,128)(2,1)S(1)}, u32[]{:S(2)}, u32[]{:S(2)}) %collective-permute-start.3) | collective-permute-done | bytes 81952 | tf_op jit(solution)/shard_map/ppermute | solution.py:411
  15.8 0.9 %collective-permute-done.2 = bf16[8,40,128]{2,1,0:T(8,128)(2,1)S(1)} collective-permute-done((bf16[8,40,128]{2,1,0:T(8,128)(2,1)S(1)}, bf16[8,40,128]{2,1,0:T(8,128)(2,1)S(1)}, u32[]{:S(2)}, u32[]{:S(2)}) %collective-permute-start.2) | collective-permute-done | bytes 81952 | tf_op jit(solution)/shard_map/ppermute | solution.py:411
  16.7 1.0 %collective-permute-done.1 = bf16[8,40,128]{2,1,0:T(8,128)(2,1)S(1)} collective-permute-done((bf16[8,40,128]{2,1,0:T(8,128)(2,1)S(1)}, bf16[8,40,128]{2,1,0:T(8,128)(2,1)S(1)}, u32[]{:S(2)}, u32[]{:S(2)}) %collective-permute-start.1) | collective-permute-done | bytes 81952 | tf_op jit(solution)/shard_map/ppermute | solution.py:411
  17.8 0.0 copy-start.2
  17.8 0.1 collective-permute-start.7
  17.9 1.1 %collective-permute-start.6 = (bf16[8,40,128]{2,1,0:T(8,128)(2,1)S(1)}, bf16[8,40,128]{2,1,0:T(8,128)(2,1)S(1)}, u32[]{:S(2)}, u32[]{:S(2)}) collective-permute-start(bf16[8,40,128]{2,1,0:T(8,128)(2,1)S(1)} %pad_maximum_fusion), channel_id=1, source_target_pairs={{0,6},{1,7},{2,4},{3,5},{4,2},{5,3},{6,0},{7,1},{8,14},{9,15},{10,... | collective-permute-start | bytes 245768 | tf_op jit(solution)/shard_map/ppermute | solution.py:411
  19.0 0.9 %collective-permute-start.5 = (bf16[8,40,128]{2,1,0:T(8,128)(2,1)S(1)}, bf16[8,40,128]{2,1,0:T(8,128)(2,1)S(1)}, u32[]{:S(2)}, u32[]{:S(2)}) collective-permute-start(bf16[8,40,128]{2,1,0:T(8,128)(2,1)S(1)} %pad_maximum_fusion), channel_id=1, source_target_pairs={{0,4},{1,5},{2,6},{3,7},{4,0},{5,1},{6,2},{7,3},{8,12},{9,13},{10,... | collective-permute-start | bytes 245768 | tf_op jit(solution)/shard_map/ppermute | solution.py:411
  19.9 1.6 %collective-permute-start.4 = (bf16[8,40,128]{2,1,0:T(8,128)(2,1)S(1)}, bf16[8,40,128]{2,1,0:T(8,128)(2,1)S(1)}, u32[]{:S(2)}, u32[]{:S(2)}) collective-permute-start(bf16[8,40,128]{2,1,0:T(8,128)(2,1)S(1)} %pad_maximum_fusion), channel_id=1, source_target_pairs={{0,2},{1,3},{2,0},{3,1},{4,6},{5,7},{6,4},{7,5},{8,10},{9,11},{10,... | collective-permute-start | bytes 245768 | tf_op jit(solution)/shard_map/ppermute | solution.py:411
  21.4 0.0 collective-permute-done.7.other
  21.4 0.9 %copy-done.1 = bf16[256,256]{1,0:T(8,128)(2,1)S(1)} copy-done((bf16[256,256]{1,0:T(8,128)(2,1)S(1)}, bf16[256,256]{1,0:T(8,128)(2,1)}, u32[]{:S(2)}) %copy-start.1) | copy-done | bytes 131096
  22.4 23.2 %shard_map.92 = (f32[2,8,128,128]{3,2,1,0:T(8,128)}, bf16[2,8,128,128]{3,2,1,0:T(8,128)(2,1)S(1)}) custom-call(bf16[32,40,128]{2,1,0:T(8,128)(2,1)S(1)} %constant_dynamic-update-slice_fusion.own, bf16[32,40,128]{2,1,0:T(8,128)(2,1)S(1)} %collective-permute-done.7.other, bf16[256,256]{1,0:T(8,128)(2,1)S(1)} %copy-done.1, ...), custom_call_target="tpu_custom_call" | custom-call | flops 6442450944 | bytes 8388608 | tf_op jit(solution)/shard_map/pallas_call | solution.py:328
  45.6 0.0 collective-permute-done.6
  45.7 0.1 collective-permute-start.8
  45.8 0.0 copy-start
  45.8 1.7 %collective-permute-start.9 = (bf16[2,8,128,128]{3,2,1,0:T(8,128)(2,1)S(1)}, bf16[2,8,128,128]{3,2,1,0:T(8,128)(2,1)S(1)}, u32[]{:S(2)}, u32[]{:S(2)}) collective-permute-start(bf16[2,8,128,128]{3,2,1,0:T(8,128)(2,1)S(1)} %get-tuple-element.28), channel_id=1, source_target_pairs={{0,16},{16,0},{1,17},{17,1},{2,18},{18,2},{3,19},{19,3},{4,20},{20... | collective-permute-start | bytes 1572872 | tf_op jit(solution)/shard_map/ppermute | solution.py:454
  47.5 22.6 %shard_map.93.second = f32[2,8,128,128]{3,2,1,0:T(8,128)S(1)} custom-call(bf16[32,40,128]{2,1,0:T(8,128)(2,1)S(1)} %constant_dynamic-update-slice_fusion.4.own, bf16[32,40,128]{2,1,0:T(8,128)(2,1)S(1)} %collective-permute-done.8.other, bf16[256,256]{1,0:T(8,128)(2,1)S(1)} %copy-done.2, bf16[16,2,8,128,128]{4,3,2,1,0:T(8,128)(2,1)} %maps_hbm.3, ...), custom_call_target="tpu_custom_call" | custom-call | flops 6442450944 | bytes 8388608 | tf_op jit(solution)/shard_map/pallas_call | solution.py:328
  70.1 1.5 %shard_map.94 = f32[2,2,8,128,128]{4,3,2,1,0:T(8,128)} custom-call(f32[2,8,128,128]{3,2,1,0:T(8,128)S(1)} %copy-done, f32[2,8,128,128]{3,2,1,0:T(8,128)S(1)} %shard_map.93.second, bf16[2,8,128,128]{3,2,1,0:T(8,128)(2,1)S(1)} %collective-permute-done.9.rest_0_), custom_call_target="tpu_custom_call" | custom-call | tf_op jit(solution)/shard_map/pallas_call | solution.py:396
  (18 shorter events, 0.2 us)
Async XLA Ops:
  1.6 8.4 %collective-permute-start = (bf16[2,4,40,128]{3,2,1,0:T(8,128)(2,1)}, bf16[2,4,40,128]{3,2,1,0:T(8,128)(2,1)S(1)}, u32[]{:S(2)}, u32[]{:S(2)}) collective-permute-start(bf16[2,4,40,128]{3,2,1,0:T(8,128)(2,1)} %shard_map.91), channel_id=1, source_target_pairs={{0,8},{1,9},{2,10},{3,11},{4,12},{5,13},{6,14},{7,15},{8,0},{9,1},... | collective-permute-start | bytes 245768 | tf_op jit(solution)/shard_map/ppermute | solution.py:411
  10.0 5.8 %collective-permute-start.3 = (bf16[8,40,128]{2,1,0:T(8,128)(2,1)S(1)}, bf16[8,40,128]{2,1,0:T(8,128)(2,1)S(1)}, u32[]{:S(2)}, u32[]{:S(2)}) collective-permute-start(bf16[8,40,128]{2,1,0:T(8,128)(2,1)S(1)} %pad_maximum_fusion.1), channel_id=1, source_target_pairs={{0,6},{1,7},{2,4},{3,5},{4,2},{5,3},{6,0},{7,1},{8,14},{9,15},{10,... | collective-permute-start | bytes 245768 | tf_op jit(solution)/shard_map/ppermute | solution.py:411
  11.9 4.8 %collective-permute-start.2 = (bf16[8,40,128]{2,1,0:T(8,128)(2,1)S(1)}, bf16[8,40,128]{2,1,0:T(8,128)(2,1)S(1)}, u32[]{:S(2)}, u32[]{:S(2)}) collective-permute-start(bf16[8,40,128]{2,1,0:T(8,128)(2,1)S(1)} %pad_maximum_fusion.1), channel_id=1, source_target_pairs={{0,4},{1,5},{2,6},{3,7},{4,0},{5,1},{6,2},{7,3},{8,12},{9,13},{10,... | collective-permute-start | bytes 245768 | tf_op jit(solution)/shard_map/ppermute | solution.py:411
  13.3 4.4 %collective-permute-start.1 = (bf16[8,40,128]{2,1,0:T(8,128)(2,1)S(1)}, bf16[8,40,128]{2,1,0:T(8,128)(2,1)S(1)}, u32[]{:S(2)}, u32[]{:S(2)}) collective-permute-start(bf16[8,40,128]{2,1,0:T(8,128)(2,1)S(1)} %pad_maximum_fusion.1), channel_id=1, source_target_pairs={{0,2},{1,3},{2,0},{3,1},{4,6},{5,7},{6,4},{7,5},{8,10},{9,11},{10,... | collective-permute-start | bytes 245768 | tf_op jit(solution)/shard_map/ppermute | solution.py:411
  17.8 29.7 %copy-start.2 = (bf16[256,256]{1,0:T(8,128)(2,1)S(1)}, bf16[256,256]{1,0:T(8,128)(2,1)}, u32[]{:S(2)}) copy-start(bf16[256,256]{1,0:T(8,128)(2,1)} %constant.2.clone.plane_hbm) | copy-start | bytes 393220
  17.8 3.6 %collective-permute-start.7 = (bf16[32,40,128]{2,1,0:T(8,128)(2,1)S(1)}, bf16[32,40,128]{2,1,0:T(8,128)(2,1)S(1)}, u32[]{:S(2)}, u32[]{:S(2)}) collective-permute-start(bf16[32,40,128]{2,1,0:T(8,128)(2,1)S(1)} %constant_dynamic-update-slice_fusion.own), channel_id=1, source_target_pairs={{0,1},{1,0},{2,3},{3,2},{4,5},{5,4},{6,7},{7,6},{8,9},{9,8},{10,11... | collective-permute-start | bytes 983048 | tf_op jit(solution)/shard_map/ppermute | solution.py:411
  17.9 27.7 %collective-permute-start.6 = (bf16[8,40,128]{2,1,0:T(8,128)(2,1)S(1)}, bf16[8,40,128]{2,1,0:T(8,128)(2,1)S(1)}, u32[]{:S(2)}, u32[]{:S(2)}) collective-permute-start(bf16[8,40,128]{2,1,0:T(8,128)(2,1)S(1)} %pad_maximum_fusion), channel_id=1, source_target_pairs={{0,6},{1,7},{2,4},{3,5},{4,2},{5,3},{6,0},{7,1},{8,14},{9,15},{10,... | collective-permute-start | bytes 245768 | tf_op jit(solution)/shard_map/ppermute | solution.py:411
  19.0 26.6 %collective-permute-start.5 = (bf16[8,40,128]{2,1,0:T(8,128)(2,1)S(1)}, bf16[8,40,128]{2,1,0:T(8,128)(2,1)S(1)}, u32[]{:S(2)}, u32[]{:S(2)}) collective-permute-start(bf16[8,40,128]{2,1,0:T(8,128)(2,1)S(1)} %pad_maximum_fusion), channel_id=1, source_target_pairs={{0,4},{1,5},{2,6},{3,7},{4,0},{5,1},{6,2},{7,3},{8,12},{9,13},{10,... | collective-permute-start | bytes 245768 | tf_op jit(solution)/shard_map/ppermute | solution.py:411
  19.9 25.8 %collective-permute-start.4 = (bf16[8,40,128]{2,1,0:T(8,128)(2,1)S(1)}, bf16[8,40,128]{2,1,0:T(8,128)(2,1)S(1)}, u32[]{:S(2)}, u32[]{:S(2)}) collective-permute-start(bf16[8,40,128]{2,1,0:T(8,128)(2,1)S(1)} %pad_maximum_fusion), channel_id=1, source_target_pairs={{0,2},{1,3},{2,0},{3,1},{4,6},{5,7},{6,4},{7,5},{8,10},{9,11},{10,... | collective-permute-start | bytes 245768 | tf_op jit(solution)/shard_map/ppermute | solution.py:411
  21.4 0.9 %copy-start.1 = (bf16[256,256]{1,0:T(8,128)(2,1)S(1)}, bf16[256,256]{1,0:T(8,128)(2,1)}, u32[]{:S(2)}) copy-start(bf16[256,256]{1,0:T(8,128)(2,1)} %constant.2.clone.plane_hbm) | copy-start | bytes 393220
  45.7 1.8 %collective-permute-start.8 = (bf16[32,40,128]{2,1,0:T(8,128)(2,1)S(1)}, bf16[32,40,128]{2,1,0:T(8,128)(2,1)S(1)}, u32[]{:S(2)}, u32[]{:S(2)}) collective-permute-start(bf16[32,40,128]{2,1,0:T(8,128)(2,1)S(1)} %constant_dynamic-update-slice_fusion.4.own), channel_id=1, source_target_pairs={{0,1},{1,0},{2,3},{3,2},{4,5},{5,4},{6,7},{7,6},{8,9},{9,8},{10,11... | collective-permute-start | bytes 983048 | tf_op jit(solution)/shard_map/ppermute | solution.py:411
  45.8 24.3 %copy-start = (f32[2,8,128,128]{3,2,1,0:T(8,128)S(1)}, f32[2,8,128,128]{3,2,1,0:T(8,128)}, u32[]{:S(2)}) copy-start(f32[2,8,128,128]{3,2,1,0:T(8,128)} %get-tuple-element.23.first) | copy-start | bytes 3145732
  45.8 24.3 %collective-permute-start.9 = (bf16[2,8,128,128]{3,2,1,0:T(8,128)(2,1)S(1)}, bf16[2,8,128,128]{3,2,1,0:T(8,128)(2,1)S(1)}, u32[]{:S(2)}, u32[]{:S(2)}) collective-permute-start(bf16[2,8,128,128]{3,2,1,0:T(8,128)(2,1)S(1)} %get-tuple-element.28), channel_id=1, source_target_pairs={{0,16},{16,0},{1,17},{17,1},{2,18},{18,2},{3,19},{19,3},{4,20},{20... | collective-permute-start | bytes 1572872 | tf_op jit(solution)/shard_map/ppermute | solution.py:454
